TPU v7x, 32 devices: a whole 2x2x4 slice. The times are simulated.
32 devices in a mesh: seq: 8 (over z, y), tp: 4 (over x, core).
Axes of the slice: x: 2, y: 2, z: 4, core: 2. Of those that a mesh axis runs over, the one named last changes fastest.
Arguments:
- layer_input: bfloat16 [1024, 1600], P(('seq', 'tp')), may hold values from -6 to 6
- out_grad: bfloat16 [1024, 1600], P(('seq', 'tp')), may hold values from -2.5 to 2.5
- w_in: bfloat16 [1600, 1600], P('tp'), may hold values from -0.15625 to 0.15625
- w_gate: bfloat16 [1600, 1600], P('tp'), may hold values from -0.15625 to 0.15625
- w_out: bfloat16 [1600, 1600], P('tp'), may hold values from -0.15625 to 0.15625
- b_proj: bfloat16 [16, 1024], P(None, 'seq'), may hold values from -3 to 3
- c_proj: bfloat16 [16, 1024], P(None, 'seq'), may hold values from -3 to 3
- log_decay: bfloat16 [25, 1024], P(None, 'seq'), may hold values from -1 to 0
- d_skip: float32 [1600], P('tp'), may hold values from 0.5 to 1.5
- entry_state: float32 [16, 1600], P(None, 'tp'), may hold values from -6 to 6
- doc_start: int32 [1024], P('seq'), may hold values 0 or 1
Outputs:
- input_grad: bfloat16 [1024, 1600], P(('seq', 'tp'))
- b_grad: float32 [16, 1024], P(None, 'seq')
- c_grad: float32 [16, 1024], P(None, 'seq')
All inputs are finite; a program needn't handle non-finite values. No bound on the sum of `doc_start` on one device may be relied on, other than what follows from the above.
Results may differ from a plain program's by a relative error of at most 0.0065.
Values may be sent and summed in bfloat16 or wider, within the bound.
No kernel may reach another device: no remote copies, remote signals or barrier semaphores. Data moves between devices by JAX's collectives and lax.ppermute only.
A program may use at most 128 MiB of HBM per device.

v0:
```python
import math

import jax
import jax.numpy as jnp
from jax import lax
from jax.sharding import PartitionSpec as P

HDIM = 64
UNIT = 2
BLK = 128


FULL_PRECISION = lax.Precision.HIGHEST


def silu_slope(values):
    logistic = jax.nn.sigmoid(values)
    return logistic * (1.0 + values * (1.0 - logistic))


def combine_pairs(earlier, later_pair):
    return (earlier[0] * later_pair[0], later_pair[0][..., None, :] * earlier[1] + later_pair[1])


def split_blocks(values):
    leading = values.shape[:-1]
    block_count = values.shape[-1] // BLK
    return jnp.moveaxis(values.reshape(leading + (block_count, BLK)), -2, 0)


def join_blocks(values):
    moved_axes = jnp.moveaxis(values, 0, -2)
    return moved_axes.reshape(moved_axes.shape[:-2] + (moved_axes.shape[-2] * BLK,))


def prepare(x_rows, y_grads, log_rows, marks, b_rows, c_rows):
    log_blocks = split_blocks(log_rows)
    mark_blocks = split_blocks(marks)
    cumulative = jnp.cumsum(log_blocks, axis=-1)
    counts = jnp.cumsum(mark_blocks, axis=-1)
    fresh_rows = (counts == 0).astype(jnp.float32)
    inside = (counts == counts[:, -1:]).astype(jnp.float32)
    totals = cumulative[..., -1]
    scales = jnp.where(mark_blocks[:, None, :] == 1, 1.0, jnp.sqrt(-jnp.expm1(2.0 * log_blocks)))
    scaled = split_blocks(x_rows).astype(jnp.float32) * scales
    gradient = split_blocks(y_grads).astype(jnp.float32)
    b_blocks = split_blocks(b_rows).astype(jnp.float32)
    c_blocks = split_blocks(c_rows).astype(jnp.float32)
    carry_in = jnp.exp(cumulative) * fresh_rows[:, None, :]
    carry_out = jnp.exp(totals[..., None] - cumulative) * inside[:, None, :]
    factor = jnp.exp(totals) * fresh_rows[:, -1:]
    state_part = jnp.einsum("bnq,bmq->bnm", b_blocks, scaled * carry_out, precision=FULL_PRECISION)
    grad_part = jnp.einsum("bnq,bmq->bnm", c_blocks, gradient * carry_in, precision=FULL_PRECISION)
    return (
        cumulative,
        counts,
        scaled,
        gradient,
        b_blocks,
        c_blocks,
        carry_in,
        carry_out,
        scales,
        factor,
        state_part,
        grad_part,
    )


def block_scans(parts):
    factor, state_part, grad_part = (parts[9], parts[10], parts[11])
    inc_factor, inc_state = lax.associative_scan(combine_pairs, (factor, state_part))
    rev_factor, rev_grad = lax.associative_scan(combine_pairs, (factor, grad_part), reverse=True)
    unit_rows = jnp.ones_like(factor[:1])
    empty_rows = jnp.zeros_like(state_part[:1])
    before = (
        jnp.concatenate([unit_rows, inc_factor[:-1]], axis=0),
        jnp.concatenate([empty_rows, inc_state[:-1]], axis=0),
    )
    behind = (
        jnp.concatenate([rev_factor[1:], unit_rows], axis=0),
        jnp.concatenate([rev_grad[1:], empty_rows], axis=0),
    )
    return (before, behind, (inc_factor[-1], inc_state[-1], rev_grad[0]))


def block_pass(pieces):
    cumulative, counts, scaled, gradient, b_blk, c_blk, carry_in, carry_out, state_in, grad_in = (
        pieces
    )
    centre = cumulative[:, BLK // 2][:, None]
    rising = jnp.exp(cumulative - centre)
    falling = jnp.exp(centre - cumulative)
    upper_rows = gradient * rising
    lower_rows = scaled * falling
    positions = jnp.arange(BLK)
    causal_mask = (positions[:, None] >= positions[None, :]) & (counts[:, None] == counts[None, :])
    crossed = jnp.where(causal_mask, jnp.dot(c_blk.T, b_blk, precision=FULL_PRECISION), 0.0)
    weight = jnp.where(
        causal_mask, jnp.dot(upper_rows.T, lower_rows, precision=FULL_PRECISION), 0.0
    )
    ssm_part = rising * jnp.dot(
        lower_rows, crossed.T, precision=FULL_PRECISION
    ) + carry_in * jnp.dot(state_in.T, c_blk, precision=FULL_PRECISION)
    x_part = falling * jnp.dot(upper_rows, crossed, precision=FULL_PRECISION) + carry_out * jnp.dot(
        grad_in.T, b_blk, precision=FULL_PRECISION
    )
    c_part = jnp.dot(b_blk, weight.T, precision=FULL_PRECISION) + jnp.dot(
        state_in, gradient * carry_in, precision=FULL_PRECISION
    )
    b_part = jnp.dot(c_blk, weight, precision=FULL_PRECISION) + jnp.dot(
        grad_in, scaled * carry_out, precision=FULL_PRECISION
    )
    return (ssm_part, x_part, b_part, c_part)


def group_leading(values, group_size):
    return values.reshape((values.shape[0] // group_size, group_size) + values.shape[1:])


def ungroup_leading(values):
    return values.reshape((values.shape[0] * values.shape[1],) + values.shape[2:])


def finish(parts, edges, state_dev, grad_dev, skip_gain, x_rows, y_grads):
    before, behind = (edges[0], edges[1])
    state_in = before[0][:, None, :] * state_dev[None] + before[1]
    grad_in = behind[0][:, None, :] * grad_dev[None] + behind[1]
    pieces = parts[:8] + (state_in, grad_in)
    block_count = parts[0].shape[0]
    group_size = math.gcd(block_count, 16)
    grouped = tuple((group_leading(values, group_size) for values in pieces))
    results = lax.map(jax.vmap(block_pass), grouped)
    ssm_blocks, x_blocks, b_blocks, c_blocks = tuple(
        (ungroup_leading(values) for values in results)
    )
    ssm_out = (join_blocks(ssm_blocks) + skip_gain[:, None] * x_rows.astype(jnp.float32)).astype(
        jnp.bfloat16
    )
    x_grad = (
        join_blocks(x_blocks * parts[8]) + skip_gain[:, None] * y_grads.astype(jnp.float32)
    ).astype(jnp.bfloat16)
    return (ssm_out, x_grad, join_blocks(b_blocks), join_blocks(c_blocks))


def shards(
    layer_input,
    out_grad,
    w_in,
    w_gate,
    w_out,
    b_proj,
    c_proj,
    log_decay,
    d_skip,
    entry_state,
    doc_start,
):
    rows_in, rows_grad = (
        lax.all_gather(layer_input, "tp", axis=0, tiled=True),
        lax.all_gather(out_grad, "tp", axis=0, tiled=True),
    )
    contract = (((1,), (1,)), ((), ()))
    pre_act = lax.dot_general(w_in, rows_in, contract, preferred_element_type=jnp.float32)
    gate_act = lax.dot_general(w_gate, rows_in, contract, preferred_element_type=jnp.float32)
    mix_grad = lax.dot_general(w_out, rows_grad, contract, preferred_element_type=jnp.float32)
    x_rows = jax.nn.silu(pre_act).astype(jnp.bfloat16)
    y_grads = (mix_grad * jax.nn.silu(gate_act)).astype(jnp.bfloat16)
    channels, tokens_here = x_rows.shape
    head_count = log_decay.shape[0]
    head_of = (lax.axis_index("tp") * channels + jnp.arange(channels)) // HDIM
    pick_head = (head_of[:, None] == jnp.arange(head_count)[None, :]).astype(jnp.bfloat16)
    log_rows = jnp.dot(pick_head, log_decay, preferred_element_type=jnp.float32)
    owners = lax.axis_size("seq")
    units = channels // UNIT
    capacity = units // owners + 1
    slot_count = capacity * owners
    width = capacity * UNIT

    def pack(values):
        padded = jnp.pad(values, ((0, slot_count * UNIT - channels), (0, 0)))
        return padded.reshape(owners, width, tokens_here)

    owned_x, owned_grad, owned_log = (
        lax.all_to_all(pack(x_rows), "seq", split_axis=0, concat_axis=2, tiled=True),
        lax.all_to_all(pack(y_grads), "seq", split_axis=0, concat_axis=2, tiled=True),
        lax.all_to_all(
            pack(log_rows.astype(jnp.bfloat16)), "seq", split_axis=0, concat_axis=2, tiled=True
        ),
    )
    b_all, c_all, start_all = (
        lax.all_gather(b_proj, "seq", axis=1, tiled=True),
        lax.all_gather(c_proj, "seq", axis=1, tiled=True),
        lax.all_gather(doc_start.astype(jnp.bfloat16), "seq", axis=0, tiled=True),
    )
    span = start_all.shape[0]
    marks = start_all.astype(jnp.int32) * (jnp.arange(span) > 0).astype(jnp.int32)
    owner_index = lax.axis_index("seq")

    def own(values):
        leading = values.shape[:-1]
        padded = jnp.pad(values, [(0, 0)] * len(leading) + [(0, slot_count * UNIT - channels)])
        return lax.dynamic_slice_in_dim(padded, owner_index * width, width, len(leading))

    x_own = owned_x.reshape(width, span)
    grad_own = owned_grad.reshape(width, span)
    log_own = owned_log.reshape(width, span).astype(jnp.float32)
    entry_own = own(entry_state)
    parts = prepare(x_own, grad_own, log_own, marks, b_all, c_all)
    edges = block_scans(parts)
    ssm_own, xgrad_own, b_part, c_part = finish(
        parts, edges, entry_own, jnp.zeros_like(entry_own), own(d_skip), x_own, grad_own
    )
    ssm_back, xgrad_back = (
        lax.all_to_all(
            ssm_own.reshape(1, width, span), "seq", split_axis=2, concat_axis=0, tiled=True
        ),
        lax.all_to_all(
            xgrad_own.reshape(1, width, span), "seq", split_axis=2, concat_axis=0, tiled=True
        ),
    )
    ssm_rows = ssm_back.reshape(slot_count * UNIT, tokens_here)[:channels]
    x_grad = xgrad_back.reshape(slot_count * UNIT, tokens_here)[:channels]
    state_size = b_part.shape[0]
    b_pieces, c_pieces = (
        lax.all_to_all(
            b_part.reshape(state_size, owners, tokens_here),
            "seq",
            split_axis=1,
            concat_axis=1,
            tiled=True,
        ),
        lax.all_to_all(
            c_part.reshape(state_size, owners, tokens_here),
            "seq",
            split_axis=1,
            concat_axis=1,
            tiled=True,
        ),
    )
    b_local = jnp.sum(b_pieces, axis=1)
    c_local = jnp.sum(c_pieces, axis=1)
    b_grad, c_grad = lax.psum((b_local, c_local), "tp")
    pre_grad = (x_grad.astype(jnp.float32) * silu_slope(pre_act)).astype(jnp.bfloat16)
    gate_grad = (mix_grad * ssm_rows.astype(jnp.float32) * silu_slope(gate_act)).astype(
        jnp.bfloat16
    )
    outer = (((0,), (0,)), ((), ()))
    from_pre = lax.dot_general(pre_grad, w_in, outer, preferred_element_type=jnp.float32)
    from_gate = lax.dot_general(gate_grad, w_gate, outer, preferred_element_type=jnp.float32)
    input_grad = lax.psum_scatter(
        from_pre + from_gate, "tp", scatter_dimension=0, tiled=True
    ).astype(jnp.bfloat16)
    return (input_grad, b_grad, c_grad)


def solution(mesh):
    in_specs = (
        P(("seq", "tp"), None),
        P(("seq", "tp"), None),
        P("tp", None),
        P("tp", None),
        P("tp", None),
        P(None, "seq"),
        P(None, "seq"),
        P(None, "seq"),
        P("tp"),
        P(None, "tp"),
        P("seq"),
    )
    out_specs = (P(("seq", "tp"), None), P(None, "seq"), P(None, "seq"))
    return jax.shard_map(shards, mesh=mesh, in_specs=in_specs, out_specs=out_specs, check_vma=False)
```

profile of v0, /device:TPU:0, one launch (start us, length us, event | category | flops | bytes accessed | tf_op | source)
XLA Modules:
  0.0 312.9 jit_solution(9583434936186511018)
XLA Ops:
  9.0 7.3 %all-to-all-start = ((bf16[8,52,128]{2,1,0:T(8,128)(2,1)}), bf16[8,52,128]{2,1,0:T(8,128)(2,1)S(1)}, u32[]{:S(2)}, u32[]{:S(2)}) async-start(bf16[8,52,128]{2,1,0:T(8,128)(2,1)} %reshape.268), calls=%async_computation | async-start | bytes 229376 | tf_op jit(solution)/shard_map/all_to_all | solution.py:187
  17.6 20.9 %all-gather = bf16[8,1,128]{2,1,0:T(2,128)(2,1)S(1)} all-gather(bf16[1,1,128]{2,1,0:T(2,128)(2,1)S(1)} %convert_bitcast_fusion.2), channel_id=1, replica_groups=mesh['seq'=8,'tp'=4] {'seq'}, dimensions={0}, use_global_device_ids=true | all-gather | bytes 2304 | tf_op jit(solution)/shard_map/all_gather | solution.py:194
  40.3 6.8 %all_gather.16 = bf16[128,1600]{1,0:T(8,128)(2,1)S(1)} all-gather(bf16[32,1600]{1,0:T(8,128)(2,1)} %param.11), channel_id=1, replica_groups=mesh['seq'=8,'tp'=4] {'tp'}, dimensions={0}, use_global_device_ids=true | all-gather | bytes 512000 | tf_op jit(solution)/shard_map/all_gather | solution.py:160
  47.1 6.9 %all_gather.15 = bf16[128,1600]{1,0:T(8,128)(2,1)S(1)} all-gather(bf16[32,1600]{1,0:T(8,128)(2,1)S(1)} %copy-done.16), channel_id=1, replica_groups=mesh['seq'=8,'tp'=4] {'tp'}, dimensions={0}, use_global_device_ids=true | all-gather | bytes 512000 | tf_op jit(solution)/shard_map/all_gather | solution.py:161
  57.1 26.9 %all_gather.18 = bf16[16,1024]{1,0:T(8,128)(2,1)} all-gather(bf16[16,128]{1,0:T(8,128)(2,1)S(1)} %copy-done.33), channel_id=1, replica_groups=mesh['seq'=8,'tp'=4] {'seq'}, dimensions={1}, use_global_device_ids=true | all-gather | bytes 36864 | tf_op jit(solution)/shard_map/all_gather | solution.py:193
  86.0 26.0 %all_gather.19 = bf16[16,1024]{1,0:T(8,128)(2,1)S(1)} all-gather(bf16[16,128]{1,0:T(8,128)(2,1)S(1)} %copy-done.34), channel_id=1, replica_groups=mesh['seq'=8,'tp'=4] {'seq'}, dimensions={1}, use_global_device_ids=true | all-gather | bytes 36864 | tf_op jit(solution)/shard_map/all_gather | solution.py:192
  115.0 3.4 %all-to-all-start.1 = ((bf16[8,52,128]{2,1,0:T(8,128)(2,1)}), bf16[8,52,128]{2,1,0:T(8,128)(2,1)S(1)}, u32[]{:S(2)}, u32[]{:S(2)}) async-start(bf16[8,52,128]{2,1,0:T(8,128)(2,1)} %reshape.269), calls=%async_computation.1 | async-start | bytes 229376 | tf_op jit(solution)/shard_map/all_to_all | solution.py:186
  118.3 4.3 %reduce_window_sum.24 = f32[8,52,128]{2,1,0:T(8,128)S(1)} reduce-window(bf16[8,52,128]{2,1,0:T(8,128)(2,1)} %copy-done.2, f32[]{:T(128)} %constant.79.clone.1), window={size=1x1x128 pad=0_0x0_0x127_0}, to_apply=%region_0.1 | reduce-window | flops 6762496 | bytes 319492 | tf_op jit(solution)/shard_map/jit(cumsum)/reduce_window_sum | solution.py:39
  130.7 5.9 %all-to-all-start.3 = ((bf16[8,52,128]{2,1,0:T(8,128)(2,1)}), bf16[8,52,128]{2,1,0:T(8,128)(2,1)}, u32[]{:S(2)}, u32[]{:S(2)}) async-start(bf16[8,52,128]{2,1,0:T(8,128)(2,1)} %reshape.275), calls=%async_computation.3 | async-start | bytes 229376 | tf_op jit(solution)/shard_map/all_to_all | solution.py:185
  194.4 3.2 %pad.197 = f32[8,16,52]{2,1,0:T(8,128)} pad(f32[4,16,52]{2,1,0:T(8,128)} %add.234, f32[]{:T(128)} %constant.79.clone.1), padding=1_0_1x0_0_0x0_0_0 | pad | bytes 39940
  199.0 3.2 %pad.147 = f32[7,16,52]{2,1,0:T(8,128)} pad(f32[4,16,52]{2,1,0:T(8,128)} %pad_maximum_fusion, f32[]{:T(128)} %constant.79.clone.1), padding=0_0_1x0_0_0x0_0_0 | pad | bytes 36612 | tf_op jit(solution)/shard_map/slice | solution.py:82
  207.0 3.2 %pad.198 = f32[8,16,52]{2,1,0:T(8,128)} pad(f32[4,16,52]{2,1,0:T(8,128)} %add.251, f32[]{:T(128)} %constant.79.clone.1), padding=1_0_1x0_0_0x0_0_0 | pad | bytes 39940
  211.6 3.2 %pad.149 = f32[7,16,52]{2,1,0:T(8,128)} pad(f32[4,16,52]{2,1,0:T(8,128)} %pad_maximum_fusion.1, f32[]{:T(128)} %constant.79.clone.1), padding=0_0_1x0_0_0x0_0_0 | pad | bytes 36612 | tf_op jit(solution)/shard_map/slice | solution.py:78
  223.4 2.3 fusion.3
  231.0 3.1 reduce.8
  236.2 6.0 %all-to-all-start.2 = ((bf16[8,2,3328]{2,1,0:T(2,128)(2,1)}), bf16[8,2,3328]{2,1,0:T(2,128)(2,1)}, u32[]{:S(2)}, u32[]{:S(2)}) async-start(bf16[8,2,3328]{2,1,0:T(2,128)(2,1)} %reshape.297), calls=%async_computation.2 | async-start | bytes 212992 | tf_op jit(solution)/shard_map/all_to_all | solution.py:218
  243.5 3.1 reduce.9
  249.5 5.2 %all-to-all-start.4 = ((bf16[8,2,3328]{2,1,0:T(2,128)(2,1)}), bf16[8,2,3328]{2,1,0:T(2,128)(2,1)}, u32[]{:S(2)}, u32[]{:S(2)}) async-start(bf16[8,2,3328]{2,1,0:T(2,128)(2,1)} %reshape.299), calls=%async_computation.4 | async-start | bytes 212992 | tf_op jit(solution)/shard_map/all_to_all | solution.py:215
  259.0 3.0 all-to-all-done.4
  273.3 3.4 %all-to-all-start.5 = ((f32[16,8,128]{2,0,1:T(8,128)}), f32[16,8,128]{2,0,1:T(8,128)S(1)}, u32[]{:S(2)}, u32[]{:S(2)}) async-start(f32[16,8,128]{2,0,1:T(8,128)} %fusion.8), calls=%async_computation.6 | async-start | bytes 131072 | tf_op jit(solution)/shard_map/all_to_all | solution.py:226
  278.2 5.3 %all-to-all-done.5 = f32[16,8,128]{2,0,1:T(8,128)S(1)} async-done(((f32[16,8,128]{2,0,1:T(8,128)}), f32[16,8,128]{2,0,1:T(8,128)S(1)}, u32[]{:S(2)}, u32[]{:S(2)}) %all-to-all-start.5) | async-done | bytes 65568 | tf_op jit(solution)/shard_map/all_to_all | solution.py:226
  283.5 3.3 %all-to-all-start.6 = ((f32[16,8,128]{2,0,1:T(8,128)}), f32[16,8,128]{2,0,1:T(8,128)S(1)}, u32[]{:S(2)}, u32[]{:S(2)}) async-start(f32[16,8,128]{2,0,1:T(8,128)} %fusion.7), calls=%async_computation.7 | async-start | bytes 131072 | tf_op jit(solution)/shard_map/all_to_all | solution.py:233
  286.9 6.8 %all-to-all-done.6 = f32[16,8,128]{2,0,1:T(8,128)S(1)} async-done(((f32[16,8,128]{2,0,1:T(8,128)}), f32[16,8,128]{2,0,1:T(8,128)S(1)}, u32[]{:S(2)}, u32[]{:S(2)}) %all-to-all-start.6) | async-done | bytes 65568 | tf_op jit(solution)/shard_map/all_to_all | solution.py:233
  293.7 10.7 %all-reduce.33 = (f32[16,128]{1,0:T(8,128)}, f32[16,128]{1,0:T(8,128)}) all-reduce(f32[16,128]{1,0:T(8,128)S(1)} %reduce_sum.18, f32[16,128]{1,0:T(8,128)S(1)} %reduce_sum.19), channel_id=1, replica_groups=mesh['seq'=8,'tp'=4] {'tp'}, use_global_device_ids=true, to_apply=%region_4.5 | all-reduce | flops 4096 | bytes 32768 | tf_op jit(solution)/shard_map/psum | solution.py:243
  (222 shorter events, 124.8 us)
Async XLA Ops:
  7.2 76.9 %copy-start = (bf16[400,1600]{1,0:T(8,128)(2,1)S(1)}, bf16[400,1600]{1,0:T(8,128)(2,1)}, u32[]{:S(2)}) copy-start(bf16[400,1600]{1,0:T(8,128)(2,1)} %param.13) | copy-start | bytes 3840004
  7.2 39.9 %copy-start.16 = (bf16[32,1600]{1,0:T(8,128)(2,1)S(1)}, bf16[32,1600]{1,0:T(8,128)(2,1)}, u32[]{:S(2)}) copy-start(bf16[32,1600]{1,0:T(8,128)(2,1)} %param.12) | copy-start | bytes 307204
  7.2 46.8 %copy-start.1 = (bf16[400,1600]{1,0:T(8,128)(2,1)S(1)}, bf16[400,1600]{1,0:T(8,128)(2,1)}, u32[]{:S(2)}) copy-start(bf16[400,1600]{1,0:T(8,128)(2,1)} %param.14) | copy-start | bytes 3840004
  9.0 105.3 %all-to-all-start = ((bf16[8,52,128]{2,1,0:T(8,128)(2,1)}), bf16[8,52,128]{2,1,0:T(8,128)(2,1)S(1)}, u32[]{:S(2)}, u32[]{:S(2)}) async-start(bf16[8,52,128]{2,1,0:T(8,128)(2,1)} %reshape.268), calls=%async_computation | async-start | bytes 229376 | tf_op jit(solution)/shard_map/all_to_all | solution.py:187
  38.7 74.5 %copy-start.20 = (s32[8,128]{1,0:T(8,128)}, s32[8,128]{1,0:T(8,128)S(1)}, u32[]{:S(2)}) copy-start(s32[8,128]{1,0:T(8,128)S(1)} %reduce_window_sum.26) | copy-start | bytes 12292
  47.1 8.1 %copy-start.37 = (bf16[400,1600]{1,0:T(8,128)(2,1)S(1)}, bf16[400,1600]{1,0:T(8,128)(2,1)}, u32[]{:S(2)}) copy-start(bf16[400,1600]{1,0:T(8,128)(2,1)} %param.15) | copy-start | bytes 3840004
  84.0 27.9 %copy-start.23 = (f32[16,400]{1,0:T(8,128)S(1)}, f32[16,400]{1,0:T(8,128)}, u32[]{:S(2)}) copy-start(f32[16,400]{1,0:T(8,128)} %param.20) | copy-start | bytes 76804
  84.1 28.6 %copy-start.36 = (f32[400]{0:T(512)S(1)}, f32[400]{0:T(512)}, u32[]{:S(2)}) copy-start(f32[400]{0:T(512)} %param.19) | copy-start | bytes 4804
  84.1 29.1 %copy-start.28 = (pred[128,128]{1,0:T(8,128)(4,1)S(1)}, pred[128,128]{1,0:T(8,128)(4,1)}, u32[]{:S(2)}) copy-start(pred[128,128]{1,0:T(8,128)(4,1)} %iota_compare_fusion.2) | copy-start | bytes 49156
  115.0 15.7 %all-to-all-start.1 = ((bf16[8,52,128]{2,1,0:T(8,128)(2,1)}), bf16[8,52,128]{2,1,0:T(8,128)(2,1)S(1)}, u32[]{:S(2)}, u32[]{:S(2)}) async-start(bf16[8,52,128]{2,1,0:T(8,128)(2,1)} %reshape.269), calls=%async_computation.1 | async-start | bytes 229376 | tf_op jit(solution)/shard_map/all_to_all | solution.py:186
  123.0 38.1 %copy-start.18 = (f32[8,52]{1,0:T(8,128)}, f32[8,52]{1,0:T(8,128)S(1)}, u32[]{:S(2)}) copy-start(f32[8,52]{1,0:T(8,128)S(1)} %get-tuple-element.34) | copy-start | bytes 4996
  123.8 15.1 %copy-start.22 = (f32[4,52]{1,0:T(4,128)}, f32[4,52]{1,0:T(4,128)S(1)}, u32[]{:S(2)}) copy-start(f32[4,52]{1,0:T(4,128)S(1)} %slice.218) | copy-start | bytes 2500
  125.7 13.2 %copy-start.24 = (f32[4,52]{1,0:T(4,128)}, f32[4,52]{1,0:T(4,128)S(1)}, u32[]{:S(2)}) copy-start(f32[4,52]{1,0:T(4,128)S(1)} %slice.221) | copy-start | bytes 2500
  130.7 27.7 %all-to-all-start.3 = ((bf16[8,52,128]{2,1,0:T(8,128)(2,1)}), bf16[8,52,128]{2,1,0:T(8,128)(2,1)}, u32[]{:S(2)}, u32[]{:S(2)}) async-start(bf16[8,52,128]{2,1,0:T(8,128)(2,1)} %reshape.275), calls=%async_computation.3 | async-start | bytes 229376 | tf_op jit(solution)/shard_map/all_to_all | solution.py:185
  138.9 59.5 %slice-start = ((f32[8,16,52]{2,1,0:T(8,128)}), f32[1,16,52]{2,1,0:T(8,128)S(1)}, s32[]{:S(2)}) async-start(f32[8,16,52]{2,1,0:T(8,128)} %copy-done.10), calls=%async_computation.9 | async-start | bytes 16384 | tf_op jit(solution)/shard_map/slice | solution.py:73
  163.1 47.1 %slice-start.1 = ((f32[8,16,52]{2,1,0:T(8,128)}), f32[1,16,52]{2,1,0:T(8,128)S(1)}, s32[]{:S(2)}) async-start(f32[8,16,52]{2,1,0:T(8,128)} %copy-done.15), calls=%async_computation.10 | async-start | bytes 16384 | tf_op jit(solution)/shard_map/slice | solution.py:72
  216.0 6.2 %copy-start.17 = (f32[16,52]{1,0:T(8,128)S(1)}, f32[16,52]{1,0:T(8,128)}, u32[]{:S(2)}) copy-start(f32[16,52]{1,0:T(8,128)} %pad_dynamic-slice_fusion) | copy-start | bytes 9988
  236.2 13.3 %all-to-all-start.2 = ((bf16[8,2,3328]{2,1,0:T(2,128)(2,1)}), bf16[8,2,3328]{2,1,0:T(2,128)(2,1)}, u32[]{:S(2)}, u32[]{:S(2)}) async-start(bf16[8,2,3328]{2,1,0:T(2,128)(2,1)} %reshape.297), calls=%async_computation.2 | async-start | bytes 212992 | tf_op jit(solution)/shard_map/all_to_all | solution.py:218
  249.5 12.4 %all-to-all-start.4 = ((bf16[8,2,3328]{2,1,0:T(2,128)(2,1)}), bf16[8,2,3328]{2,1,0:T(2,128)(2,1)}, u32[]{:S(2)}, u32[]{:S(2)}) async-start(bf16[8,2,3328]{2,1,0:T(2,128)(2,1)} %reshape.299), calls=%async_computation.4 | async-start | bytes 212992 | tf_op jit(solution)/shard_map/all_to_all | solution.py:215
  254.7 49.8 %reduce-scatter.2.cloned.1.call-start = ((), (), s32[]{:S(2)}) async-start(), calls=%async_computation.8 | async-start | bytes 1064960 | tf_op jit(solution)/shard_map/reduce_scatter | solution.py:251
  268.7 7.9 %copy-start.12 = (bf16[16,1024]{1,0:T(8,128)(2,1)S(1)}, bf16[16,1024]{1,0:T(8,128)(2,1)}, u32[]{:S(2)}) copy-start(bf16[16,1024]{1,0:T(8,128)(2,1)} %copy-done.11) | copy-start | bytes 98308
  270.8 6.3 %copy-start.9 = (f32[7,16,52]{2,1,0:T(8,128)S(1)}, f32[7,16,52]{2,1,0:T(8,128)}, u32[]{:S(2)}) copy-start(f32[7,16,52]{2,1,0:T(8,128)} %copy-done.8) | copy-start | bytes 69892
  273.3 10.2 %all-to-all-start.5 = ((f32[16,8,128]{2,0,1:T(8,128)}), f32[16,8,128]{2,0,1:T(8,128)S(1)}, u32[]{:S(2)}, u32[]{:S(2)}) async-start(f32[16,8,128]{2,0,1:T(8,128)} %fusion.8), calls=%async_computation.6 | async-start | bytes 131072 | tf_op jit(solution)/shard_map/all_to_all | solution.py:226
  283.5 10.2 %all-to-all-start.6 = ((f32[16,8,128]{2,0,1:T(8,128)}), f32[16,8,128]{2,0,1:T(8,128)S(1)}, u32[]{:S(2)}, u32[]{:S(2)}) async-start(f32[16,8,128]{2,0,1:T(8,128)} %fusion.7), calls=%async_computation.7 | async-start | bytes 131072 | tf_op jit(solution)/shard_map/all_to_all | solution.py:233
  (24 other events, 48.9 us)
Sparse Core Ops, SparseCore 0:
  268.8 21.6 reduce-scatter.1
where the time goes:
time: 317 us; the launch traced here: 313 us
  blocking collectives  98.2 us (31%)
  local copies, waits for them, and re-layouts  73.5 us (23%)
  other arithmetic  53.1 us (17%)
  starting transfers between devices  34.5 us (11%)
  matrix products  22.9 us (7%)
  waiting for transfers between devices  16 us (5%)
  between operations  14.7 us (5%)
    all_gather x1, blocking collectives, shards(): lax.all_gather(c_proj, 'seq', axis=1, tiled=True)  26.9 us
    all_gather x1, blocking collectives, shards(): lax.all_gather(b_proj, 'seq', axis=1, tiled=True)  26 us
    all_gather x1, blocking collectives, shards(): lax.all_gather(doc_start.astype(jnp.bfloat16), 'seq', axis=0, tiled=True)  20.9 us
    unnamed x85, local copies, waits for them, and re-layouts  19 us
    psum x1, blocking collectives, shards(): b_grad, c_grad = lax.psum((b_local, c_local), 'tp')  10.7 us
    pad x6, local copies, waits for them, and re-layouts, block_scans(): lax.associative_scan(combine_pairs, (factor, grad_part), reverse=True)  10.5 us
    pad x6, local copies, waits for them, and re-layouts, block_scans(): lax.associative_scan(combine_pairs, (factor, state_part))  9.9 us
    slice x12, local copies, waits for them, and re-layouts, block_scans(): lax.associative_scan(combine_pairs, (factor, grad_part), reverse=True)  7.56 us
  transfers between devices with their start and end apart: 8, of which 4 were waited for; matrix products, arithmetic and copies ran while one was open for 19% of the time, Pallas kernels for 0%

commit v1 on v0

v1 whole, which is shorter than its diff:
```python
import jax
import jax.numpy as jnp
from jax import lax
from jax.experimental import pallas as pl
from jax.experimental.pallas import tpu as pltpu
from jax.sharding import PartitionSpec as P

HDIM = 64
LANE = 128
SLOT = 32

F32 = jnp.float32
BF16 = jnp.bfloat16
NN = (((1,), (0,)), ((), ()))
NT = (((1,), (1,)), ((), ()))
TN = (((0,), (0,)), ((), ()))


def dot(left, right, dims=NN):
    return lax.dot_general(left, right, dims, preferred_element_type=F32)


def round_up(value, step):
    return -(-value // step) * step


def silu_slope(values):
    logistic = jax.nn.sigmoid(values)
    return logistic * (1.0 + values * (1.0 - logistic))


def iota(shape, axis):
    return lax.broadcasted_iota(jnp.int32, shape, axis)


def one_minus_exp(values):
    series = 1.0 + values * (1.0 / 7.0)
    for term in (6.0, 5.0, 4.0, 3.0, 2.0):
        series = 1.0 + values * (1.0 / term) * series
    return jnp.where(values > -0.35, -values * series, 1.0 - jnp.exp(values))


def document_counts(doc_ref):
    tokens = doc_ref.shape[1]
    rows, columns = iota((tokens, tokens), 0), iota((tokens, tokens), 1)
    first = (iota((1, tokens), 1) == 0) & (lax.axis_index("seq") == 0)
    mark_row = jnp.where(first, 0.0, doc_ref[...].astype(F32))
    mark_row = jnp.broadcast_to(mark_row, (tokens, tokens))
    mark_column = jnp.sum(jnp.where(rows == columns, mark_row, 0.0), axis=1, keepdims=True)
    count_column = jnp.sum(jnp.where(columns <= rows, mark_row, 0.0), axis=1, keepdims=True)
    count_row = jnp.sum(
        jnp.where(rows <= columns, jnp.broadcast_to(mark_column, (tokens, tokens)), 0.0),
        axis=0,
        keepdims=True,
    )
    return mark_column, count_column, count_row


def head_picker(heads, channels, width):
    lanes = iota((heads, width), 1)
    head = iota((heads, width), 0)
    start = lax.axis_index("tp") * channels
    low = head * HDIM - start
    owned = (lanes >= low) & (lanes < low + HDIM) & (lanes < channels)
    spare = lanes - channels
    listed = (spare == head) | (spare == head + SLOT)
    return jnp.where(owned | listed, 1.0, 0.0).astype(BF16)


def decays(log_ref, doc_ref, picker):
    tokens = log_ref.shape[1]
    mark_column, count_column, count_row = document_counts(doc_ref)
    log_rows = dot(log_ref[...], picker, TN)
    rows, columns = iota((tokens, tokens), 0), iota((tokens, tokens), 1)
    lower = jnp.where(columns <= rows, 1.0, 0.0).astype(BF16)
    cumulative = dot(lower, log_rows.astype(BF16))
    scale = jnp.where(mark_column == 1.0, 1.0, jnp.sqrt(one_minus_exp(2.0 * log_rows)))
    last_count = count_column[tokens - 1 : tokens, :]
    total = cumulative[tokens - 1 : tokens, :]
    centre = cumulative[tokens // 2 : tokens // 2 + 1, :]
    rising = jnp.exp(cumulative - centre)
    falling = jnp.exp(centre - cumulative)
    fresh = jnp.where(count_column == 0.0, 1.0, 0.0)
    inside = jnp.where(count_column == last_count, 1.0, 0.0)
    carry_in = jnp.exp(cumulative) * fresh
    carry_out = jnp.exp(total - cumulative) * inside
    factor = jnp.exp(total) * fresh[tokens - 1 : tokens, :]
    return count_column, count_row, scale, rising, falling, carry_in, carry_out, factor


def two_parts(values):
    high = values.astype(BF16)
    return high, (values - high.astype(F32)).astype(BF16)


def fine_dot(left, right, dims=NN):
    (left_high, left_low), (right_high, right_low) = two_parts(left), two_parts(right)
    small = dot(left_high, right_low, dims) + dot(left_low, right_high, dims)
    return dot(left_high, right_high, dims) + small


class Staged:
    def __init__(self, ins, outs, through, refs):
        refs = list(refs)
        far_in = [name for name, (_, far) in ins.items() if far is True and name not in through]
        far_out = [name for name, (_, _, far) in outs.items() if far]
        self.refs = {name: refs.pop(0) for name in ins}
        made = {name: refs.pop(0) for name in outs}
        held = {name: refs.pop(0) for name in far_in}
        self.made = dict(made, **{name: refs.pop(0) for name in far_out})
        sems = refs.pop(0) if far_in or far_out or through else None
        self.rest = refs
        self.loads = {
            name: pltpu.make_async_copy(self.refs[name], held[name], sems.at[at])
            for at, name in enumerate(far_in)
        }
        self.stores = {
            name: pltpu.make_async_copy(self.made[name], made[name], sems.at[len(far_in) + at])
            for at, name in enumerate(far_out)
        }
        self.passed = [
            pltpu.make_async_copy(self.refs[name], made[name], sems.at[len(far_in + far_out) + at])
            for at, name in enumerate(through)
        ]
        self.refs.update(held)
        for copy in (*self.loads.values(), *self.passed):
            copy.start()

    def take(self, name):
        if name in self.loads:
            self.loads.pop(name).wait()
        return self.refs[name]

    def put(self, name, value):
        self.made[name][...] = value
        self.send(name)

    def send(self, name):
        if name in self.stores:
            self.stores[name].start()

    def finish(self):
        for copy in (*self.stores.values(), *self.passed):
            copy.wait()


def pin(value):
    return pltpu.with_memory_space_constraint(value, pltpu.HBM)


def near(*values):
    return (*values, False)


def far(*values):
    return (*values, True)


def staged_call(body, name, ins, outs, flops=0, scratch=(), through=()):
    outs = dict(outs, **{name: near(ins[name][0].shape, ins[name][0].dtype) for name in through})

    def kernel(*refs):
        staged = Staged(ins, outs, through, refs)
        body(staged, *staged.rest)
        staged.finish()

    def spec(is_far):
        return pl.BlockSpec(memory_space=pltpu.HBM if is_far else pltpu.VMEM)

    held = [
        pltpu.VMEM(value.shape, value.dtype)
        for name, (value, is_far) in ins.items()
        if is_far is True and name not in through
    ]
    held += [pltpu.VMEM(shape, dtype) for shape, dtype, is_far in outs.values() if is_far]
    copies = len(held) + len(through)
    sems = [pltpu.SemaphoreType.DMA((copies,))] if copies else []
    results = pl.pallas_call(
        kernel,
        name=name,
        out_shape=[jax.ShapeDtypeStruct(shape, dtype) for shape, dtype, _ in outs.values()],
        in_specs=[spec(is_far) for _, is_far in ins.values()],
        out_specs=[spec(is_far) for _, _, is_far in outs.values()],
        scratch_shapes=held + sems + list(scratch),
        compiler_params=pltpu.CompilerParams(vmem_limit_bytes=24 * 2**20),
        cost_estimate=pl.CostEstimate(flops=flops, bytes_accessed=2**20, transcendentals=0),
    )(*[pin(value) if is_far else value for value, is_far in ins.values()])
    return dict(zip(outs, results))


def assemble(staged, name, whole):
    for step in range(whole.shape[0] // staged.refs[name + "0"].shape[0]):
        block = staged.take(name + "%d" % step)
        piece = block.shape[0]
        start = pl.multiple_of((lax.axis_index("tp") ^ step) * piece, piece)
        whole[pl.ds(start, piece), :] = block[...]


def head_expander(channels, width):
    first = channels // LANE * LANE
    shape = (width - first, width)
    slot = iota(shape, 0) + (first - channels)
    lane = iota(shape, 1)
    spare = lane - channels
    head = jnp.where(slot < SLOT, slot, slot - SLOT)
    low = head * HDIM - lax.axis_index("tp") * channels
    owned = (lane >= low) & (lane < low + HDIM) & (lane < channels)
    listed = (spare == head) | (spare == head + SLOT)
    kept = (slot >= 0) & (slot < 2 * SLOT)
    return jnp.where(kept & (owned | listed), 1.0, 0.0).astype(BF16)


def encode(value, factor, channels):
    lane = iota(value.shape, 1)
    high = factor.astype(BF16).astype(F32)
    listed = jnp.where(lane < channels + SLOT, high, factor - high)
    return jnp.where(lane < channels, value, listed).astype(BF16)


def decode(message, expander):
    return dot(message[:, message.shape[1] - expander.shape[0] :], expander)


def partner_is_later(bit):
    return lax.axis_index("seq") % (2 * bit) < bit


def put_message(staged, state_part, grad_part, factor, channels, bit):
    message = staged.made["message"]
    states = state_part.shape[0]
    if message.shape[0] == states:
        part = jnp.where(partner_is_later(bit), state_part, grad_part)
        message[...] = encode(part, factor, channels)
    else:
        message[:states, :] = encode(state_part, factor, channels)
        message[states:, :] = encode(grad_part, factor, channels)


def prepare(staged):
    tokens, channels = staged.made["enter"].shape
    width = staged.made["factor"].shape[1]
    log_ref = staged.take("log")
    picker = head_picker(log_ref.shape[0], channels, width)
    count_column, count_row, scale, rising, falling, carry_in, carry_out, factor = decays(
        log_ref, staged.take("doc"), picker
    )
    staged.put("enter", carry_in[:, :channels])
    staged.put("leave", (scale * carry_out)[:, :channels])
    staged.put("rise", rising[:, :channels])
    staged.put("fall", (scale * falling)[:, :channels])
    staged.put("factor", jnp.broadcast_to(factor, staged.made["factor"].shape))
    staged.put("expander", head_expander(channels, width))
    rows, columns = iota((tokens, tokens), 0), iota((tokens, tokens), 1)
    same = count_column == count_row
    causal = (rows >= columns) & same
    anticausal = (rows <= columns) & same
    b_rows, c_rows = staged.take("b_in")[...], staged.take("c_in")[...]
    staged.put("causal", jnp.where(causal, 1.0, 0.0))
    staged.put("crossed", jnp.where(causal, dot(c_rows, b_rows, TN), 0.0))
    staged.put("crossed_back", jnp.where(anticausal, dot(b_rows, c_rows, TN), 0.0))
    staged.put("b", b_rows)
    staged.put("c", c_rows)


def put_summary(staged, name, vectors, values):
    part = staged.made[name]
    part[...] = jnp.zeros_like(part)
    part[:, : values.shape[1]] = dot(staged.take(vectors)[...], values)


def project(staged, rows_ref):
    assemble(staged, "rows", rows_ref)
    rows = rows_ref[...]
    pre = dot(rows, staged.take("w_in")[...], NT)
    staged.put("pre", pre)
    x_rows = (pre * jax.nn.sigmoid(pre)).astype(BF16)
    staged.put("x", x_rows)
    leaving = (x_rows.astype(F32) * staged.take("leave")[...]).astype(BF16)
    staged.put("leaving", leaving)
    put_summary(staged, "state", "b", leaving)
    gate = dot(rows, staged.take("w_gate")[...], NT)
    staged.put("gate", gate)
    staged.put("gated", gate * jax.nn.sigmoid(gate))


def front(staged, grad_ref):
    channels = staged.made["mix"].shape[1]
    assemble(staged, "grad", grad_ref)
    mix = dot(grad_ref[...], staged.take("w_out")[...], NT)
    staged.put("mix", mix)
    y_grads = (mix * staged.take("gated")[...]).astype(BF16)
    staged.put("y", y_grads)
    entering = (y_grads.astype(F32) * staged.take("enter")[...]).astype(BF16)
    staged.put("entering", entering)
    put_summary(staged, "grad", "c", entering)
    state_part, grad_part = staged.take("state")[...], staged.made["grad"][...]
    put_message(staged, state_part, grad_part, staged.take("factor")[...], channels, 1)


def join(channels, bit):
    def body(staged):
        received, expander = staged.take("received"), staged.take("expander")[...]
        factor, state, grad = (staged.take(name)[...] for name in ("factor", "state", "grad"))
        states = state.shape[0]
        other_state = received[:states, :].astype(F32)
        other_grad = received[states:, :].astype(F32)
        other = decode(received[:states, :], expander)
        later = partner_is_later(bit)
        if bit == 1:
            before = jnp.where(later, 1.0, other), jnp.where(later, 0.0, other_state)
            behind = jnp.where(later, other, 1.0), jnp.where(later, other_grad, 0.0)
        else:
            keep, held, back_keep, back_held = (
                staged.take(name)[...] for name in ("keep", "held", "back_keep", "back_held")
            )
            before = (
                jnp.where(later, keep, keep * other),
                jnp.where(later, held, keep * other_state + held),
            )
            behind = (
                jnp.where(later, back_keep * other, back_keep),
                jnp.where(later, back_keep * other_grad + back_held, back_held),
            )
        staged.put("keep", before[0])
        staged.put("held", before[1])
        staged.put("back_keep", behind[0])
        staged.put("back_held", behind[1])
        joined_state = jnp.where(later, other * state + other_state, factor * other_state + state)
        joined_grad = jnp.where(later, grad + factor * other_grad, other_grad + other * grad)
        joined = factor * other
        put_message(staged, joined_state, joined_grad, joined, channels, 2 * bit)
        if "state" in staged.made:
            staged.put("state", joined_state)
            staged.put("grad", joined_grad)
            staged.put("factor", joined)

    return body


def slopes(staged):
    staged.put("pre_slope", silu_slope(staged.take("pre")[...]))
    staged.put("gate_slope", staged.take("mix")[...] * silu_slope(staged.take("gate")[...]))


def local_vectors(staged):
    upper = staged.take("y")[...].astype(F32) * staged.take("rise")[...]
    lower = staged.take("x")[...].astype(F32) * staged.take("fall")[...]
    causal = staged.take("causal")[...] > 0.0
    high, low = two_parts(jnp.where(causal, fine_dot(upper, lower, NT), 0.0))
    b_rows, c_rows = staged.take("b")[...], staged.take("c")[...]
    states = b_rows.shape[0]
    bc = staged.made["bc"]
    bc[:states, :] = dot(c_rows, high) + dot(c_rows, low)
    bc[states:, :] = dot(b_rows, high, NT) + dot(b_rows, low, NT)


def local_channels(staged):
    x_rows, y_grads = staged.take("x")[...].astype(F32), staged.take("y")[...].astype(F32)
    rise, fall, skip = staged.take("rise")[...], staged.take("fall")[...], staged.take("skip")[...]
    ssm = rise * fine_dot(staged.take("crossed")[...], x_rows * fall)
    staged.put("ssm", ssm + skip * x_rows)
    x_grad = fall * fine_dot(staged.take("crossed_back")[...], y_grads * rise)
    staged.put("x_grad", x_grad + skip * y_grads)


def put_pieces(staged, steps, gate_rows, pre_rows, bc):
    piece = gate_rows.shape[0] // len(steps)
    partial = dot(gate_rows, staged.take("w_gate")[...])
    partial += dot(pre_rows, staged.take("w_in")[...])
    depth = partial.shape[1]
    for at, step in enumerate(steps):
        made = staged.made["part%d" % step]
        split = made.shape[1] - bc.shape[1]
        if split > depth:
            made[:, split - LANE : split] = jnp.zeros((piece, LANE), made.dtype)
        made[:, :depth] = partial[at * piece : (at + 1) * piece, :].astype(made.dtype)
        made[: bc.shape[0], split:] = bc.astype(made.dtype)


def back(bit, urgent, later_steps):
    def body(staged, gate_ref, pre_ref):
        entry = staged.take("entry")[...]
        states, channels = entry.shape
        received = staged.take("received")
        other_part = received[:, :channels].astype(F32)
        other = decode(received[...], staged.take("expander")[...])[:, :channels]
        later = partner_is_later(bit)
        keep, held, back_keep, back_held = (
            staged.take(name)[:, :channels] for name in ("keep", "held", "back_keep", "back_held")
        )
        state = jnp.where(later, entry, other * entry + other_part)
        state_in = (keep * state + held).astype(BF16)
        grad_in = jnp.where(later, back_keep * other_part + back_held, back_held).astype(BF16)
        carried = dot(staged.take("c")[...], state_in, TN)
        ssm_out = staged.take("ssm")[...] + staged.take("enter")[...] * carried
        gate_ref[...] = (
            ssm_out.astype(BF16).astype(F32) * staged.take("gate_slope")[...]
        ).astype(BF16)
        carried = dot(staged.take("b")[...], grad_in, TN)
        x_grad = staged.take("x_grad")[...] + staged.take("leave")[...] * carried
        pre_ref[...] = (
            x_grad.astype(BF16).astype(F32) * staged.take("pre_slope")[...]
        ).astype(BF16)
        bc = staged.made["bc"]
        local = staged.take("bc")
        bc[:states, :] = local[:states, :] + dot(grad_in, staged.take("leaving")[...], NT)
        bc[states:, :] = local[states:, :] + dot(state_in, staged.take("entering")[...], NT)
        piece = gate_ref.shape[0] // len(urgent + later_steps)

        def gathered(ref, steps):
            tp = lax.axis_index("tp")
            starts = [pl.multiple_of((tp ^ step) * piece, piece) for step in steps]
            return jnp.concatenate([ref[pl.ds(start, piece), :] for start in starts], axis=0)

        staged.put("gate_rows", gathered(gate_ref, later_steps))
        staged.put("pre_rows", gathered(pre_ref, later_steps))
        put_pieces(staged, urgent, gathered(gate_ref, urgent), gathered(pre_ref, urgent), bc[...])

    return body


def rest(steps):
    def body(staged):
        gate_rows, pre_rows = staged.take("gate_rows")[...], staged.take("pre_rows")[...]
        put_pieces(staged, steps, gate_rows, pre_rows, staged.take("bc")[...])

    return body


def add(staged):
    values = [staged.take(name)[...].astype(F32) for name in staged.refs]
    staged.put("sum", sum(values).astype(BF16))


def total(staged):
    depth = staged.made["grad"].shape[1]
    states, tokens = staged.made["b"].shape
    received = [staged.take(name) for name in staged.refs]
    split = received[0].shape[1] - tokens
    staged.put("grad", sum(part[:, :depth].astype(F32) for part in received).astype(BF16))
    staged.put("b", sum(part[:states, split:].astype(F32) for part in received))
    staged.put("c", sum(part[states : 2 * states, split:].astype(F32) for part in received))


def swap_masks(parts):
    masks, bit = [], parts // 2
    while bit:
        masks.append(bit)
        bit //= 2
    return masks


def reached(masks):
    steps = {0}
    for mask in masks:
        steps |= {step ^ mask for step in steps}
    return steps


def shards(
    layer_input, out_grad, w_in, w_gate, w_out, b_proj, c_proj, log_decay, d_skip, entry_state,
    doc_start,
):
    owners, parts = lax.axis_size("seq"), lax.axis_size("tp")
    assert owners > 2 and owners & (owners - 1) == 0 and parts & (parts - 1) == 0
    piece, depth = layer_input.shape
    tokens = piece * parts
    channels = w_in.shape[0]
    states = b_proj.shape[0]
    width = round_up(channels + 2 * SLOT, LANE)
    wide = near((tokens, channels), F32)
    half = near((tokens, channels), BF16)
    square = near((tokens, tokens), F32)
    row = near((states, tokens), BF16)
    summary = near((states, width), F32)

    def ordered(value, after):
        return lax.optimization_barrier((value, after))[0]

    def swap(value, axis, bit):
        size = lax.axis_size(axis)
        return lax.ppermute(value, axis, [(at, at ^ bit) for at in range(size)])

    def call(body, name, ins, outs, **options):
        ins = {key: near(value) if hasattr(value, "shape") else value for key, value in ins.items()}
        return staged_call(body, name, ins, outs, **options)

    def pick(source, names):
        return {name: source[name] for name in names}

    far_ins = dict(
        log=log_decay, doc=doc_start.reshape(1, tokens), b_in=b_proj, c_in=c_proj, w_gate=w_gate,
        w_in=w_in, w_out=w_out, rows0=layer_input, grad0=out_grad, entry=entry_state,
        skip=d_skip.reshape(1, channels),
    )
    ready = call(
        prepare, "prepare", {name: far(value) for name, value in far_ins.items()},
        dict(enter=wide, leave=wide, rise=wide, fall=wide, factor=summary,
             expander=near((width - channels // LANE * LANE, width), BF16), causal=square,
             crossed=square, crossed_back=square, b=row, c=row),
        flops=8 * tokens * channels * tokens,
        through=("w_gate", "w_in", "w_out", "rows0", "grad0", "entry", "skip"),
    )
    grad_blocks, row_blocks = {0: out_grad}, {0: layer_input}
    masks = swap_masks(parts)
    for mask in masks:
        for blocks in (row_blocks, grad_blocks):
            for step in list(blocks):
                block = blocks[step]
                if mask != masks[0]:
                    block = ordered(block, ready["expander"])
                blocks[step ^ mask] = swap(block, "tp", mask)
    rows = {"rows%d" % step: block for step, block in row_blocks.items()}
    grads = {"grad%d" % step: block for step, block in grad_blocks.items()}
    rows["rows0"], grads["grad0"] = ready["rows0"], ready["grad0"]
    assembled = pltpu.VMEM((tokens, depth), BF16)
    both = near((2 * states, width), BF16)
    one = near((states, width), BF16)
    first = call(
        project, "project",
        dict(rows, **pick(ready, ("w_gate", "w_in", "b", "leave"))),
        dict(gate=wide, gated=wide, pre=wide, x=half, leaving=half, state=summary),
        flops=4 * tokens * channels * depth, scratch=(assembled,),
    )
    first.update(call(
        front, "front",
        dict(grads, **pick(ready, ("w_out", "c", "enter", "factor")),
             **pick(first, ("gated", "state"))),
        dict(mix=wide, y=half, entering=half, grad=summary, message=both),
        flops=2 * tokens * channels * depth, scratch=(assembled,),
    ))
    group = dict(pick(first, ("state", "grad")), factor=ready["factor"])
    received = swap(first["message"], "seq", 1)
    slope = call(
        slopes, "slopes", pick(first, ("pre", "gate", "mix")),
        dict(pre_slope=wide, gate_slope=wide), flops=tokens * channels * 32,
    )
    received = ordered(received, slope["pre_slope"])
    x_rows, y_grads = first["x"], first["y"]
    results, bit = {}, 1
    while 2 * bit < owners:
        last = 4 * bit >= owners
        outs = dict(keep=summary, held=summary, back_keep=summary, back_held=summary,
                    message=one if last else both)
        if not last:
            outs.update(state=summary, grad=summary, factor=summary)
        group = call(
            join(channels, bit), "join", dict(group, received=received, expander=ready["expander"]),
            outs,
        )
        received = swap(group.pop("message"), "seq", 2 * bit)
        if bit == 1:
            results.update(call(
                local_vectors, "local_vectors",
                dict(pick(ready, ("rise", "fall", "causal", "b", "c")),
                     x=ordered(x_rows, group["keep"]), y=y_grads),
                dict(bc=near((2 * states, tokens), F32)), flops=8 * tokens * channels * tokens,
            ))
            if not last:
                received = ordered(received, results["bc"])
        if last:
            results.update(call(
                local_channels, "local_channels",
                dict(pick(ready, ("rise", "fall", "crossed", "crossed_back", "skip")),
                     x=ordered(x_rows, group["keep"]), y=y_grads),
                dict(ssm=wide, x_grad=wide), flops=16 * tokens * channels * tokens,
            ))
        bit *= 2
    span = round_up(depth, LANE) + tokens
    graded = pltpu.VMEM((tokens, channels), BF16)
    kept = reached(masks[:-1])
    urgent = sorted(set(range(parts)) - kept - {masks[-1]})
    others = sorted(set(range(parts)) - set(urgent))
    pieces = {"part%d" % step: near((piece, span), F32 if step in kept else BF16)
              for step in range(parts)}
    rest_rows = near((piece * len(others), channels), BF16)
    held = call(
        back(bit, urgent, others), "back",
        dict(group, received=received, **results, **slope, **pick(first, ("entering", "leaving")),
             **pick(ready, ("entry", "expander", "enter", "leave", "b", "c", "w_gate", "w_in"))),
        dict(pick(pieces, ["part%d" % step for step in urgent]), gate_rows=rest_rows,
             pre_rows=rest_rows, bc=near((2 * states, tokens), F32)),
        flops=4 * len(urgent) * piece * channels * depth, scratch=(graded, graded),
    )
    held.update(call(
        rest(others), "rest",
        dict(pick(held, ("gate_rows", "pre_rows", "bc")), **pick(ready, ("w_gate", "w_in"))),
        pick(pieces, ["part%d" % step for step in others]),
        flops=4 * len(others) * piece * channels * depth,
    ))
    terms = {step: [held["part%d" % step]] for step in range(parts)}

    def summed(values):
        if len(values) == 1:
            return values[0]
        ins = {"term%d" % at: value for at, value in enumerate(values)}
        return call(add, "add", ins, dict(sum=near((piece, span), BF16)))["sum"]

    for level in reversed(range(len(masks))):
        for step in sorted(set(terms) - reached(masks[:level]), reverse=True):
            terms[step ^ masks[level]].append(swap(summed(terms.pop(step)), "tp", masks[level]))
    result = call(
        total, "total", {"term%d" % at: value for at, value in enumerate(terms[0])},
        dict(grad=near((piece, depth), BF16), b=near((states, tokens), F32),
             c=near((states, tokens), F32)),
    )
    return result["grad"], result["b"], result["c"]


def solution(mesh):
    in_specs = (
        P(("seq", "tp"), None),
        P(("seq", "tp"), None),
        P("tp", None),
        P("tp", None),
        P("tp", None),
        P(None, "seq"),
        P(None, "seq"),
        P(None, "seq"),
        P("tp"),
        P(None, "tp"),
        P("seq"),
    )
    out_specs = (P(("seq", "tp"), None), P(None, "seq"), P(None, "seq"))
    return jax.shard_map(shards, mesh=mesh, in_specs=in_specs, out_specs=out_specs, check_vma=False)
```

time: 317 us -> 32.5 us (0.10); the launches traced: 313 us -> 32.4 us
  blocking collectives: 98.2 us -> 0 us
  local copies, waits for them, and re-layouts: 73.5 us -> 0.01 us
  other arithmetic: 53.1 us -> 0 us
  matrix products: 22.9 us -> 0 us
  starting transfers between devices: 34.5 us -> 12.7 us
  between operations: 14.7 us -> 0.73 us
  Pallas kernels: 0 us -> 7.72 us
  waiting for transfers between devices: 16 us -> 11.2 us
    all_gather x5 -> x0, blocking collectives: 87.5 us -> none  [the longest x1 26.9 us: shards(): lax.all_gather(c_proj, 'seq', axis=1, tiled=True)]
    all_to_all x7 -> x0, starting transfers between devices: 34.4 us -> none  [the longest x1 7.28 us: shards(): lax.all_to_all(pack(log_rows.astype(jnp.bfloat16)), 'seq', split_axis=0,...]
    dot_general x18 -> x0, matrix products: 22.9 us -> none  [the longest x1 2.27 us: block_pass(): jnp.dot(lower_rows, crossed.T, precision=FULL_PRECISION)]
    slice x25 -> x0, local copies, waits for them, and re-layouts: 21.6 us -> none  [the longest x12 7.56 us: block_scans(): lax.associative_scan(combine_pairs, (factor, grad_part), reverse=True)]
    pad x15 -> x0, local copies, waits for them, and re-layouts: 20.4 us -> none  [the longest x6 10.5 us: block_scans(): lax.associative_scan(combine_pairs, (factor, grad_part), reverse=True)]
    unnamed x85 -> x4, local copies, waits for them, and re-layouts: 19 us -> 0.01 us
    add x20 -> x0, other arithmetic: 16.5 us -> none  [the longest x8 6.26 us: combine_pairs(): later_pair[0][..., None, :] * earlier[1] + later_pair[1]]
    all_to_all x7 -> x0, waiting for transfers between devices: 16 us -> none  [the longest x1 6.82 us: shards(): lax.all_to_all(c_part.reshape(state_size, owners, tokens_here), 'seq', sp...]
  transfers between devices with their start and end apart: 8 -> 12, of which waited for: 4 -> 8; matrix products, arithmetic and copies ran while one was open for 19% -> 0% of each run, Pallas kernels for 0% -> 16%
where the time goes in v1:
time: 32.5 us; the launch traced here: 32.4 us
  starting transfers between devices  12.7 us (39%)
  waiting for transfers between devices  11.2 us (34%)
  Pallas kernels  7.72 us (24%)
  between operations  0.73 us (2%)
    ppermute x12, starting transfers between devices, swap(): return lax.ppermute(value, axis, [(at, at ^ bit) for at in range(size)])  12.7 us
    ppermute x12, waiting for transfers between devices, swap(): return lax.ppermute(value, axis, [(at, at ^ bit) for at in range(size)])  11.2 us
    pallas_call x12, Pallas kernels, staged_call(): pl.pallas_call(kernel, name=name, out_shape=[jax.ShapeDtypeStruct(shape,...  7.72 us
  transfers between devices with their start and end apart: 12, of which 8 were waited for; matrix products, arithmetic and copies ran while one was open for 0% of the time, Pallas kernels for 16%

profile of v1, /device:TPU:0, one launch (start us, length us, event | category | flops | bytes accessed | tf_op | source)
XLA Modules:
  0.0 32.4 jit_solution(3658929102652529061)
XLA Ops:
  0.6 3.0 %collective-permute-start = (bf16[32,1600]{1,0:T(8,128)(2,1)}, bf16[32,1600]{1,0:T(8,128)(2,1)S(1)}, u32[]{:S(2)}, u32[]{:S(2)}) collective-permute-start(bf16[32,1600]{1,0:T(8,128)(2,1)} %refs_7_.1), channel_id=1, source_target_pairs={{0,2},{1,3},{2,0},{3,1},{4,6},{5,7},{6,4},{7,5},{8,10},{9,11},{10,... | collective-permute-start | bytes 307208 | tf_op jit(solution)/shard_map/ppermute | solution.py:482
  3.7 2.3 %prepare.1 = (f32[128,400]{1,0:T(8,128)S(1)}, f32[128,400]{1,0:T(8,128)S(1)}, f32[128,400]{1,0:T(8,128)S(1)}, f32[128,400]{1,0:T(8,128)S(1)}, f32[16,512]{1,0:T(...) custom-call(bf16[25,128]{1,0:T(8,128)(2,1)} %refs_0_.1, ...), custom_call_target="tpu_custom_call" | custom-call | flops 52428800 | bytes 1048576 | tf_op jit(solution)/shard_map/prepare/pallas_call | solution.py:178
  6.1 1.5 %collective-permute-done.refs_1_ = bf16[32,1600]{1,0:T(8,128)(2,1)S(1)} collective-permute-done((bf16[32,1600]{1,0:T(8,128)(2,1)}, bf16[32,1600]{1,0:T(8,128)(2,1)S(1)}, u32[]{:S(2)}, u32[]{:S(2)}) %collective-permute-start) | collective-permute-done | bytes 102432 | tf_op jit(solution)/shard_map/ppermute | solution.py:482
  7.6 0.5 %collective-permute-start.4 = (bf16[32,1600]{1,0:T(8,128)(2,1)S(1)}, bf16[32,1600]{1,0:T(8,128)(2,1)S(1)}, u32[]{:S(2)}, u32[]{:S(2)}) collective-permute-start(bf16[32,1600]{1,0:T(8,128)(2,1)S(1)} %copy-done.1), channel_id=1, source_target_pairs={{0,1},{1,0},{2,3},{3,2},{4,5},{5,4},{6,7},{7,6},{8,9},{9,8},{10,11... | collective-permute-start | bytes 307208 | tf_op jit(solution)/shard_map/ppermute | solution.py:482
  8.1 1.0 %collective-permute-done.3.refs_1_ = bf16[32,1600]{1,0:T(8,128)(2,1)S(1)} collective-permute-done((bf16[32,1600]{1,0:T(8,128)(2,1)}, bf16[32,1600]{1,0:T(8,128)(2,1)S(1)}, u32[]{:S(2)}, u32[]{:S(2)}) %collective-permute-start.3) | collective-permute-done | bytes 102432 | tf_op jit(solution)/shard_map/ppermute | solution.py:482
  9.1 1.1 %project.1 = (f32[128,400]{1,0:T(8,128)S(1)}, f32[128,400]{1,0:T(8,128)S(1)}, f32[128,400]{1,0:T(8,128)S(1)}, bf16[128,400]{1,0:T(8,128)(2,1)S(1)}, bf16[128,400]{1,0:T(8,128)(2,1)S(1)}, /*index=5*/f32[16,512]{1,0:T(8,128)S(1)}) custom-call(bf16[32,1600]{1,0:T(8,128)(2,1)S(1)} %get-tuple-element.64.refs_0_, ...), custom_call_target="tpu_custom_call" | custom-call | flops 327680000 | bytes 1048576 | tf_op jit(solution)/shard_map/project/pallas_call | solution.py:178
  10.2 0.2 collective-permute-done.5.refs_3_
  10.4 0.7 %front.1 = (f32[128,400]{1,0:T(8,128)S(1)}, bf16[128,400]{1,0:T(8,128)(2,1)S(1)}, bf16[128,400]{1,0:T(8,128)(2,1)S(1)}, f32[16,512]{1,0:T(8,128)S(1)}, bf16[32,512]{1,0:T(8,128)(2,1)S(1)}) custom-call(bf16[32,1600]{1,0:T(8,128)(2,1)S(1)} %get-tuple-element.73.refs_0_, bf16[32,1600]{1,0:T(8,128)(2,1)S(1)} %collective-permute-done.3.refs_1_, ...), custom_call_target="tpu_custom_call" | custom-call | flops 163840000 | bytes 1048576 | tf_op jit(solution)/shard_map/front/pallas_call | solution.py:178
  11.1 1.8 %collective-permute-start.6 = (bf16[32,512]{1,0:T(8,128)(2,1)S(1)}, bf16[32,512]{1,0:T(8,128)(2,1)S(1)}, u32[]{:S(2)}, u32[]{:S(2)}) collective-permute-start(bf16[32,512]{1,0:T(8,128)(2,1)S(1)} %get-tuple-element.82), channel_id=1, source_target_pairs={{0,4},{4,0},{8,12},{12,8},{16,20},{20,16},{24,28},{28,24},{1,5},{5... | collective-permute-start | bytes 98312 | tf_op jit(solution)/shard_map/ppermute | solution.py:482
  12.9 0.2 slopes.1
  13.1 2.0 %collective-permute-done.6.refs_3_ = bf16[32,512]{1,0:T(8,128)(2,1)S(1)} collective-permute-done((bf16[32,512]{1,0:T(8,128)(2,1)S(1)}, bf16[32,512]{1,0:T(8,128)(2,1)S(1)}, u32[]{:S(2)}, u32[]{:S(2)}) %collective-permute-start.6) | collective-permute-done | bytes 32800 | tf_op jit(solution)/shard_map/ppermute | solution.py:482
  15.2 1.9 %collective-permute-start.7 = (bf16[32,512]{1,0:T(8,128)(2,1)S(1)}, bf16[32,512]{1,0:T(8,128)(2,1)S(1)}, u32[]{:S(2)}, u32[]{:S(2)}) collective-permute-start(bf16[32,512]{1,0:T(8,128)(2,1)S(1)} %get-tuple-element.95), channel_id=1, source_target_pairs={{0,8},{4,12},{8,0},{12,4},{16,24},{20,28},{24,16},{28,20},{1,9},{5... | collective-permute-start | bytes 98312 | tf_op jit(solution)/shard_map/ppermute | solution.py:482
  17.1 0.5 %local_vectors.1.refs_5_ = f32[32,128]{1,0:T(8,128)S(1)} custom-call(f32[128,400]{1,0:T(8,128)S(1)} %get-tuple-element.96.refs_0_, f32[128,400]{1,0:T(8,128)S(1)} %get-tuple-element.97.refs_1_, f32[128,128]{1,0:T(8,128)S(1)} %get-tuple-element.98.refs_2_, bf16[16,128]{1,0:T(8,128)(2,1)S(1)} %get-tuple-element.70.refs_6_.refs_3_.refs_16_, ...), custom_call_target="tpu_custom_call" | custom-call | flops 52428800 | bytes 1048576 | tf_op jit(solution)/shard_map/local_vectors/pallas_call | solution.py:178
  17.6 1.6 %collective-permute-done.7.refs_7_ = bf16[32,512]{1,0:T(8,128)(2,1)S(1)} collective-permute-done((bf16[32,512]{1,0:T(8,128)(2,1)S(1)}, bf16[32,512]{1,0:T(8,128)(2,1)S(1)}, u32[]{:S(2)}, u32[]{:S(2)}) %collective-permute-start.7) | collective-permute-done | bytes 32800 | tf_op jit(solution)/shard_map/ppermute | solution.py:482
  19.2 0.1 join.3
  19.3 2.9 %collective-permute-start.8 = (bf16[16,512]{1,0:T(8,128)(2,1)S(1)}, bf16[16,512]{1,0:T(8,128)(2,1)S(1)}, u32[]{:S(2)}, u32[]{:S(2)}) collective-permute-start(bf16[16,512]{1,0:T(8,128)(2,1)S(1)} %get-tuple-element.107), channel_id=1, source_target_pairs={{0,16},{4,20},{8,24},{12,28},{16,0},{20,4},{24,8},{28,12},{1,17},{... | collective-permute-start | bytes 49160 | tf_op jit(solution)/shard_map/ppermute | solution.py:482
  22.2 0.4 %local_channels.1 = (f32[128,400]{1,0:T(8,128)S(1)}, f32[128,400]{1,0:T(8,128)S(1)}) custom-call(f32[128,400]{1,0:T(8,128)S(1)} %get-tuple-element.96.refs_0_, f32[128,400]{1,0:T(8,128)S(1)} %get-tuple-element.97.refs_1_, f32[128,128]{1,0:T(8,128)S(1)} %get-tuple-element.108.refs_2_, f32[128,128]{1,0:T(8,128)S(1)} %get-tuple-element.109.refs_3_, ...), custom_call_target="tpu_custom_call" | custom-call | flops 104857600 | bytes 1048576 | tf_op jit(solution)/shard_map/local_channels/pallas_call | solution.py:178
  22.6 1.4 %collective-permute-done.8.refs_4_ = bf16[16,512]{1,0:T(8,128)(2,1)S(1)} collective-permute-done((bf16[16,512]{1,0:T(8,128)(2,1)S(1)}, bf16[16,512]{1,0:T(8,128)(2,1)S(1)}, u32[]{:S(2)}, u32[]{:S(2)}) %collective-permute-start.8) | collective-permute-done | bytes 16416 | tf_op jit(solution)/shard_map/ppermute | solution.py:482
  24.0 1.0 %back.1 = (bf16[32,1792]{1,0:T(8,128)(2,1)S(1)}, bf16[96,400]{1,0:T(8,128)(2,1)S(1)}, bf16[96,400]{1,0:T(8,128)(2,1)S(1)}, f32[32,128]{1,0:T(8,128)S(1)}) custom-call(f32[16,512]{1,0:T(8,128)S(1)} %get-tuple-element.103.refs_0_, f32[16,512]{1,0:T(8,128)S(1)} %get-tuple-element.104.refs_1_, f32[16,512]{1,0:T(8,128)S(1)} %get-tuple-element.105.refs_2_, ...), custom_call_target="tpu_custom_call" | custom-call | flops 81920000 | bytes 1048576 | tf_op jit(solution)/shard_map/back/pallas_call | solution.py:178
  25.1 0.6 %rest.1 = (f32[32,1792]{1,0:T(8,128)S(1)}, bf16[32,1792]{1,0:T(8,128)(2,1)S(1)}, f32[32,1792]{1,0:T(8,128)S(1)}) custom-call(bf16[96,400]{1,0:T(8,128)(2,1)S(1)} %get-tuple-element.118.refs_0_, bf16[96,400]{1,0:T(8,128)(2,1)S(1)} %get-tuple-element.119.refs_1_, f32[32,128]{1,0:T(8,128)S(1)} %get-tuple-element.120.refs_2_, ...), custom_call_target="tpu_custom_call" | custom-call | flops 245760000 | bytes 1048576 | tf_op jit(solution)/shard_map/rest/pallas_call | solution.py:178
  25.7 0.6 %collective-permute-start.9 = (bf16[32,1792]{1,0:T(8,128)(2,1)S(1)}, bf16[32,1792]{1,0:T(8,128)(2,1)S(1)}, u32[]{:S(2)}, u32[]{:S(2)}) collective-permute-start(bf16[32,1792]{1,0:T(8,128)(2,1)S(1)} %get-tuple-element.122), channel_id=1, source_target_pairs={{0,1},{1,0},{2,3},{3,2},{4,5},{5,4},{6,7},{7,6},{8,9},{9,8},{10,11... | collective-permute-start | bytes 344072 | tf_op jit(solution)/shard_map/ppermute | solution.py:482
  26.4 1.8 %collective-permute-start.11 = (bf16[32,1792]{1,0:T(8,128)(2,1)S(1)}, bf16[32,1792]{1,0:T(8,128)(2,1)S(1)}, u32[]{:S(2)}, u32[]{:S(2)}) collective-permute-start(bf16[32,1792]{1,0:T(8,128)(2,1)S(1)} %add.1), channel_id=1, source_target_pairs={{0,2},{1,3},{2,0},{3,1},{4,6},{5,7},{6,4},{7,5},{8,10},{9,11},{10,... | collective-permute-start | bytes 344072 | tf_op jit(solution)/shard_map/ppermute | solution.py:482
  28.2 3.5 %collective-permute-done.11.refs_2_ = bf16[32,1792]{1,0:T(8,128)(2,1)S(1)} collective-permute-done((bf16[32,1792]{1,0:T(8,128)(2,1)S(1)}, bf16[32,1792]{1,0:T(8,128)(2,1)S(1)}, u32[]{:S(2)}, u32[]{:S(2)}) %collective-permute-start.11) | collective-permute-done | bytes 114720 | tf_op jit(solution)/shard_map/ppermute | solution.py:482
  31.7 0.7 %total.1 = (bf16[32,1600]{1,0:T(8,128)(2,1)}, f32[16,128]{1,0:T(8,128)}, f32[16,128]{1,0:T(8,128)}) custom-call(f32[32,1792]{1,0:T(8,128)S(1)} %get-tuple-element.121.refs_0_, bf16[32,1792]{1,0:T(8,128)(2,1)S(1)} %collective-permute-done.9.refs_1_, bf16[32,1792]{1,0:T(8,128)(2,1)S(1)} %collective-permute-done.11.refs_2_), custom_call_target="tpu_custom_call" | custom-call | bytes 1048576 | tf_op jit(solution)/shard_map/total/pallas_call | solution.py:178
  (16 shorter events, 0.5 us)
Async XLA Ops:
  0.6 7.0 %collective-permute-start = (bf16[32,1600]{1,0:T(8,128)(2,1)}, bf16[32,1600]{1,0:T(8,128)(2,1)S(1)}, u32[]{:S(2)}, u32[]{:S(2)}) collective-permute-start(bf16[32,1600]{1,0:T(8,128)(2,1)} %refs_7_.1), channel_id=1, source_target_pairs={{0,2},{1,3},{2,0},{3,1},{4,6},{5,7},{6,4},{7,5},{8,10},{9,11},{10,... | collective-permute-start | bytes 307208 | tf_op jit(solution)/shard_map/ppermute | solution.py:482
  3.6 5.5 %collective-permute-start.3 = (bf16[32,1600]{1,0:T(8,128)(2,1)}, bf16[32,1600]{1,0:T(8,128)(2,1)S(1)}, u32[]{:S(2)}, u32[]{:S(2)}) collective-permute-start(bf16[32,1600]{1,0:T(8,128)(2,1)} %refs_8_.1), channel_id=1, source_target_pairs={{0,2},{1,3},{2,0},{3,1},{4,6},{5,7},{6,4},{7,5},{8,10},{9,11},{10,... | collective-permute-start | bytes 307208 | tf_op jit(solution)/shard_map/ppermute | solution.py:482
  3.7 2.3 %copy-start = (bf16[32,1600]{1,0:T(8,128)(2,1)S(1)}, bf16[32,1600]{1,0:T(8,128)(2,1)}, u32[]{:S(2)}) copy-start(bf16[32,1600]{1,0:T(8,128)(2,1)} %refs_7_.1) | copy-start | bytes 307204
  3.7 3.9 %copy-start.1 = (bf16[32,1600]{1,0:T(8,128)(2,1)S(1)}, bf16[32,1600]{1,0:T(8,128)(2,1)}, u32[]{:S(2)}) copy-start(bf16[32,1600]{1,0:T(8,128)(2,1)} %refs_8_.1) | copy-start | bytes 307204
  6.1 3.0 %collective-permute-start.1 = (bf16[32,1600]{1,0:T(8,128)(2,1)S(1)}, bf16[32,1600]{1,0:T(8,128)(2,1)S(1)}, u32[]{:S(2)}, u32[]{:S(2)}) collective-permute-start(bf16[32,1600]{1,0:T(8,128)(2,1)S(1)} %copy-done), channel_id=1, source_target_pairs={{0,1},{1,0},{2,3},{3,2},{4,5},{5,4},{6,7},{7,6},{8,9},{9,8},{10,11... | collective-permute-start | bytes 307208 | tf_op jit(solution)/shard_map/ppermute | solution.py:482
  7.6 1.5 %collective-permute-start.2 = (bf16[32,1600]{1,0:T(8,128)(2,1)S(1)}, bf16[32,1600]{1,0:T(8,128)(2,1)S(1)}, u32[]{:S(2)}, u32[]{:S(2)}) collective-permute-start(bf16[32,1600]{1,0:T(8,128)(2,1)S(1)} %collective-permute-done.refs_1_), channel_id=1, source_target_pairs={{0,1},{1,0},{2,3},{3,2},{4,5},{5,4},{6,7},{7,6},{8,9},{9,8},{10,11... | collective-permute-start | bytes 307208 | tf_op jit(solution)/shard_map/ppermute | solution.py:482
  7.6 2.6 %collective-permute-start.4 = (bf16[32,1600]{1,0:T(8,128)(2,1)S(1)}, bf16[32,1600]{1,0:T(8,128)(2,1)S(1)}, u32[]{:S(2)}, u32[]{:S(2)}) collective-permute-start(bf16[32,1600]{1,0:T(8,128)(2,1)S(1)} %copy-done.1), channel_id=1, source_target_pairs={{0,1},{1,0},{2,3},{3,2},{4,5},{5,4},{6,7},{7,6},{8,9},{9,8},{10,11... | collective-permute-start | bytes 307208 | tf_op jit(solution)/shard_map/ppermute | solution.py:482
  9.1 1.3 %collective-permute-start.5 = (bf16[32,1600]{1,0:T(8,128)(2,1)S(1)}, bf16[32,1600]{1,0:T(8,128)(2,1)S(1)}, u32[]{:S(2)}, u32[]{:S(2)}) collective-permute-start(bf16[32,1600]{1,0:T(8,128)(2,1)S(1)} %collective-permute-done.3.refs_1_), channel_id=1, source_target_pairs={{0,1},{1,0},{2,3},{3,2},{4,5},{5,4},{6,7},{7,6},{8,9},{9,8},{10,11... | collective-permute-start | bytes 307208 | tf_op jit(solution)/shard_map/ppermute | solution.py:482
  11.1 3.9 %collective-permute-start.6 = (bf16[32,512]{1,0:T(8,128)(2,1)S(1)}, bf16[32,512]{1,0:T(8,128)(2,1)S(1)}, u32[]{:S(2)}, u32[]{:S(2)}) collective-permute-start(bf16[32,512]{1,0:T(8,128)(2,1)S(1)} %get-tuple-element.82), channel_id=1, source_target_pairs={{0,4},{4,0},{8,12},{12,8},{16,20},{20,16},{24,28},{28,24},{1,5},{5... | collective-permute-start | bytes 98312 | tf_op jit(solution)/shard_map/ppermute | solution.py:482
  15.2 4.0 %collective-permute-start.7 = (bf16[32,512]{1,0:T(8,128)(2,1)S(1)}, bf16[32,512]{1,0:T(8,128)(2,1)S(1)}, u32[]{:S(2)}, u32[]{:S(2)}) collective-permute-start(bf16[32,512]{1,0:T(8,128)(2,1)S(1)} %get-tuple-element.95), channel_id=1, source_target_pairs={{0,8},{4,12},{8,0},{12,4},{16,24},{20,28},{24,16},{28,20},{1,9},{5... | collective-permute-start | bytes 98312 | tf_op jit(solution)/shard_map/ppermute | solution.py:482
  19.3 4.7 %collective-permute-start.8 = (bf16[16,512]{1,0:T(8,128)(2,1)S(1)}, bf16[16,512]{1,0:T(8,128)(2,1)S(1)}, u32[]{:S(2)}, u32[]{:S(2)}) collective-permute-start(bf16[16,512]{1,0:T(8,128)(2,1)S(1)} %get-tuple-element.107), channel_id=1, source_target_pairs={{0,16},{4,20},{8,24},{12,28},{16,0},{20,4},{24,8},{28,12},{1,17},{... | collective-permute-start | bytes 49160 | tf_op jit(solution)/shard_map/ppermute | solution.py:482
  25.0 1.4 %collective-permute-start.10 = (bf16[32,1792]{1,0:T(8,128)(2,1)S(1)}, bf16[32,1792]{1,0:T(8,128)(2,1)S(1)}, u32[]{:S(2)}, u32[]{:S(2)}) collective-permute-start(bf16[32,1792]{1,0:T(8,128)(2,1)S(1)} %get-tuple-element.124), channel_id=1, source_target_pairs={{0,1},{1,0},{2,3},{3,2},{4,5},{5,4},{6,7},{7,6},{8,9},{9,8},{10,11... | collective-permute-start | bytes 344072 | tf_op jit(solution)/shard_map/ppermute | solution.py:482
  25.7 2.5 %collective-permute-start.9 = (bf16[32,1792]{1,0:T(8,128)(2,1)S(1)}, bf16[32,1792]{1,0:T(8,128)(2,1)S(1)}, u32[]{:S(2)}, u32[]{:S(2)}) collective-permute-start(bf16[32,1792]{1,0:T(8,128)(2,1)S(1)} %get-tuple-element.122), channel_id=1, source_target_pairs={{0,1},{1,0},{2,3},{3,2},{4,5},{5,4},{6,7},{7,6},{8,9},{9,8},{10,11... | collective-permute-start | bytes 344072 | tf_op jit(solution)/shard_map/ppermute | solution.py:482
  26.4 5.3 %collective-permute-start.11 = (bf16[32,1792]{1,0:T(8,128)(2,1)S(1)}, bf16[32,1792]{1,0:T(8,128)(2,1)S(1)}, u32[]{:S(2)}, u32[]{:S(2)}) collective-permute-start(bf16[32,1792]{1,0:T(8,128)(2,1)S(1)} %add.1), channel_id=1, source_target_pairs={{0,2},{1,3},{2,0},{3,1},{4,6},{5,7},{6,4},{7,5},{8,10},{9,11},{10,... | collective-permute-start | bytes 344072 | tf_op jit(solution)/shard_map/ppermute | solution.py:482

commit v2 on v1

v2 whole, which is shorter than its diff:
```python
import jax
import jax.numpy as jnp
from jax import lax
from jax.experimental import pallas as pl
from jax.experimental.pallas import tpu as pltpu
from jax.sharding import PartitionSpec as P

HDIM = 64
LANE = 128
SLOT = 32
SEQ, TP = "seq", "tp"

F32 = jnp.float32
BF16 = jnp.bfloat16
NN = (((1,), (0,)), ((), ()))
NT = (((1,), (1,)), ((), ()))
TN = (((0,), (0,)), ((), ()))


def dot(left, right, dims=NN):
    return lax.dot_general(left, right, dims, preferred_element_type=F32)


def round_up(value, step):
    return -(-value // step) * step


def silu_slope(values):
    logistic = jax.nn.sigmoid(values)
    return logistic * (1.0 + values * (1.0 - logistic))


def iota(shape, axis):
    return lax.broadcasted_iota(jnp.int32, shape, axis)


def one_minus_exp(values):
    series = 1.0 + values * (1.0 / 7.0)
    for term in (6.0, 5.0, 4.0, 3.0, 2.0):
        series = 1.0 + values * (1.0 / term) * series
    return jnp.where(values > -0.35, -values * series, 1.0 - jnp.exp(values))


def document_counts(doc_ref):
    tokens = doc_ref.shape[1]
    rows, columns = iota((tokens, tokens), 0), iota((tokens, tokens), 1)
    first = (iota((1, tokens), 1) == 0) & (lax.axis_index(SEQ) == 0)
    mark_row = jnp.where(first, 0.0, doc_ref[...].astype(F32))
    mark_row = jnp.broadcast_to(mark_row, (tokens, tokens))
    mark_column = jnp.sum(jnp.where(rows == columns, mark_row, 0.0), axis=1, keepdims=True)
    count_column = jnp.sum(jnp.where(columns <= rows, mark_row, 0.0), axis=1, keepdims=True)
    count_row = jnp.sum(
        jnp.where(rows <= columns, jnp.broadcast_to(mark_column, (tokens, tokens)), 0.0),
        axis=0,
        keepdims=True,
    )
    return mark_column, count_column, count_row


def head_picker(heads, channels, width):
    lanes = iota((heads, width), 1)
    head = iota((heads, width), 0)
    start = lax.axis_index(TP) * channels
    low = head * HDIM - start
    owned = (lanes >= low) & (lanes < low + HDIM) & (lanes < channels)
    spare = lanes - channels
    listed = (spare == head) | (spare == head + SLOT)
    return jnp.where(owned | listed, 1.0, 0.0).astype(BF16)


def decays(log_ref, doc_ref, picker):
    tokens = log_ref.shape[1]
    mark_column, count_column, count_row = document_counts(doc_ref)
    log_rows = dot(log_ref[...], picker, TN)
    rows, columns = iota((tokens, tokens), 0), iota((tokens, tokens), 1)
    lower = jnp.where(columns <= rows, 1.0, 0.0).astype(BF16)
    cumulative = dot(lower, log_rows.astype(BF16))
    scale = jnp.where(mark_column == 1.0, 1.0, jnp.sqrt(one_minus_exp(2.0 * log_rows)))
    last_count = count_column[tokens - 1 : tokens, :]
    total = cumulative[tokens - 1 : tokens, :]
    centre = cumulative[tokens // 2 : tokens // 2 + 1, :]
    rising = jnp.exp(cumulative - centre)
    falling = jnp.exp(centre - cumulative)
    fresh = jnp.where(count_column == 0.0, 1.0, 0.0)
    inside = jnp.where(count_column == last_count, 1.0, 0.0)
    carry_in = jnp.exp(cumulative) * fresh
    carry_out = jnp.exp(total - cumulative) * inside
    factor = jnp.exp(total) * fresh[tokens - 1 : tokens, :]
    return count_column, count_row, scale, rising, falling, carry_in, carry_out, factor


def two_parts(values):
    high = values.astype(BF16)
    return high, (values - high.astype(F32)).astype(BF16)


def fine_dot(left, right, dims=NN):
    (left_high, left_low), (right_high, right_low) = two_parts(left), two_parts(right)
    small = dot(left_high, right_low, dims) + dot(left_low, right_high, dims)
    return dot(left_high, right_high, dims) + small


class Values(dict):
    __getattr__ = dict.__getitem__


class Staged:
    def __init__(self, ins, outs, through, refs):
        refs = list(refs)
        far_in = [name for name, (_, far) in ins.items() if far is True and name not in through]
        far_out = [name for name, (_, _, far) in outs.items() if far]
        self.refs = {name: refs.pop(0) for name in ins}
        made = {name: refs.pop(0) for name in outs}
        held = {name: refs.pop(0) for name in far_in}
        self.made = Values(made, **{name: refs.pop(0) for name in far_out})
        sems = refs.pop(0) if far_in or far_out or through else None
        self.rest = refs
        self.loads = {
            name: pltpu.make_async_copy(self.refs[name], held[name], sems.at[at])
            for at, name in enumerate(far_in)
        }
        self.stores = {
            name: pltpu.make_async_copy(self.made[name], made[name], sems.at[len(far_in) + at])
            for at, name in enumerate(far_out)
        }
        self.passed = [
            pltpu.make_async_copy(self.refs[name], made[name], sems.at[len(far_in + far_out) + at])
            for at, name in enumerate(through)
        ]
        self.refs.update(held)
        for copy in (*self.loads.values(), *self.passed):
            copy.start()

    def take(self, name):
        if name in self.loads:
            self.loads.pop(name).wait()
        return self.refs[name]

    def __getattr__(self, name):
        return self.take(name)

    def put(self, **values):
        for name, value in values.items():
            self.made[name][...] = value
            self.send(name)

    def send(self, name):
        if name in self.stores:
            self.stores[name].start()

    def finish(self):
        for copy in (*self.stores.values(), *self.passed):
            copy.wait()


def pin(value):
    return pltpu.with_memory_space_constraint(value, pltpu.HBM)


def near(*values):
    return (*values, False)


def far(*values):
    return (*values, True)


def staged_call(body, ins, outs, flops=0, scratch=(), through=()):
    outs = dict(outs, **{name: near(ins[name][0].shape, ins[name][0].dtype) for name in through})

    def kernel(*refs):
        staged = Staged(ins, outs, through, refs)
        body(staged, *staged.rest)
        staged.finish()

    def spec(is_far):
        return pl.BlockSpec(memory_space=pltpu.HBM if is_far else pltpu.VMEM)

    held = [
        pltpu.VMEM(value.shape, value.dtype)
        for name, (value, is_far) in ins.items()
        if is_far is True and name not in through
    ]
    held += [pltpu.VMEM(shape, dtype) for shape, dtype, is_far in outs.values() if is_far]
    copies = len(held) + len(through)
    sems = [pltpu.SemaphoreType.DMA((copies,))] if copies else []
    results = pl.pallas_call(
        kernel,
        name=body.__name__,
        out_shape=[jax.ShapeDtypeStruct(shape, dtype) for shape, dtype, _ in outs.values()],
        in_specs=[spec(is_far) for _, is_far in ins.values()],
        out_specs=[spec(is_far) for _, _, is_far in outs.values()],
        scratch_shapes=held + sems + list(scratch),
        compiler_params=pltpu.CompilerParams(vmem_limit_bytes=24 * 2**20),
        cost_estimate=pl.CostEstimate(flops=flops, bytes_accessed=2**20, transcendentals=0),
    )(*[pin(value) if is_far else value for value, is_far in ins.values()])
    return Values(zip(outs, results))


def assemble(staged, name, whole):
    for step in range(whole.shape[0] // staged.refs[name + "0"].shape[0]):
        block = staged.take(name + "%d" % step)
        piece = block.shape[0]
        start = pl.multiple_of((lax.axis_index(TP) ^ step) * piece, piece)
        whole[pl.ds(start, piece), :] = block[...]


def head_expander(channels, width):
    first = channels // LANE * LANE
    shape = (width - first, width)
    slot = iota(shape, 0) + (first - channels)
    lane = iota(shape, 1)
    spare = lane - channels
    head = jnp.where(slot < SLOT, slot, slot - SLOT)
    low = head * HDIM - lax.axis_index(TP) * channels
    owned = (lane >= low) & (lane < low + HDIM) & (lane < channels)
    listed = (spare == head) | (spare == head + SLOT)
    kept = (slot >= 0) & (slot < 2 * SLOT)
    return jnp.where(kept & (owned | listed), 1.0, 0.0).astype(BF16)


def encode(value, factor, channels):
    lane = iota(value.shape, 1)
    high = factor.astype(BF16).astype(F32)
    listed = jnp.where(lane < channels + SLOT, high, factor - high)
    return jnp.where(lane < channels, value, listed).astype(BF16)


def decode(message, expander):
    return dot(message[:, message.shape[1] - expander.shape[0] :], expander)


def partner_is_later(bit):
    return lax.axis_index(SEQ) % (2 * bit) < bit


def put_message(staged, state_part, grad_part, factor, channels, bit):
    message = staged.made.message
    states = state_part.shape[0]
    if message.shape[0] == states:
        part = jnp.where(partner_is_later(bit), state_part, grad_part)
        message[...] = encode(part, factor, channels)
    else:
        message[:states, :] = encode(state_part, factor, channels)
        message[states:, :] = encode(grad_part, factor, channels)


def prepare(staged):
    tokens, channels = staged.made.enter.shape
    width = staged.made.factor.shape[1]
    log_ref = staged.log
    picker = head_picker(log_ref.shape[0], channels, width)
    count_column, count_row, scale, rising, falling, carry_in, carry_out, factor = decays(
        log_ref, staged.doc, picker
    )
    staged.put(enter=carry_in[:, :channels])
    staged.put(leave=(scale * carry_out)[:, :channels])
    staged.put(rise=rising[:, :channels])
    staged.put(fall=(scale * falling)[:, :channels])
    staged.put(factor=jnp.broadcast_to(factor, staged.made.factor.shape))
    staged.put(expander=head_expander(channels, width))
    rows, columns = iota((tokens, tokens), 0), iota((tokens, tokens), 1)
    same = count_column == count_row
    causal = (rows >= columns) & same
    anticausal = (rows <= columns) & same
    b_rows, c_rows = staged.b_in[...], staged.c_in[...]
    staged.put(causal=jnp.where(causal, 1.0, 0.0))
    staged.put(crossed=jnp.where(causal, dot(c_rows, b_rows, TN), 0.0))
    staged.put(crossed_back=jnp.where(anticausal, dot(b_rows, c_rows, TN), 0.0))
    staged.put(b=b_rows)
    staged.put(c=c_rows)


def put_summary(staged, name, vectors, values):
    part = staged.made[name]
    part[...] = jnp.zeros_like(part)
    part[:, : values.shape[1]] = dot(staged.take(vectors)[...], values)


def project(staged, rows_ref):
    assemble(staged, "rows", rows_ref)
    rows = rows_ref[...]
    pre = dot(rows, staged.w_in[...], NT)
    staged.put(pre=pre)
    x_rows = (pre * jax.nn.sigmoid(pre)).astype(BF16)
    staged.put(x=x_rows)
    leaving = (x_rows.astype(F32) * staged.leave[...]).astype(BF16)
    staged.put(leaving=leaving)
    put_summary(staged, "state", "b", leaving)
    gate = dot(rows, staged.w_gate[...], NT)
    staged.put(gate=gate)
    staged.put(gated=gate * jax.nn.sigmoid(gate))


def front(staged, grad_ref):
    channels = staged.made.mix.shape[1]
    assemble(staged, "grad", grad_ref)
    mix = dot(grad_ref[...], staged.w_out[...], NT)
    staged.put(mix=mix)
    y_grads = (mix * staged.gated[...]).astype(BF16)
    staged.put(y=y_grads)
    entering = (y_grads.astype(F32) * staged.enter[...]).astype(BF16)
    staged.put(entering=entering)
    put_summary(staged, "grad", "c", entering)
    state_part, grad_part = staged.state[...], staged.made.grad[...]
    put_message(staged, state_part, grad_part, staged.factor[...], channels, 1)


def join(channels, bit):
    def join_body(staged):
        received, expander = staged.received, staged.expander[...]
        factor, state, grad = (staged.take(name)[...] for name in ("factor", "state", "grad"))
        states = state.shape[0]
        other_state = received[:states, :].astype(F32)
        other_grad = received[states:, :].astype(F32)
        other = decode(received[:states, :], expander)
        later = partner_is_later(bit)
        if bit == 1:
            before = jnp.where(later, 1.0, other), jnp.where(later, 0.0, other_state)
            behind = jnp.where(later, other, 1.0), jnp.where(later, other_grad, 0.0)
        else:
            keep, held, back_keep, back_held = (
                staged.take(name)[...] for name in ("keep", "held", "back_keep", "back_held")
            )
            before = (
                jnp.where(later, keep, keep * other),
                jnp.where(later, held, keep * other_state + held),
            )
            behind = (
                jnp.where(later, back_keep * other, back_keep),
                jnp.where(later, back_keep * other_grad + back_held, back_held),
            )
        staged.put(keep=before[0])
        staged.put(held=before[1])
        staged.put(back_keep=behind[0])
        staged.put(back_held=behind[1])
        joined_state = jnp.where(later, other * state + other_state, factor * other_state + state)
        joined_grad = jnp.where(later, grad + factor * other_grad, other_grad + other * grad)
        joined = factor * other
        put_message(staged, joined_state, joined_grad, joined, channels, 2 * bit)
        if "state" in staged.made:
            staged.put(state=joined_state)
            staged.put(grad=joined_grad)
            staged.put(factor=joined)

    return join_body


def slopes(staged):
    staged.put(pre_slope=silu_slope(staged.pre[...]))
    staged.put(gate_slope=staged.mix[...] * silu_slope(staged.gate[...]))


def local_vectors(staged):
    upper = staged.y[...].astype(F32) * staged.rise[...]
    lower = staged.x[...].astype(F32) * staged.fall[...]
    causal = staged.causal[...] > 0.0
    high, low = two_parts(jnp.where(causal, fine_dot(upper, lower, NT), 0.0))
    b_rows, c_rows = staged.b[...], staged.c[...]
    states = b_rows.shape[0]
    bc = staged.made.bc
    bc[:states, :] = dot(c_rows, high) + dot(c_rows, low)
    bc[states:, :] = dot(b_rows, high, NT) + dot(b_rows, low, NT)


def local_channels(staged):
    x_rows, y_grads = staged.x[...].astype(F32), staged.y[...].astype(F32)
    rise, fall, skip = staged.rise[...], staged.fall[...], staged.skip[...]
    ssm = rise * fine_dot(staged.crossed[...], x_rows * fall)
    staged.put(ssm=ssm + skip * x_rows)
    x_grad = fall * fine_dot(staged.crossed_back[...], y_grads * rise)
    staged.put(x_grad=x_grad + skip * y_grads)


def back(bit):
    def back_body(staged, gate_ref, pre_ref):
        entry = staged.entry[...]
        states, channels = entry.shape
        received = staged.received
        other_part = received[:, :channels].astype(F32)
        other = decode(received[...], staged.expander[...])[:, :channels]
        later = partner_is_later(bit)
        keep, held, back_keep, back_held = (
            staged.take(name)[:, :channels] for name in ("keep", "held", "back_keep", "back_held")
        )
        state = jnp.where(later, entry, other * entry + other_part)
        state_in = (keep * state + held).astype(BF16)
        grad_in = jnp.where(later, back_keep * other_part + back_held, back_held).astype(BF16)
        carried = dot(staged.c[...], state_in, TN)
        ssm_out = staged.ssm[...] + staged.enter[...] * carried
        gate_ref[...] = (
            ssm_out.astype(BF16).astype(F32) * staged.gate_slope[...]
        ).astype(BF16)
        carried = dot(staged.b[...], grad_in, TN)
        x_grad = staged.x_grad[...] + staged.leave[...] * carried
        pre_ref[...] = (
            x_grad.astype(BF16).astype(F32) * staged.pre_slope[...]
        ).astype(BF16)
        local = staged.bc
        b_part = local[:states, :] + dot(grad_in, staged.leaving[...], NT)
        c_part = local[states:, :] + dot(state_in, staged.entering[...], NT)
        tokens = gate_ref.shape[0]
        kept, sent = staged.made.kept, staged.made.sent
        piece = tokens // (kept.shape[0] + sent.shape[0])
        count = kept.shape[0]
        tp = lax.axis_index(TP)
        steps = [2 * at for at in range(count)] + [2 * at + 1 for at in range(count)]
        starts = [pl.multiple_of((tp ^ step) * piece, piece) for step in steps]
        gate_rows, pre_rows = (
            jnp.concatenate([ref[pl.ds(start, piece), :] for start in starts], axis=0)
            for ref in (gate_ref, pre_ref)
        )
        partial = dot(gate_rows, staged.w_gate[...]) + dot(pre_rows, staged.w_in[...])
        depth = partial.shape[1]
        split = kept.shape[2] - tokens
        for at in range(2 * count):
            made, slot = (kept, at) if at < count else (sent, at - count)
            if split > depth:
                made[slot, :, split - LANE : split] = jnp.zeros((piece, LANE), made.dtype)
            made[slot, :, :depth] = partial[at * piece : (at + 1) * piece, :].astype(made.dtype)
            made[slot, :states, split:] = b_part.astype(made.dtype)
            made[slot, states : 2 * states, split:] = c_part.astype(made.dtype)

    return back_body


def add(staged):
    staged.put(far_sum=(staged.kept[1] + staged.arrived[1].astype(F32)).astype(BF16))


def total(staged):
    depth = staged.made.grad.shape[1]
    states, tokens = staged.made.b.shape
    split = staged.kept.shape[2] - tokens

    def summed(rows, lanes):
        own = staged.kept[0, rows, lanes] + staged.arrived[0, rows, lanes].astype(F32)
        return own + staged.far_sum[rows, lanes].astype(F32)

    staged.put(grad=summed(slice(None), slice(depth)).astype(BF16))
    staged.put(b=summed(slice(states), slice(split, None)))
    staged.put(c=summed(slice(states, 2 * states), slice(split, None)))


def swap_masks(parts):
    masks, bit = [], parts // 2
    while bit:
        masks.append(bit)
        bit //= 2
    return masks


def shards(
    layer_input, out_grad, w_in, w_gate, w_out, b_proj, c_proj, log_decay, d_skip, entry_state,
    doc_start,
):
    owners, parts = lax.axis_size(SEQ), lax.axis_size(TP)
    assert owners > 2 and owners & (owners - 1) == 0 and parts == 4
    piece, depth = layer_input.shape
    tokens = piece * parts
    channels = w_in.shape[0]
    states = b_proj.shape[0]
    width = round_up(channels + 2 * SLOT, LANE)
    wide = near((tokens, channels), F32)
    half = near((tokens, channels), BF16)
    square = near((tokens, tokens), F32)
    row = near((states, tokens), BF16)
    summary = near((states, width), F32)

    def ordered(value, after):
        return lax.optimization_barrier((value, after))[0]

    def swap(value, axis, bit):
        size = lax.axis_size(axis)
        return lax.ppermute(value, axis, [(at, at ^ bit) for at in range(size)])

    def call(body, ins, outs, **options):
        ins = {key: near(value) if hasattr(value, "shape") else value for key, value in ins.items()}
        return staged_call(body, ins, outs, **options)

    far_ins = dict(
        log=log_decay, doc=doc_start.reshape(1, tokens), b_in=b_proj, c_in=c_proj, w_gate=w_gate,
        w_in=w_in, w_out=w_out, rows0=layer_input, grad0=out_grad, entry=entry_state,
        skip=d_skip.reshape(1, channels),
    )
    ready = call(
        prepare, {name: far(value) for name, value in far_ins.items()},
        dict(enter=wide, leave=wide, rise=wide, fall=wide, factor=summary,
             expander=near((width - channels // LANE * LANE, width), BF16), causal=square,
             crossed=square, crossed_back=square, b=row, c=row),
        flops=8 * tokens * channels * tokens,
        through=("w_gate", "w_in", "w_out", "rows0", "grad0", "entry", "skip"),
    )
    grad_blocks, row_blocks = {0: out_grad}, {0: layer_input}
    masks = swap_masks(parts)
    for mask in masks:
        for blocks in (row_blocks, grad_blocks):
            for step in list(blocks):
                block = blocks[step]
                if mask != masks[0]:
                    block = ordered(block, ready.expander)
                blocks[step ^ mask] = swap(block, TP, mask)
    rows = {"rows%d" % step: block for step, block in row_blocks.items()}
    grads = {"grad%d" % step: block for step, block in grad_blocks.items()}
    rows["rows0"], grads["grad0"] = ready.rows0, ready.grad0
    assembled = pltpu.VMEM((tokens, depth), BF16)
    both = near((2 * states, width), BF16)
    one = near((states, width), BF16)
    first = call(
        project,
        dict(rows, **dict(w_gate=ready.w_gate, w_in=ready.w_in, b=ready.b, leave=ready.leave)),
        dict(gate=wide, gated=wide, pre=wide, x=half, leaving=half, state=summary),
        flops=4 * tokens * channels * depth, scratch=(assembled,),
    )
    first.update(call(
        front,
        dict(grads, **dict(w_out=ready.w_out, c=ready.c, enter=ready.enter, factor=ready.factor),
             **dict(gated=first.gated, state=first.state)),
        dict(mix=wide, y=half, entering=half, grad=summary, message=both),
        flops=2 * tokens * channels * depth, scratch=(assembled,),
    ))
    group = dict(dict(state=first.state, grad=first.grad), factor=ready.factor)
    received = swap(first.message, SEQ, 1)
    slope = call(
        slopes, dict(pre=first.pre, gate=first.gate, mix=first.mix),
        dict(pre_slope=wide, gate_slope=wide), flops=tokens * channels * 32,
    )
    received = ordered(received, slope.pre_slope)
    x_rows, y_grads = first.x, first.y
    results, bit = {}, 1
    while 2 * bit < owners:
        last = 4 * bit >= owners
        outs = dict(keep=summary, held=summary, back_keep=summary, back_held=summary,
                    message=one if last else both)
        if not last:
            outs.update(state=summary, grad=summary, factor=summary)
        group = call(
            join(channels, bit), dict(group, received=received, expander=ready.expander),
            outs,
        )
        received = swap(group.pop("message"), SEQ, 2 * bit)
        if bit == 1:
            results.update(call(
                local_vectors,
                dict(rise=ready.rise, fall=ready.fall, causal=ready.causal, b=ready.b, c=ready.c,
                     x=ordered(x_rows, group.keep), y=y_grads),
                dict(bc=near((2 * states, tokens), F32)), flops=8 * tokens * channels * tokens,
            ))
            if not last:
                received = ordered(received, results["bc"])
        if last:
            results.update(call(
                local_channels,
                dict(rise=ready.rise, fall=ready.fall, crossed=ready.crossed,
                     crossed_back=ready.crossed_back, skip=ready.skip,
                     x=ordered(x_rows, group.keep), y=y_grads),
                dict(ssm=wide, x_grad=wide), flops=16 * tokens * channels * tokens,
            ))
        bit *= 2
    span = round_up(depth, LANE) + tokens
    graded = pltpu.VMEM((tokens, channels), BF16)
    held = call(
        back(bit),
        dict(group, received=received, **results, **slope, entering=first.entering,
             leaving=first.leaving, entry=ready.entry, expander=ready.expander, enter=ready.enter,
             leave=ready.leave, b=ready.b, c=ready.c, w_gate=ready.w_gate, w_in=ready.w_in),
        dict(kept=near((parts // 2, piece, span), F32), sent=near((parts // 2, piece, span), BF16)),
        flops=4 * tokens * channels * depth, scratch=(graded, graded),
    )
    halves = dict(kept=held.kept, arrived=swap(held.sent, TP, 1))
    far_sum = call(add, halves, dict(far_sum=near((piece, span), BF16))).far_sum
    result = call(
        total, dict(halves, far_sum=swap(far_sum, TP, 2)),
        dict(grad=near((piece, depth), BF16), b=near((states, tokens), F32),
             c=near((states, tokens), F32)),
    )
    return result.grad, result.b, result.c


def solution(mesh):
    in_specs = (
        P((SEQ, TP), None),
        P((SEQ, TP), None),
        P(TP, None),
        P(TP, None),
        P(TP, None),
        P(None, SEQ),
        P(None, SEQ),
        P(None, SEQ),
        P(TP),
        P(None, TP),
        P(SEQ),
    )
    out_specs = (P((SEQ, TP), None), P(None, SEQ), P(None, SEQ))
    return jax.shard_map(shards, mesh=mesh, in_specs=in_specs, out_specs=out_specs, check_vma=False)
```

time: 32.5 us -> 32.7 us (level)
  waiting for transfers between devices: 11.2 us -> 12.5 us
  starting transfers between devices: 12.7 us -> 12.1 us
  Pallas kernels: 7.72 us -> 7.18 us
    ppermute x12 -> x11, waiting for transfers between devices: 11.2 us -> 12.5 us  [swap(): return lax.ppermute(value, axis, [(at, at ^ bit) for at in range(size)])]
    ppermute x12 -> x11, starting transfers between devices: 12.7 us -> 12.1 us  [swap(): return lax.ppermute(value, axis, [(at, at ^ bit) for at in range(size)])]
    pallas_call x12 -> x11, Pallas kernels: 7.72 us -> 7.18 us  [staged_call(): pl.pallas_call(kernel, name=body.__name__, out_shape=[jax.ShapeDtypeStruc...]
  transfers between devices with their start and end apart: 12 -> 11, of which waited for: 8 -> 8; matrix products, arithmetic and copies ran while one was open for 0% -> 0% of each run, Pallas kernels for 16% -> 14%
where the time goes in v2:
time: 32.7 us; the launch traced here: 32.6 us
  waiting for transfers between devices  12.5 us (38%)
  starting transfers between devices  12.1 us (37%)
  Pallas kernels  7.18 us (22%)
  between operations  0.72 us (2%)
    ppermute x11, waiting for transfers between devices, swap(): return lax.ppermute(value, axis, [(at, at ^ bit) for at in range(size)])  12.5 us
    ppermute x11, starting transfers between devices, swap(): return lax.ppermute(value, axis, [(at, at ^ bit) for at in range(size)])  12.1 us
    pallas_call x11, Pallas kernels, staged_call(): pl.pallas_call(kernel, name=body.__name__, out_shape=[jax.ShapeDtypeStruc...  7.18 us
  transfers between devices with their start and end apart: 11, of which 8 were waited for; matrix products, arithmetic and copies ran while one was open for 0% of the time, Pallas kernels for 14%

profile of v2, /device:TPU:0, one launch (start us, length us, event | category | flops | bytes accessed | tf_op | source)
XLA Modules:
  0.0 32.6 jit_solution(13660638707610331770)
XLA Ops:
  0.6 3.0 %collective-permute-start = (bf16[32,1600]{1,0:T(8,128)(2,1)}, bf16[32,1600]{1,0:T(8,128)(2,1)S(1)}, u32[]{:S(2)}, u32[]{:S(2)}) collective-permute-start(bf16[32,1600]{1,0:T(8,128)(2,1)} %refs_7_.1), channel_id=1, source_target_pairs={{0,2},{1,3},{2,0},{3,1},{4,6},{5,7},{6,4},{7,5},{8,10},{9,11},{10,... | collective-permute-start | bytes 307208 | tf_op jit(solution)/shard_map/ppermute | solution.py:475
  3.7 2.3 %prepare.1 = (f32[128,400]{1,0:T(8,128)S(1)}, f32[128,400]{1,0:T(8,128)S(1)}, f32[128,400]{1,0:T(8,128)S(1)}, f32[128,400]{1,0:T(8,128)S(1)}, f32[16,512]{1,0:T(...) custom-call(bf16[25,128]{1,0:T(8,128)(2,1)} %refs_0_.1, ...), custom_call_target="tpu_custom_call" | custom-call | flops 52428800 | bytes 1048576 | tf_op jit(solution)/shard_map/prepare/pallas_call | solution.py:187
  6.1 1.5 %collective-permute-done.refs_1_ = bf16[32,1600]{1,0:T(8,128)(2,1)S(1)} collective-permute-done((bf16[32,1600]{1,0:T(8,128)(2,1)}, bf16[32,1600]{1,0:T(8,128)(2,1)S(1)}, u32[]{:S(2)}, u32[]{:S(2)}) %collective-permute-start) | collective-permute-done | bytes 102432 | tf_op jit(solution)/shard_map/ppermute | solution.py:475
  7.6 0.5 %collective-permute-start.4 = (bf16[32,1600]{1,0:T(8,128)(2,1)S(1)}, bf16[32,1600]{1,0:T(8,128)(2,1)S(1)}, u32[]{:S(2)}, u32[]{:S(2)}) collective-permute-start(bf16[32,1600]{1,0:T(8,128)(2,1)S(1)} %copy-done.1), channel_id=1, source_target_pairs={{0,1},{1,0},{2,3},{3,2},{4,5},{5,4},{6,7},{7,6},{8,9},{9,8},{10,11... | collective-permute-start | bytes 307208 | tf_op jit(solution)/shard_map/ppermute | solution.py:475
  8.1 1.0 %collective-permute-done.3.refs_1_ = bf16[32,1600]{1,0:T(8,128)(2,1)S(1)} collective-permute-done((bf16[32,1600]{1,0:T(8,128)(2,1)}, bf16[32,1600]{1,0:T(8,128)(2,1)S(1)}, u32[]{:S(2)}, u32[]{:S(2)}) %collective-permute-start.3) | collective-permute-done | bytes 102432 | tf_op jit(solution)/shard_map/ppermute | solution.py:475
  9.1 1.1 %project.1 = (f32[128,400]{1,0:T(8,128)S(1)}, f32[128,400]{1,0:T(8,128)S(1)}, f32[128,400]{1,0:T(8,128)S(1)}, bf16[128,400]{1,0:T(8,128)(2,1)S(1)}, bf16[128,400]{1,0:T(8,128)(2,1)S(1)}, /*index=5*/f32[16,512]{1,0:T(8,128)S(1)}) custom-call(bf16[32,1600]{1,0:T(8,128)(2,1)S(1)} %get-tuple-element.59.refs_0_, ...), custom_call_target="tpu_custom_call" | custom-call | flops 327680000 | bytes 1048576 | tf_op jit(solution)/shard_map/project/pallas_call | solution.py:187
  10.2 0.2 collective-permute-done.5.refs_3_
  10.4 0.7 %front.1 = (f32[128,400]{1,0:T(8,128)S(1)}, bf16[128,400]{1,0:T(8,128)(2,1)S(1)}, bf16[128,400]{1,0:T(8,128)(2,1)S(1)}, f32[16,512]{1,0:T(8,128)S(1)}, bf16[32,512]{1,0:T(8,128)(2,1)S(1)}) custom-call(bf16[32,1600]{1,0:T(8,128)(2,1)S(1)} %get-tuple-element.68.refs_0_, bf16[32,1600]{1,0:T(8,128)(2,1)S(1)} %collective-permute-done.3.refs_1_, ...), custom_call_target="tpu_custom_call" | custom-call | flops 163840000 | bytes 1048576 | tf_op jit(solution)/shard_map/front/pallas_call | solution.py:187
  11.1 1.8 %collective-permute-start.6 = (bf16[32,512]{1,0:T(8,128)(2,1)S(1)}, bf16[32,512]{1,0:T(8,128)(2,1)S(1)}, u32[]{:S(2)}, u32[]{:S(2)}) collective-permute-start(bf16[32,512]{1,0:T(8,128)(2,1)S(1)} %get-tuple-element.77), channel_id=1, source_target_pairs={{0,4},{4,0},{8,12},{12,8},{16,20},{20,16},{24,28},{28,24},{1,5},{5... | collective-permute-start | bytes 98312 | tf_op jit(solution)/shard_map/ppermute | solution.py:475
  12.9 0.2 slopes.1
  13.1 2.0 %collective-permute-done.6.refs_3_ = bf16[32,512]{1,0:T(8,128)(2,1)S(1)} collective-permute-done((bf16[32,512]{1,0:T(8,128)(2,1)S(1)}, bf16[32,512]{1,0:T(8,128)(2,1)S(1)}, u32[]{:S(2)}, u32[]{:S(2)}) %collective-permute-start.6) | collective-permute-done | bytes 32800 | tf_op jit(solution)/shard_map/ppermute | solution.py:475
  15.0 0.1 join_body.2
  15.2 1.9 %collective-permute-start.7 = (bf16[32,512]{1,0:T(8,128)(2,1)S(1)}, bf16[32,512]{1,0:T(8,128)(2,1)S(1)}, u32[]{:S(2)}, u32[]{:S(2)}) collective-permute-start(bf16[32,512]{1,0:T(8,128)(2,1)S(1)} %get-tuple-element.90), channel_id=1, source_target_pairs={{0,8},{4,12},{8,0},{12,4},{16,24},{20,28},{24,16},{28,20},{1,9},{5... | collective-permute-start | bytes 98312 | tf_op jit(solution)/shard_map/ppermute | solution.py:475
  17.1 0.5 %local_vectors.1.refs_5_ = f32[32,128]{1,0:T(8,128)S(1)} custom-call(f32[128,400]{1,0:T(8,128)S(1)} %get-tuple-element.91.refs_0_, f32[128,400]{1,0:T(8,128)S(1)} %get-tuple-element.92.refs_1_, f32[128,128]{1,0:T(8,128)S(1)} %get-tuple-element.93.refs_2_, bf16[16,128]{1,0:T(8,128)(2,1)S(1)} %get-tuple-element.65.refs_6_.refs_3_.refs_16_, ...), custom_call_target="tpu_custom_call" | custom-call | flops 52428800 | bytes 1048576 | tf_op jit(solution)/shard_map/local_vectors/pallas_call | solution.py:187
  17.6 1.6 %collective-permute-done.7.refs_7_ = bf16[32,512]{1,0:T(8,128)(2,1)S(1)} collective-permute-done((bf16[32,512]{1,0:T(8,128)(2,1)S(1)}, bf16[32,512]{1,0:T(8,128)(2,1)S(1)}, u32[]{:S(2)}, u32[]{:S(2)}) %collective-permute-start.7) | collective-permute-done | bytes 32800 | tf_op jit(solution)/shard_map/ppermute | solution.py:475
  19.2 0.1 join_body.3
  19.3 2.9 %collective-permute-start.8 = (bf16[16,512]{1,0:T(8,128)(2,1)S(1)}, bf16[16,512]{1,0:T(8,128)(2,1)S(1)}, u32[]{:S(2)}, u32[]{:S(2)}) collective-permute-start(bf16[16,512]{1,0:T(8,128)(2,1)S(1)} %get-tuple-element.102), channel_id=1, source_target_pairs={{0,16},{4,20},{8,24},{12,28},{16,0},{20,4},{24,8},{28,12},{1,17},{... | collective-permute-start | bytes 49160 | tf_op jit(solution)/shard_map/ppermute | solution.py:475
  22.2 0.4 %local_channels.1 = (f32[128,400]{1,0:T(8,128)S(1)}, f32[128,400]{1,0:T(8,128)S(1)}) custom-call(f32[128,400]{1,0:T(8,128)S(1)} %get-tuple-element.91.refs_0_, f32[128,400]{1,0:T(8,128)S(1)} %get-tuple-element.92.refs_1_, f32[128,128]{1,0:T(8,128)S(1)} %get-tuple-element.103.refs_2_, f32[128,128]{1,0:T(8,128)S(1)} %get-tuple-element.104.refs_3_, ...), custom_call_target="tpu_custom_call" | custom-call | flops 104857600 | bytes 1048576 | tf_op jit(solution)/shard_map/local_channels/pallas_call | solution.py:187
  22.6 1.4 %collective-permute-done.8.refs_4_ = bf16[16,512]{1,0:T(8,128)(2,1)S(1)} collective-permute-done((bf16[16,512]{1,0:T(8,128)(2,1)S(1)}, bf16[16,512]{1,0:T(8,128)(2,1)S(1)}, u32[]{:S(2)}, u32[]{:S(2)}) %collective-permute-start.8) | collective-permute-done | bytes 16416 | tf_op jit(solution)/shard_map/ppermute | solution.py:475
  24.0 1.0 %back_body.1 = (f32[2,32,1792]{2,1,0:T(8,128)S(1)}, bf16[2,32,1792]{2,1,0:T(8,128)(2,1)S(1)}) custom-call(f32[16,512]{1,0:T(8,128)S(1)} %get-tuple-element.98.refs_0_, f32[16,512]{1,0:T(8,128)S(1)} %get-tuple-element.99.refs_1_, f32[16,512]{1,0:T(8,128)S(1)} %get-tuple-element.100.refs_2_, f32[16,512]{1,0:T(8,128)S(1)} %get-tuple-element.101.refs_3_, ...), custom_call_target="tpu_custom_call" | custom-call | flops 327680000 | bytes 1048576 | tf_op jit(solution)/shard_map/back_body/pallas_call | solution.py:187
  25.2 1.5 %collective-permute-done.9.refs_1_ = bf16[2,32,1792]{2,1,0:T(8,128)(2,1)S(1)} collective-permute-done((bf16[2,32,1792]{2,1,0:T(8,128)(2,1)S(1)}, bf16[2,32,1792]{2,1,0:T(8,128)(2,1)S(1)}, u32[]{:S(2)}, u32[]{:S(2)}) %collective-permute-start.9) | collective-permute-done | bytes 229408 | tf_op jit(solution)/shard_map/ppermute | solution.py:475
  26.7 1.8 %collective-permute-start.10 = (bf16[32,1792]{1,0:T(8,128)(2,1)S(1)}, bf16[32,1792]{1,0:T(8,128)(2,1)S(1)}, u32[]{:S(2)}, u32[]{:S(2)}) collective-permute-start(bf16[32,1792]{1,0:T(8,128)(2,1)S(1)} %add.1), channel_id=1, source_target_pairs={{0,2},{1,3},{2,0},{3,1},{4,6},{5,7},{6,4},{7,5},{8,10},{9,11},{10,... | collective-permute-start | bytes 344072 | tf_op jit(solution)/shard_map/ppermute | solution.py:475
  28.5 3.4 %collective-permute-done.10.refs_2_ = bf16[32,1792]{1,0:T(8,128)(2,1)S(1)} collective-permute-done((bf16[32,1792]{1,0:T(8,128)(2,1)S(1)}, bf16[32,1792]{1,0:T(8,128)(2,1)S(1)}, u32[]{:S(2)}, u32[]{:S(2)}) %collective-permute-start.10) | collective-permute-done | bytes 114720 | tf_op jit(solution)/shard_map/ppermute | solution.py:475
  31.9 0.7 %total.1 = (bf16[32,1600]{1,0:T(8,128)(2,1)}, f32[16,128]{1,0:T(8,128)}, f32[16,128]{1,0:T(8,128)}) custom-call(f32[2,32,1792]{2,1,0:T(8,128)S(1)} %get-tuple-element.113.refs_0_, bf16[2,32,1792]{2,1,0:T(8,128)(2,1)S(1)} %collective-permute-done.9.refs_1_, bf16[32,1792]{1,0:T(8,128)(2,1)S(1)} %collective-permute-done.10.refs_2_), custom_call_target="tpu_custom_call" | custom-call | bytes 1048576 | tf_op jit(solution)/shard_map/total/pallas_call | solution.py:187
  (13 shorter events, 0.3 us)
Async XLA Ops:
  0.6 7.0 %collective-permute-start = (bf16[32,1600]{1,0:T(8,128)(2,1)}, bf16[32,1600]{1,0:T(8,128)(2,1)S(1)}, u32[]{:S(2)}, u32[]{:S(2)}) collective-permute-start(bf16[32,1600]{1,0:T(8,128)(2,1)} %refs_7_.1), channel_id=1, source_target_pairs={{0,2},{1,3},{2,0},{3,1},{4,6},{5,7},{6,4},{7,5},{8,10},{9,11},{10,... | collective-permute-start | bytes 307208 | tf_op jit(solution)/shard_map/ppermute | solution.py:475
  3.6 5.5 %collective-permute-start.3 = (bf16[32,1600]{1,0:T(8,128)(2,1)}, bf16[32,1600]{1,0:T(8,128)(2,1)S(1)}, u32[]{:S(2)}, u32[]{:S(2)}) collective-permute-start(bf16[32,1600]{1,0:T(8,128)(2,1)} %refs_8_.1), channel_id=1, source_target_pairs={{0,2},{1,3},{2,0},{3,1},{4,6},{5,7},{6,4},{7,5},{8,10},{9,11},{10,... | collective-permute-start | bytes 307208 | tf_op jit(solution)/shard_map/ppermute | solution.py:475
  3.7 2.3 %copy-start = (bf16[32,1600]{1,0:T(8,128)(2,1)S(1)}, bf16[32,1600]{1,0:T(8,128)(2,1)}, u32[]{:S(2)}) copy-start(bf16[32,1600]{1,0:T(8,128)(2,1)} %refs_7_.1) | copy-start | bytes 307204
  3.7 3.9 %copy-start.1 = (bf16[32,1600]{1,0:T(8,128)(2,1)S(1)}, bf16[32,1600]{1,0:T(8,128)(2,1)}, u32[]{:S(2)}) copy-start(bf16[32,1600]{1,0:T(8,128)(2,1)} %refs_8_.1) | copy-start | bytes 307204
  6.1 3.0 %collective-permute-start.1 = (bf16[32,1600]{1,0:T(8,128)(2,1)S(1)}, bf16[32,1600]{1,0:T(8,128)(2,1)S(1)}, u32[]{:S(2)}, u32[]{:S(2)}) collective-permute-start(bf16[32,1600]{1,0:T(8,128)(2,1)S(1)} %copy-done), channel_id=1, source_target_pairs={{0,1},{1,0},{2,3},{3,2},{4,5},{5,4},{6,7},{7,6},{8,9},{9,8},{10,11... | collective-permute-start | bytes 307208 | tf_op jit(solution)/shard_map/ppermute | solution.py:475
  7.6 1.5 %collective-permute-start.2 = (bf16[32,1600]{1,0:T(8,128)(2,1)S(1)}, bf16[32,1600]{1,0:T(8,128)(2,1)S(1)}, u32[]{:S(2)}, u32[]{:S(2)}) collective-permute-start(bf16[32,1600]{1,0:T(8,128)(2,1)S(1)} %collective-permute-done.refs_1_), channel_id=1, source_target_pairs={{0,1},{1,0},{2,3},{3,2},{4,5},{5,4},{6,7},{7,6},{8,9},{9,8},{10,11... | collective-permute-start | bytes 307208 | tf_op jit(solution)/shard_map/ppermute | solution.py:475
  7.6 2.6 %collective-permute-start.4 = (bf16[32,1600]{1,0:T(8,128)(2,1)S(1)}, bf16[32,1600]{1,0:T(8,128)(2,1)S(1)}, u32[]{:S(2)}, u32[]{:S(2)}) collective-permute-start(bf16[32,1600]{1,0:T(8,128)(2,1)S(1)} %copy-done.1), channel_id=1, source_target_pairs={{0,1},{1,0},{2,3},{3,2},{4,5},{5,4},{6,7},{7,6},{8,9},{9,8},{10,11... | collective-permute-start | bytes 307208 | tf_op jit(solution)/shard_map/ppermute | solution.py:475
  9.1 1.3 %collective-permute-start.5 = (bf16[32,1600]{1,0:T(8,128)(2,1)S(1)}, bf16[32,1600]{1,0:T(8,128)(2,1)S(1)}, u32[]{:S(2)}, u32[]{:S(2)}) collective-permute-start(bf16[32,1600]{1,0:T(8,128)(2,1)S(1)} %collective-permute-done.3.refs_1_), channel_id=1, source_target_pairs={{0,1},{1,0},{2,3},{3,2},{4,5},{5,4},{6,7},{7,6},{8,9},{9,8},{10,11... | collective-permute-start | bytes 307208 | tf_op jit(solution)/shard_map/ppermute | solution.py:475
  11.1 3.9 %collective-permute-start.6 = (bf16[32,512]{1,0:T(8,128)(2,1)S(1)}, bf16[32,512]{1,0:T(8,128)(2,1)S(1)}, u32[]{:S(2)}, u32[]{:S(2)}) collective-permute-start(bf16[32,512]{1,0:T(8,128)(2,1)S(1)} %get-tuple-element.77), channel_id=1, source_target_pairs={{0,4},{4,0},{8,12},{12,8},{16,20},{20,16},{24,28},{28,24},{1,5},{5... | collective-permute-start | bytes 98312 | tf_op jit(solution)/shard_map/ppermute | solution.py:475
  15.2 4.0 %collective-permute-start.7 = (bf16[32,512]{1,0:T(8,128)(2,1)S(1)}, bf16[32,512]{1,0:T(8,128)(2,1)S(1)}, u32[]{:S(2)}, u32[]{:S(2)}) collective-permute-start(bf16[32,512]{1,0:T(8,128)(2,1)S(1)} %get-tuple-element.90), channel_id=1, source_target_pairs={{0,8},{4,12},{8,0},{12,4},{16,24},{20,28},{24,16},{28,20},{1,9},{5... | collective-permute-start | bytes 98312 | tf_op jit(solution)/shard_map/ppermute | solution.py:475
  19.3 4.7 %collective-permute-start.8 = (bf16[16,512]{1,0:T(8,128)(2,1)S(1)}, bf16[16,512]{1,0:T(8,128)(2,1)S(1)}, u32[]{:S(2)}, u32[]{:S(2)}) collective-permute-start(bf16[16,512]{1,0:T(8,128)(2,1)S(1)} %get-tuple-element.102), channel_id=1, source_target_pairs={{0,16},{4,20},{8,24},{12,28},{16,0},{20,4},{24,8},{28,12},{1,17},{... | collective-permute-start | bytes 49160 | tf_op jit(solution)/shard_map/ppermute | solution.py:475
  25.1 1.6 %collective-permute-start.9 = (bf16[2,32,1792]{2,1,0:T(8,128)(2,1)S(1)}, bf16[2,32,1792]{2,1,0:T(8,128)(2,1)S(1)}, u32[]{:S(2)}, u32[]{:S(2)}) collective-permute-start(bf16[2,32,1792]{2,1,0:T(8,128)(2,1)S(1)} %get-tuple-element.114), channel_id=1, source_target_pairs={{0,1},{1,0},{2,3},{3,2},{4,5},{5,4},{6,7},{7,6},{8,9},{9,8},{10,11... | collective-permute-start | bytes 688136 | tf_op jit(solution)/shard_map/ppermute | solution.py:475
  26.7 5.3 %collective-permute-start.10 = (bf16[32,1792]{1,0:T(8,128)(2,1)S(1)}, bf16[32,1792]{1,0:T(8,128)(2,1)S(1)}, u32[]{:S(2)}, u32[]{:S(2)}) collective-permute-start(bf16[32,1792]{1,0:T(8,128)(2,1)S(1)} %add.1), channel_id=1, source_target_pairs={{0,2},{1,3},{2,0},{3,1},{4,6},{5,7},{6,4},{7,5},{8,10},{9,11},{10,... | collective-permute-start | bytes 344072 | tf_op jit(solution)/shard_map/ppermute | solution.py:475

commit v3 on v2

--- a/solution.py
+++ b/solution.py
@@ -372,7 +372,21 @@
     staged.put(x_grad=x_grad + skip * y_grads)
 
 
-def back(bit):
+def put_pieces(staged, steps, gate_rows, pre_rows, bc):
+    piece = gate_rows.shape[0] // len(steps)
+    partial = dot(gate_rows, staged.w_gate[...])
+    partial += dot(pre_rows, staged.w_in[...])
+    depth = partial.shape[1]
+    for at, step in enumerate(steps):
+        made = staged.made["part%d" % step]
+        split = made.shape[1] - bc.shape[1]
+        if split > depth:
+            made[:, split - LANE : split] = jnp.zeros((piece, LANE), made.dtype)
+        made[:, :depth] = partial[at * piece : (at + 1) * piece, :].astype(made.dtype)
+        made[: bc.shape[0], split:] = bc.astype(made.dtype)
+
+
+def back(bit, urgent, later_steps):
     def back_body(staged, gate_ref, pre_ref):
         entry = staged.entry[...]
         states, channels = entry.shape
@@ -396,50 +410,45 @@
         pre_ref[...] = (
             x_grad.astype(BF16).astype(F32) * staged.pre_slope[...]
         ).astype(BF16)
+        bc = staged.made.bc
         local = staged.bc
-        b_part = local[:states, :] + dot(grad_in, staged.leaving[...], NT)
-        c_part = local[states:, :] + dot(state_in, staged.entering[...], NT)
-        tokens = gate_ref.shape[0]
-        kept, sent = staged.made.kept, staged.made.sent
-        piece = tokens // (kept.shape[0] + sent.shape[0])
-        count = kept.shape[0]
-        tp = lax.axis_index(TP)
-        steps = [2 * at for at in range(count)] + [2 * at + 1 for at in range(count)]
-        starts = [pl.multiple_of((tp ^ step) * piece, piece) for step in steps]
-        gate_rows, pre_rows = (
-            jnp.concatenate([ref[pl.ds(start, piece), :] for start in starts], axis=0)
-            for ref in (gate_ref, pre_ref)
-        )
-        partial = dot(gate_rows, staged.w_gate[...]) + dot(pre_rows, staged.w_in[...])
-        depth = partial.shape[1]
-        split = kept.shape[2] - tokens
-        for at in range(2 * count):
-            made, slot = (kept, at) if at < count else (sent, at - count)
-            if split > depth:
-                made[slot, :, split - LANE : split] = jnp.zeros((piece, LANE), made.dtype)
-            made[slot, :, :depth] = partial[at * piece : (at + 1) * piece, :].astype(made.dtype)
-            made[slot, :states, split:] = b_part.astype(made.dtype)
-            made[slot, states : 2 * states, split:] = c_part.astype(made.dtype)
+        bc[:states, :] = local[:states, :] + dot(grad_in, staged.leaving[...], NT)
+        bc[states:, :] = local[states:, :] + dot(state_in, staged.entering[...], NT)
+        piece = gate_ref.shape[0] // len(urgent + later_steps)
+
+        def gathered(ref, steps):
+            tp = lax.axis_index(TP)
+            starts = [pl.multiple_of((tp ^ step) * piece, piece) for step in steps]
+            return jnp.concatenate([ref[pl.ds(start, piece), :] for start in starts], axis=0)
+
+        staged.put(gate_rows=gathered(gate_ref, later_steps))
+        staged.put(pre_rows=gathered(pre_ref, later_steps))
+        put_pieces(staged, urgent, gathered(gate_ref, urgent), gathered(pre_ref, urgent), bc[...])
 
     return back_body
 
 
+def rest(steps):
+    def rest_body(staged):
+        gate_rows, pre_rows = staged.gate_rows[...], staged.pre_rows[...]
+        put_pieces(staged, steps, gate_rows, pre_rows, staged.bc[...])
+
+    return rest_body
+
+
 def add(staged):
-    staged.put(far_sum=(staged.kept[1] + staged.arrived[1].astype(F32)).astype(BF16))
+    values = [staged.take(name)[...].astype(F32) for name in staged.refs]
+    staged.put(sum=sum(values).astype(staged.made.sum.dtype))
 
 
 def total(staged):
     depth = staged.made.grad.shape[1]
     states, tokens = staged.made.b.shape
-    split = staged.kept.shape[2] - tokens
-
-    def summed(rows, lanes):
-        own = staged.kept[0, rows, lanes] + staged.arrived[0, rows, lanes].astype(F32)
-        return own + staged.far_sum[rows, lanes].astype(F32)
-
-    staged.put(grad=summed(slice(None), slice(depth)).astype(BF16))
-    staged.put(b=summed(slice(states), slice(split, None)))
-    staged.put(c=summed(slice(states, 2 * states), slice(split, None)))
+    received = [staged.take(name) for name in staged.refs]
+    split = received[0].shape[1] - tokens
+    staged.put(grad=sum(part[:, :depth].astype(F32) for part in received).astype(BF16))
+    staged.put(b=sum(part[:states, split:].astype(F32) for part in received))
+    staged.put(c=sum(part[states : 2 * states, split:].astype(F32) for part in received))
 
 
 def swap_masks(parts):
@@ -559,18 +568,38 @@
         bit *= 2
     span = round_up(depth, LANE) + tokens
     graded = pltpu.VMEM((tokens, channels), BF16)
+    kept, urgent, others = (0, 2), (2, 3), (0, 1)
+
+    def named(steps):
+        types = {step: F32 if step in kept else BF16 for step in steps}
+        return {"part%d" % step: near((piece, span), types[step]) for step in steps}
+
+    rest_rows = near((piece * len(others), channels), BF16)
     held = call(
-        back(bit),
+        back(bit, urgent, others),
         dict(group, received=received, **results, **slope, entering=first.entering,
              leaving=first.leaving, entry=ready.entry, expander=ready.expander, enter=ready.enter,
              leave=ready.leave, b=ready.b, c=ready.c, w_gate=ready.w_gate, w_in=ready.w_in),
-        dict(kept=near((parts // 2, piece, span), F32), sent=near((parts // 2, piece, span), BF16)),
-        flops=4 * tokens * channels * depth, scratch=(graded, graded),
-    )
-    halves = dict(kept=held.kept, arrived=swap(held.sent, TP, 1))
-    far_sum = call(add, halves, dict(far_sum=near((piece, span), BF16))).far_sum
+        dict(named(urgent), gate_rows=rest_rows,
+             pre_rows=rest_rows, bc=near((2 * states, tokens), F32)),
+        flops=4 * len(urgent) * piece * channels * depth, scratch=(graded, graded),
+    )
+
+    def added(dtype, one, two, **options):
+        return call(add, dict(one=one, two=two), dict(sum=near((piece, span), dtype)), **options).sum
+
+    far_sum = added(BF16, held.part2, swap(held.part3, TP, 1))
+    distant = swap(far_sum, TP, 2)
+    held.update(call(
+        rest(others),
+        dict(gate_rows=ordered(held.gate_rows, far_sum), pre_rows=held.pre_rows, bc=held.bc,
+             w_gate=ready.w_gate, w_in=ready.w_in),
+        named(others),
+        flops=4 * len(others) * piece * channels * depth,
+    ))
+    own = added(F32, held.part0, distant, flops=tokens * channels * depth)
     result = call(
-        total, dict(halves, far_sum=swap(far_sum, TP, 2)),
+        total, dict(own=own, across=swap(held.part1, TP, 1)),
         dict(grad=near((piece, depth), BF16), b=near((states, tokens), F32),
              c=near((states, tokens), F32)),
     )

time: 32.7 us -> 32.6 us (level)
  waiting for transfers between devices: 12.5 us -> 11.7 us
  Pallas kernels: 7.18 us -> 7.75 us
    ppermute x11 -> x12, waiting for transfers between devices: 12.5 us -> 11.7 us  [swap(): return lax.ppermute(value, axis, [(at, at ^ bit) for at in range(size)])]
    pallas_call x11 -> x13, Pallas kernels: 7.18 us -> 7.75 us  [staged_call(): pl.pallas_call(kernel, name=body.__name__, out_shape=[jax.ShapeDtypeStruc...]
    ppermute x11 -> x12, starting transfers between devices: 12.1 us -> 12.2 us  [swap(): return lax.ppermute(value, axis, [(at, at ^ bit) for at in range(size)])]
  transfers between devices with their start and end apart: 11 -> 12, of which waited for: 8 -> 8; matrix products, arithmetic and copies ran while one was open for 0% -> 0% of each run, Pallas kernels for 14% -> 16%
where the time goes in v3:
time: 32.6 us; the launch traced here: 32.4 us
  starting transfers between devices  12.2 us (37%)
  waiting for transfers between devices  11.7 us (36%)
  Pallas kernels  7.75 us (24%)
  between operations  0.75 us (2%)
    ppermute x12, starting transfers between devices, swap(): return lax.ppermute(value, axis, [(at, at ^ bit) for at in range(size)])  12.2 us
    ppermute x12, waiting for transfers between devices, swap(): return lax.ppermute(value, axis, [(at, at ^ bit) for at in range(size)])  11.7 us
    pallas_call x13, Pallas kernels, staged_call(): pl.pallas_call(kernel, name=body.__name__, out_shape=[jax.ShapeDtypeStruc...  7.75 us
  transfers between devices with their start and end apart: 12, of which 8 were waited for; matrix products, arithmetic and copies ran while one was open for 0% of the time, Pallas kernels for 16%

profile of v3, /device:TPU:0, one launch (start us, length us, event | category | flops | bytes accessed | tf_op | source)
XLA Modules:
  0.0 32.4 jit_solution(880737938923681414)
XLA Ops:
  0.6 3.0 %collective-permute-start = (bf16[32,1600]{1,0:T(8,128)(2,1)}, bf16[32,1600]{1,0:T(8,128)(2,1)S(1)}, u32[]{:S(2)}, u32[]{:S(2)}) collective-permute-start(bf16[32,1600]{1,0:T(8,128)(2,1)} %refs_7_.1), channel_id=1, source_target_pairs={{0,2},{1,3},{2,0},{3,1},{4,6},{5,7},{6,4},{7,5},{8,10},{9,11},{10,... | collective-permute-start | bytes 307208 | tf_op jit(solution)/shard_map/ppermute | solution.py:484
  3.7 2.3 %prepare.1 = (f32[128,400]{1,0:T(8,128)S(1)}, f32[128,400]{1,0:T(8,128)S(1)}, f32[128,400]{1,0:T(8,128)S(1)}, f32[128,400]{1,0:T(8,128)S(1)}, f32[16,512]{1,0:T(...) custom-call(bf16[25,128]{1,0:T(8,128)(2,1)} %refs_0_.1, ...), custom_call_target="tpu_custom_call" | custom-call | flops 52428800 | bytes 1048576 | tf_op jit(solution)/shard_map/prepare/pallas_call | solution.py:187
  6.1 1.5 %collective-permute-done.refs_1_ = bf16[32,1600]{1,0:T(8,128)(2,1)S(1)} collective-permute-done((bf16[32,1600]{1,0:T(8,128)(2,1)}, bf16[32,1600]{1,0:T(8,128)(2,1)S(1)}, u32[]{:S(2)}, u32[]{:S(2)}) %collective-permute-start) | collective-permute-done | bytes 102432 | tf_op jit(solution)/shard_map/ppermute | solution.py:484
  7.6 0.5 %collective-permute-start.4 = (bf16[32,1600]{1,0:T(8,128)(2,1)S(1)}, bf16[32,1600]{1,0:T(8,128)(2,1)S(1)}, u32[]{:S(2)}, u32[]{:S(2)}) collective-permute-start(bf16[32,1600]{1,0:T(8,128)(2,1)S(1)} %copy-done.1), channel_id=1, source_target_pairs={{0,1},{1,0},{2,3},{3,2},{4,5},{5,4},{6,7},{7,6},{8,9},{9,8},{10,11... | collective-permute-start | bytes 307208 | tf_op jit(solution)/shard_map/ppermute | solution.py:484
  8.1 1.0 %collective-permute-done.3.refs_1_ = bf16[32,1600]{1,0:T(8,128)(2,1)S(1)} collective-permute-done((bf16[32,1600]{1,0:T(8,128)(2,1)}, bf16[32,1600]{1,0:T(8,128)(2,1)S(1)}, u32[]{:S(2)}, u32[]{:S(2)}) %collective-permute-start.3) | collective-permute-done | bytes 102432 | tf_op jit(solution)/shard_map/ppermute | solution.py:484
  9.1 1.1 %project.1 = (f32[128,400]{1,0:T(8,128)S(1)}, f32[128,400]{1,0:T(8,128)S(1)}, f32[128,400]{1,0:T(8,128)S(1)}, bf16[128,400]{1,0:T(8,128)(2,1)S(1)}, bf16[128,400]{1,0:T(8,128)(2,1)S(1)}, /*index=5*/f32[16,512]{1,0:T(8,128)S(1)}) custom-call(bf16[32,1600]{1,0:T(8,128)(2,1)S(1)} %get-tuple-element.65.refs_0_, ...), custom_call_target="tpu_custom_call" | custom-call | flops 327680000 | bytes 1048576 | tf_op jit(solution)/shard_map/project/pallas_call | solution.py:187
  10.2 0.2 collective-permute-done.5.refs_3_
  10.4 0.7 %front.1 = (f32[128,400]{1,0:T(8,128)S(1)}, bf16[128,400]{1,0:T(8,128)(2,1)S(1)}, bf16[128,400]{1,0:T(8,128)(2,1)S(1)}, f32[16,512]{1,0:T(8,128)S(1)}, bf16[32,512]{1,0:T(8,128)(2,1)S(1)}) custom-call(bf16[32,1600]{1,0:T(8,128)(2,1)S(1)} %get-tuple-element.74.refs_0_, bf16[32,1600]{1,0:T(8,128)(2,1)S(1)} %collective-permute-done.3.refs_1_, ...), custom_call_target="tpu_custom_call" | custom-call | flops 163840000 | bytes 1048576 | tf_op jit(solution)/shard_map/front/pallas_call | solution.py:187
  11.1 1.8 %collective-permute-start.6 = (bf16[32,512]{1,0:T(8,128)(2,1)S(1)}, bf16[32,512]{1,0:T(8,128)(2,1)S(1)}, u32[]{:S(2)}, u32[]{:S(2)}) collective-permute-start(bf16[32,512]{1,0:T(8,128)(2,1)S(1)} %get-tuple-element.83), channel_id=1, source_target_pairs={{0,4},{4,0},{8,12},{12,8},{16,20},{20,16},{24,28},{28,24},{1,5},{5... | collective-permute-start | bytes 98312 | tf_op jit(solution)/shard_map/ppermute | solution.py:484
  12.9 0.2 slopes.1
  13.1 2.0 %collective-permute-done.6.refs_3_ = bf16[32,512]{1,0:T(8,128)(2,1)S(1)} collective-permute-done((bf16[32,512]{1,0:T(8,128)(2,1)S(1)}, bf16[32,512]{1,0:T(8,128)(2,1)S(1)}, u32[]{:S(2)}, u32[]{:S(2)}) %collective-permute-start.6) | collective-permute-done | bytes 32800 | tf_op jit(solution)/shard_map/ppermute | solution.py:484
  15.2 1.9 %collective-permute-start.7 = (bf16[32,512]{1,0:T(8,128)(2,1)S(1)}, bf16[32,512]{1,0:T(8,128)(2,1)S(1)}, u32[]{:S(2)}, u32[]{:S(2)}) collective-permute-start(bf16[32,512]{1,0:T(8,128)(2,1)S(1)} %get-tuple-element.96), channel_id=1, source_target_pairs={{0,8},{4,12},{8,0},{12,4},{16,24},{20,28},{24,16},{28,20},{1,9},{5... | collective-permute-start | bytes 98312 | tf_op jit(solution)/shard_map/ppermute | solution.py:484
  17.1 0.5 %local_vectors.1.refs_5_ = f32[32,128]{1,0:T(8,128)S(1)} custom-call(f32[128,400]{1,0:T(8,128)S(1)} %get-tuple-element.97.refs_0_, f32[128,400]{1,0:T(8,128)S(1)} %get-tuple-element.98.refs_1_, f32[128,128]{1,0:T(8,128)S(1)} %get-tuple-element.99.refs_2_, bf16[16,128]{1,0:T(8,128)(2,1)S(1)} %get-tuple-element.71.refs_6_.refs_3_.refs_16_, ...), custom_call_target="tpu_custom_call" | custom-call | flops 52428800 | bytes 1048576 | tf_op jit(solution)/shard_map/local_vectors/pallas_call | solution.py:187
  17.6 1.6 %collective-permute-done.7.refs_7_ = bf16[32,512]{1,0:T(8,128)(2,1)S(1)} collective-permute-done((bf16[32,512]{1,0:T(8,128)(2,1)S(1)}, bf16[32,512]{1,0:T(8,128)(2,1)S(1)}, u32[]{:S(2)}, u32[]{:S(2)}) %collective-permute-start.7) | collective-permute-done | bytes 32800 | tf_op jit(solution)/shard_map/ppermute | solution.py:484
  19.2 0.1 join_body.3
  19.3 2.9 %collective-permute-start.8 = (bf16[16,512]{1,0:T(8,128)(2,1)S(1)}, bf16[16,512]{1,0:T(8,128)(2,1)S(1)}, u32[]{:S(2)}, u32[]{:S(2)}) collective-permute-start(bf16[16,512]{1,0:T(8,128)(2,1)S(1)} %get-tuple-element.108), channel_id=1, source_target_pairs={{0,16},{4,20},{8,24},{12,28},{16,0},{20,4},{24,8},{28,12},{1,17},{... | collective-permute-start | bytes 49160 | tf_op jit(solution)/shard_map/ppermute | solution.py:484
  22.2 0.4 %local_channels.1 = (f32[128,400]{1,0:T(8,128)S(1)}, f32[128,400]{1,0:T(8,128)S(1)}) custom-call(f32[128,400]{1,0:T(8,128)S(1)} %get-tuple-element.97.refs_0_, f32[128,400]{1,0:T(8,128)S(1)} %get-tuple-element.98.refs_1_, f32[128,128]{1,0:T(8,128)S(1)} %get-tuple-element.109.refs_2_, f32[128,128]{1,0:T(8,128)S(1)} %get-tuple-element.110.refs_3_, ...), custom_call_target="tpu_custom_call" | custom-call | flops 104857600 | bytes 1048576 | tf_op jit(solution)/shard_map/local_channels/pallas_call | solution.py:187
  22.6 1.4 %collective-permute-done.8.refs_4_ = bf16[16,512]{1,0:T(8,128)(2,1)S(1)} collective-permute-done((bf16[16,512]{1,0:T(8,128)(2,1)S(1)}, bf16[16,512]{1,0:T(8,128)(2,1)S(1)}, u32[]{:S(2)}, u32[]{:S(2)}) %collective-permute-start.8) | collective-permute-done | bytes 16416 | tf_op jit(solution)/shard_map/ppermute | solution.py:484
  24.0 1.0 %back_body.1 = (f32[32,1792]{1,0:T(8,128)S(1)}, bf16[32,1792]{1,0:T(8,128)(2,1)S(1)}, bf16[64,400]{1,0:T(8,128)(2,1)S(1)}, bf16[64,400]{1,0:T(8,128)(2,1)S(1)}, f32[32,128]{1,0:T(8,128)S(1)}) custom-call(f32[16,512]{1,0:T(8,128)S(1)} %get-tuple-element.104.refs_0_, f32[16,512]{1,0:T(8,128)S(1)} %get-tuple-element.105.refs_1_, ...), custom_call_target="tpu_custom_call" | custom-call | flops 163840000 | bytes 1048576 | tf_op jit(solution)/shard_map/back_body/pallas_call | solution.py:187
  25.1 1.3 %collective-permute-done.9.refs_1_ = bf16[32,1792]{1,0:T(8,128)(2,1)S(1)} collective-permute-done((bf16[32,1792]{1,0:T(8,128)(2,1)S(1)}, bf16[32,1792]{1,0:T(8,128)(2,1)S(1)}, u32[]{:S(2)}, u32[]{:S(2)}) %collective-permute-start.9) | collective-permute-done | bytes 114720 | tf_op jit(solution)/shard_map/ppermute | solution.py:484
  26.4 1.8 %collective-permute-start.10 = (bf16[32,1792]{1,0:T(8,128)(2,1)S(1)}, bf16[32,1792]{1,0:T(8,128)(2,1)S(1)}, u32[]{:S(2)}, u32[]{:S(2)}) collective-permute-start(bf16[32,1792]{1,0:T(8,128)(2,1)S(1)} %add.2), channel_id=1, source_target_pairs={{0,2},{1,3},{2,0},{3,1},{4,6},{5,7},{6,4},{7,5},{8,10},{9,11},{10,... | collective-permute-start | bytes 344072 | tf_op jit(solution)/shard_map/ppermute | solution.py:484
  28.3 0.6 %rest_body.1 = (f32[32,1792]{1,0:T(8,128)S(1)}, bf16[32,1792]{1,0:T(8,128)(2,1)S(1)}) custom-call(bf16[64,400]{1,0:T(8,128)(2,1)S(1)} %get-tuple-element.122.refs_0_, bf16[64,400]{1,0:T(8,128)(2,1)S(1)} %get-tuple-element.123.refs_1_, f32[32,128]{1,0:T(8,128)S(1)} %get-tuple-element.124.refs_2_, ...), custom_call_target="tpu_custom_call" | custom-call | flops 163840000 | bytes 1048576 | tf_op jit(solution)/shard_map/rest_body/pallas_call | solution.py:187
  28.9 2.8 %collective-permute-done.10.refs_1_ = bf16[32,1792]{1,0:T(8,128)(2,1)S(1)} collective-permute-done((bf16[32,1792]{1,0:T(8,128)(2,1)S(1)}, bf16[32,1792]{1,0:T(8,128)(2,1)S(1)}, u32[]{:S(2)}, u32[]{:S(2)}) %collective-permute-start.10) | collective-permute-done | bytes 114720 | tf_op jit(solution)/shard_map/ppermute | solution.py:484
  31.8 0.7 %total.1 = (bf16[32,1600]{1,0:T(8,128)(2,1)}, f32[16,128]{1,0:T(8,128)}, f32[16,128]{1,0:T(8,128)}) custom-call(f32[32,1792]{1,0:T(8,128)S(1)} %add.3.refs_0_, bf16[32,1792]{1,0:T(8,128)(2,1)S(1)} %collective-permute-done.11.refs_1_), custom_call_target="tpu_custom_call" | custom-call | bytes 1048576 | tf_op jit(solution)/shard_map/total/pallas_call | solution.py:187
  (17 shorter events, 0.5 us)
Async XLA Ops:
  0.6 7.0 %collective-permute-start = (bf16[32,1600]{1,0:T(8,128)(2,1)}, bf16[32,1600]{1,0:T(8,128)(2,1)S(1)}, u32[]{:S(2)}, u32[]{:S(2)}) collective-permute-start(bf16[32,1600]{1,0:T(8,128)(2,1)} %refs_7_.1), channel_id=1, source_target_pairs={{0,2},{1,3},{2,0},{3,1},{4,6},{5,7},{6,4},{7,5},{8,10},{9,11},{10,... | collective-permute-start | bytes 307208 | tf_op jit(solution)/shard_map/ppermute | solution.py:484
  3.6 5.5 %collective-permute-start.3 = (bf16[32,1600]{1,0:T(8,128)(2,1)}, bf16[32,1600]{1,0:T(8,128)(2,1)S(1)}, u32[]{:S(2)}, u32[]{:S(2)}) collective-permute-start(bf16[32,1600]{1,0:T(8,128)(2,1)} %refs_8_.1), channel_id=1, source_target_pairs={{0,2},{1,3},{2,0},{3,1},{4,6},{5,7},{6,4},{7,5},{8,10},{9,11},{10,... | collective-permute-start | bytes 307208 | tf_op jit(solution)/shard_map/ppermute | solution.py:484
  3.7 2.3 %copy-start = (bf16[32,1600]{1,0:T(8,128)(2,1)S(1)}, bf16[32,1600]{1,0:T(8,128)(2,1)}, u32[]{:S(2)}) copy-start(bf16[32,1600]{1,0:T(8,128)(2,1)} %refs_7_.1) | copy-start | bytes 307204
  3.7 3.9 %copy-start.1 = (bf16[32,1600]{1,0:T(8,128)(2,1)S(1)}, bf16[32,1600]{1,0:T(8,128)(2,1)}, u32[]{:S(2)}) copy-start(bf16[32,1600]{1,0:T(8,128)(2,1)} %refs_8_.1) | copy-start | bytes 307204
  6.1 3.0 %collective-permute-start.1 = (bf16[32,1600]{1,0:T(8,128)(2,1)S(1)}, bf16[32,1600]{1,0:T(8,128)(2,1)S(1)}, u32[]{:S(2)}, u32[]{:S(2)}) collective-permute-start(bf16[32,1600]{1,0:T(8,128)(2,1)S(1)} %copy-done), channel_id=1, source_target_pairs={{0,1},{1,0},{2,3},{3,2},{4,5},{5,4},{6,7},{7,6},{8,9},{9,8},{10,11... | collective-permute-start | bytes 307208 | tf_op jit(solution)/shard_map/ppermute | solution.py:484
  7.6 1.5 %collective-permute-start.2 = (bf16[32,1600]{1,0:T(8,128)(2,1)S(1)}, bf16[32,1600]{1,0:T(8,128)(2,1)S(1)}, u32[]{:S(2)}, u32[]{:S(2)}) collective-permute-start(bf16[32,1600]{1,0:T(8,128)(2,1)S(1)} %collective-permute-done.refs_1_), channel_id=1, source_target_pairs={{0,1},{1,0},{2,3},{3,2},{4,5},{5,4},{6,7},{7,6},{8,9},{9,8},{10,11... | collective-permute-start | bytes 307208 | tf_op jit(solution)/shard_map/ppermute | solution.py:484
  7.6 2.6 %collective-permute-start.4 = (bf16[32,1600]{1,0:T(8,128)(2,1)S(1)}, bf16[32,1600]{1,0:T(8,128)(2,1)S(1)}, u32[]{:S(2)}, u32[]{:S(2)}) collective-permute-start(bf16[32,1600]{1,0:T(8,128)(2,1)S(1)} %copy-done.1), channel_id=1, source_target_pairs={{0,1},{1,0},{2,3},{3,2},{4,5},{5,4},{6,7},{7,6},{8,9},{9,8},{10,11... | collective-permute-start | bytes 307208 | tf_op jit(solution)/shard_map/ppermute | solution.py:484
  9.1 1.3 %collective-permute-start.5 = (bf16[32,1600]{1,0:T(8,128)(2,1)S(1)}, bf16[32,1600]{1,0:T(8,128)(2,1)S(1)}, u32[]{:S(2)}, u32[]{:S(2)}) collective-permute-start(bf16[32,1600]{1,0:T(8,128)(2,1)S(1)} %collective-permute-done.3.refs_1_), channel_id=1, source_target_pairs={{0,1},{1,0},{2,3},{3,2},{4,5},{5,4},{6,7},{7,6},{8,9},{9,8},{10,11... | collective-permute-start | bytes 307208 | tf_op jit(solution)/shard_map/ppermute | solution.py:484
  11.1 3.9 %collective-permute-start.6 = (bf16[32,512]{1,0:T(8,128)(2,1)S(1)}, bf16[32,512]{1,0:T(8,128)(2,1)S(1)}, u32[]{:S(2)}, u32[]{:S(2)}) collective-permute-start(bf16[32,512]{1,0:T(8,128)(2,1)S(1)} %get-tuple-element.83), channel_id=1, source_target_pairs={{0,4},{4,0},{8,12},{12,8},{16,20},{20,16},{24,28},{28,24},{1,5},{5... | collective-permute-start | bytes 98312 | tf_op jit(solution)/shard_map/ppermute | solution.py:484
  15.2 4.0 %collective-permute-start.7 = (bf16[32,512]{1,0:T(8,128)(2,1)S(1)}, bf16[32,512]{1,0:T(8,128)(2,1)S(1)}, u32[]{:S(2)}, u32[]{:S(2)}) collective-permute-start(bf16[32,512]{1,0:T(8,128)(2,1)S(1)} %get-tuple-element.96), channel_id=1, source_target_pairs={{0,8},{4,12},{8,0},{12,4},{16,24},{20,28},{24,16},{28,20},{1,9},{5... | collective-permute-start | bytes 98312 | tf_op jit(solution)/shard_map/ppermute | solution.py:484
  19.3 4.7 %collective-permute-start.8 = (bf16[16,512]{1,0:T(8,128)(2,1)S(1)}, bf16[16,512]{1,0:T(8,128)(2,1)S(1)}, u32[]{:S(2)}, u32[]{:S(2)}) collective-permute-start(bf16[16,512]{1,0:T(8,128)(2,1)S(1)} %get-tuple-element.108), channel_id=1, source_target_pairs={{0,16},{4,20},{8,24},{12,28},{16,0},{20,4},{24,8},{28,12},{1,17},{... | collective-permute-start | bytes 49160 | tf_op jit(solution)/shard_map/ppermute | solution.py:484
  25.0 1.4 %collective-permute-start.9 = (bf16[32,1792]{1,0:T(8,128)(2,1)S(1)}, bf16[32,1792]{1,0:T(8,128)(2,1)S(1)}, u32[]{:S(2)}, u32[]{:S(2)}) collective-permute-start(bf16[32,1792]{1,0:T(8,128)(2,1)S(1)} %get-tuple-element.121), channel_id=1, source_target_pairs={{0,1},{1,0},{2,3},{3,2},{4,5},{5,4},{6,7},{7,6},{8,9},{9,8},{10,11... | collective-permute-start | bytes 344072 | tf_op jit(solution)/shard_map/ppermute | solution.py:484
  26.4 5.3 %collective-permute-start.10 = (bf16[32,1792]{1,0:T(8,128)(2,1)S(1)}, bf16[32,1792]{1,0:T(8,128)(2,1)S(1)}, u32[]{:S(2)}, u32[]{:S(2)}) collective-permute-start(bf16[32,1792]{1,0:T(8,128)(2,1)S(1)} %add.2), channel_id=1, source_target_pairs={{0,2},{1,3},{2,0},{3,1},{4,6},{5,7},{6,4},{7,5},{8,10},{9,11},{10,... | collective-permute-start | bytes 344072 | tf_op jit(solution)/shard_map/ppermute | solution.py:484
  28.9 2.9 %collective-permute-start.11 = (bf16[32,1792]{1,0:T(8,128)(2,1)S(1)}, bf16[32,1792]{1,0:T(8,128)(2,1)S(1)}, u32[]{:S(2)}, u32[]{:S(2)}) collective-permute-start(bf16[32,1792]{1,0:T(8,128)(2,1)S(1)} %get-tuple-element.126), channel_id=1, source_target_pairs={{0,1},{1,0},{2,3},{3,2},{4,5},{5,4},{6,7},{7,6},{8,9},{9,8},{10,11... | collective-permute-start | bytes 344072 | tf_op jit(solution)/shard_map/ppermute | solution.py:484

commit v4 on v3

--- a/solution.py
+++ b/solution.py
@@ -269,6 +269,8 @@
     staged.put(crossed_back=jnp.where(anticausal, dot(b_rows, c_rows, TN), 0.0))
     staged.put(b=b_rows)
     staged.put(c=c_rows)
+    staged.put(b_columns=b_rows.astype(F32).T.astype(BF16))
+    staged.put(c_columns=c_rows.astype(F32).T.astype(BF16))
 
 
 def put_summary(staged, name, vectors, values):
@@ -306,42 +308,53 @@
     put_message(staged, state_part, grad_part, staged.factor[...], channels, 1)
 
 
-def join(channels, bit):
+def joined(mine, other, later):
+    factor, state, grad = mine
+    other_factor, other_state, other_grad = other
+    return (
+        factor * other_factor,
+        jnp.where(later, other_factor * state + other_state, factor * other_state + state),
+        jnp.where(later, grad + factor * other_grad, other_grad + other_factor * grad),
+    )
+
+
+def entered(edges, other, later):
+    keep, held, back_keep, back_held = edges
+    factor, state, grad = other
+    return (
+        jnp.where(later, keep, keep * factor),
+        jnp.where(later, held, keep * state + held),
+        jnp.where(later, back_keep * factor, back_keep),
+        jnp.where(later, back_keep * grad + back_held, back_held),
+    )
+
+
+def join(channels, bit, flips):
     def join_body(staged):
-        received, expander = staged.received, staged.expander[...]
-        factor, state, grad = (staged.take(name)[...] for name in ("factor", "state", "grad"))
-        states = state.shape[0]
-        other_state = received[:states, :].astype(F32)
-        other_grad = received[states:, :].astype(F32)
-        other = decode(received[:states, :], expander)
+        expander = staged.expander[...]
+        mine = staged.factor[...], staged.state[...], staged.grad[...]
+        states = mine[1].shape[0]
+        others = []
+        for flip in flips:
+            received = staged.take("received%d" % flip)
+            summaries = received[:states, :].astype(F32), received[states:, :].astype(F32)
+            others.append((decode(received[:states, :], expander), *summaries))
+        if "keep" in staged.refs:
+            refs = staged.keep, staged.held, staged.back_keep, staged.back_held
+            edges = tuple(ref[...] for ref in refs)
+        else:
+            one, none = jnp.ones_like(mine[0]), jnp.zeros_like(mine[0])
+            edges = one, none, one, none
         later = partner_is_later(bit)
-        if bit == 1:
-            before = jnp.where(later, 1.0, other), jnp.where(later, 0.0, other_state)
-            behind = jnp.where(later, other, 1.0), jnp.where(later, other_grad, 0.0)
-        else:
-            keep, held, back_keep, back_held = (
-                staged.take(name)[...] for name in ("keep", "held", "back_keep", "back_held")
-            )
-            before = (
-                jnp.where(later, keep, keep * other),
-                jnp.where(later, held, keep * other_state + held),
-            )
-            behind = (
-                jnp.where(later, back_keep * other, back_keep),
-                jnp.where(later, back_keep * other_grad + back_held, back_held),
-            )
-        staged.put(keep=before[0])
-        staged.put(held=before[1])
-        staged.put(back_keep=behind[0])
-        staged.put(back_held=behind[1])
-        joined_state = jnp.where(later, other * state + other_state, factor * other_state + state)
-        joined_grad = jnp.where(later, grad + factor * other_grad, other_grad + other * grad)
-        joined = factor * other
-        put_message(staged, joined_state, joined_grad, joined, channels, 2 * bit)
+        edges, mine = entered(edges, others[0], later), joined(mine, others[0], later)
+        if len(flips) == 3:
+            pair, later = joined(others[1], others[2], later), partner_is_later(2 * bit)
+            edges, mine = entered(edges, pair, later), joined(mine, pair, later)
+        staged.put(keep=edges[0], held=edges[1], back_keep=edges[2], back_held=edges[3])
+        factor, state, grad = mine
+        put_message(staged, state, grad, factor, channels, bit * (len(flips) + 1))
         if "state" in staged.made:
-            staged.put(state=joined_state)
-            staged.put(grad=joined_grad)
-            staged.put(factor=joined)
+            staged.put(state=state, grad=grad, factor=factor)
 
     return join_body
 
@@ -372,10 +385,23 @@
     staged.put(x_grad=x_grad + skip * y_grads)
 
 
-def put_pieces(staged, steps, gate_rows, pre_rows, bc):
-    piece = gate_rows.shape[0] // len(steps)
-    partial = dot(gate_rows, staged.w_gate[...])
-    partial += dot(pre_rows, staged.w_in[...])
+def put_pieces(staged, steps, state_in, grad_in, bc, gate_ref, pre_ref):
+    tp = lax.axis_index(TP)
+    tokens = gate_ref.shape[0]
+    piece = tokens // len(steps)
+    half = pl.ds(pl.multiple_of((tp ^ steps[0]) // 2 * tokens, tokens), tokens)
+    carried = dot(staged.c_columns[half, :], state_in)
+    ssm_out = staged.ssm[half, :] + staged.enter[half, :] * carried
+    gate_ref[...] = (ssm_out.astype(BF16).astype(F32) * staged.gate_slope[half, :]).astype(BF16)
+    carried = dot(staged.b_columns[half, :], grad_in)
+    x_grad = staged.x_grad[half, :] + staged.leave[half, :] * carried
+    pre_ref[...] = (x_grad.astype(BF16).astype(F32) * staged.pre_slope[half, :]).astype(BF16)
+    starts = [pl.multiple_of((tp ^ step) % 2 * piece, piece) for step in steps]
+    gate_rows, pre_rows = (
+        jnp.concatenate([ref[pl.ds(start, piece), :] for start in starts], axis=0)
+        for ref in (gate_ref, pre_ref)
+    )
+    partial = dot(gate_rows, staged.w_gate[...]) + dot(pre_rows, staged.w_in[...])
     depth = partial.shape[1]
     for at, step in enumerate(steps):
         made = staged.made["part%d" % step]
@@ -386,7 +412,7 @@
         made[: bc.shape[0], split:] = bc.astype(made.dtype)
 
 
-def back(bit, urgent, later_steps):
+def back(bit, steps):
     def back_body(staged, gate_ref, pre_ref):
         entry = staged.entry[...]
         states, channels = entry.shape
@@ -395,43 +421,26 @@
         other = decode(received[...], staged.expander[...])[:, :channels]
         later = partner_is_later(bit)
         keep, held, back_keep, back_held = (
-            staged.take(name)[:, :channels] for name in ("keep", "held", "back_keep", "back_held")
+            ref[:, :channels]
+            for ref in (staged.keep, staged.held, staged.back_keep, staged.back_held)
         )
         state = jnp.where(later, entry, other * entry + other_part)
         state_in = (keep * state + held).astype(BF16)
         grad_in = jnp.where(later, back_keep * other_part + back_held, back_held).astype(BF16)
-        carried = dot(staged.c[...], state_in, TN)
-        ssm_out = staged.ssm[...] + staged.enter[...] * carried
-        gate_ref[...] = (
-            ssm_out.astype(BF16).astype(F32) * staged.gate_slope[...]
-        ).astype(BF16)
-        carried = dot(staged.b[...], grad_in, TN)
-        x_grad = staged.x_grad[...] + staged.leave[...] * carried
-        pre_ref[...] = (
-            x_grad.astype(BF16).astype(F32) * staged.pre_slope[...]
-        ).astype(BF16)
+        staged.put(state_in=state_in, grad_in=grad_in)
         bc = staged.made.bc
         local = staged.bc
         bc[:states, :] = local[:states, :] + dot(grad_in, staged.leaving[...], NT)
         bc[states:, :] = local[states:, :] + dot(state_in, staged.entering[...], NT)
-        piece = gate_ref.shape[0] // len(urgent + later_steps)
-
-        def gathered(ref, steps):
-            tp = lax.axis_index(TP)
-            starts = [pl.multiple_of((tp ^ step) * piece, piece) for step in steps]
-            return jnp.concatenate([ref[pl.ds(start, piece), :] for start in starts], axis=0)
-
-        staged.put(gate_rows=gathered(gate_ref, later_steps))
-        staged.put(pre_rows=gathered(pre_ref, later_steps))
-        put_pieces(staged, urgent, gathered(gate_ref, urgent), gathered(pre_ref, urgent), bc[...])
+        put_pieces(staged, steps, state_in, grad_in, bc[...], gate_ref, pre_ref)
 
     return back_body
 
 
 def rest(steps):
-    def rest_body(staged):
-        gate_rows, pre_rows = staged.gate_rows[...], staged.pre_rows[...]
-        put_pieces(staged, steps, gate_rows, pre_rows, staged.bc[...])
+    def rest_body(staged, gate_ref, pre_ref):
+        state_in, grad_in = staged.state_in[...], staged.grad_in[...]
+        put_pieces(staged, steps, state_in, grad_in, staged.bc[...], gate_ref, pre_ref)
 
     return rest_body
 
@@ -474,6 +483,7 @@
     half = near((tokens, channels), BF16)
     square = near((tokens, tokens), F32)
     row = near((states, tokens), BF16)
+    column = near((tokens, states), BF16)
     summary = near((states, width), F32)
 
     def ordered(value, after):
@@ -496,7 +506,7 @@
         prepare, {name: far(value) for name, value in far_ins.items()},
         dict(enter=wide, leave=wide, rise=wide, fall=wide, factor=summary,
              expander=near((width - channels // LANE * LANE, width), BF16), causal=square,
-             crossed=square, crossed_back=square, b=row, c=row),
+             crossed=square, crossed_back=square, b=row, c=row, b_columns=column, c_columns=column),
         flops=8 * tokens * channels * tokens,
         through=("w_gate", "w_in", "w_out", "rows0", "grad0", "entry", "skip"),
     )
@@ -528,61 +538,66 @@
         dict(mix=wide, y=half, entering=half, grad=summary, message=both),
         flops=2 * tokens * channels * depth, scratch=(assembled,),
     ))
-    group = dict(dict(state=first.state, grad=first.grad), factor=ready.factor)
-    received = swap(first.message, SEQ, 1)
-    slope = call(
-        slopes, dict(pre=first.pre, gate=first.gate, mix=first.mix),
-        dict(pre_slope=wide, gate_slope=wide), flops=tokens * channels * 32,
-    )
-    received = ordered(received, slope.pre_slope)
-    x_rows, y_grads = first.x, first.y
+    group = dict(state=first.state, grad=first.grad, factor=ready.factor)
+    message, x_rows, y_grads = first.message, first.x, first.y
     results, bit = {}, 1
     while 2 * bit < owners:
-        last = 4 * bit >= owners
+        flips = (bit, 2 * bit, 3 * bit) if 4 * bit < owners else (bit,)
+        arrived = {flip: swap(message, SEQ, flip) for flip in flips}
+        if bit == 1:
+            slope = call(
+                slopes, dict(pre=first.pre, gate=first.gate, mix=first.mix),
+                dict(pre_slope=wide, gate_slope=wide), flops=tokens * channels * 32,
+            )
+            results.update(call(
+                local_vectors,
+                dict(rise=ready.rise, fall=ready.fall, causal=ready.causal, b=ready.b, c=ready.c,
+                     x=x_rows, y=ordered(y_grads, slope.pre_slope)),
+                dict(bc=near((2 * states, tokens), F32)), flops=8 * tokens * channels * tokens,
+            ))
+            arrived[flips[-1]] = ordered(arrived[flips[-1]], results["bc"])
+        after = bit * (len(flips) + 1)
+        last = 2 * after >= owners
         outs = dict(keep=summary, held=summary, back_keep=summary, back_held=summary,
                     message=one if last else both)
         if not last:
             outs.update(state=summary, grad=summary, factor=summary)
         group = call(
-            join(channels, bit), dict(group, received=received, expander=ready.expander),
+            join(channels, bit, flips),
+            dict(group, expander=ready.expander,
+                 **{"received%d" % flip: value for flip, value in arrived.items()}),
             outs,
         )
-        received = swap(group.pop("message"), SEQ, 2 * bit)
-        if bit == 1:
-            results.update(call(
-                local_vectors,
-                dict(rise=ready.rise, fall=ready.fall, causal=ready.causal, b=ready.b, c=ready.c,
-                     x=ordered(x_rows, group.keep), y=y_grads),
-                dict(bc=near((2 * states, tokens), F32)), flops=8 * tokens * channels * tokens,
-            ))
-            if not last:
-                received = ordered(received, results["bc"])
-        if last:
-            results.update(call(
-                local_channels,
-                dict(rise=ready.rise, fall=ready.fall, crossed=ready.crossed,
-                     crossed_back=ready.crossed_back, skip=ready.skip,
-                     x=ordered(x_rows, group.keep), y=y_grads),
-                dict(ssm=wide, x_grad=wide), flops=16 * tokens * channels * tokens,
-            ))
-        bit *= 2
+        message = group.pop("message")
+        bit = after
+    received = swap(message, SEQ, bit)
+    results.update(call(
+        local_channels,
+        dict(rise=ready.rise, fall=ready.fall, crossed=ready.crossed,
+             crossed_back=ready.crossed_back, skip=ready.skip,
+             x=ordered(x_rows, group.keep), y=y_grads),
+        dict(ssm=wide, x_grad=wide), flops=16 * tokens * channels * tokens,
+    ))
     span = round_up(depth, LANE) + tokens
-    graded = pltpu.VMEM((tokens, channels), BF16)
+    graded = pltpu.VMEM((tokens // 2, channels), BF16)
     kept, urgent, others = (0, 2), (2, 3), (0, 1)
 
     def named(steps):
         types = {step: F32 if step in kept else BF16 for step in steps}
         return {"part%d" % step: near((piece, span), types[step]) for step in steps}
 
-    rest_rows = near((piece * len(others), channels), BF16)
+    entered = near((states, channels), BF16)
+    shared = dict(
+        results, pre_slope=slope.pre_slope, gate_slope=slope.gate_slope, enter=ready.enter,
+        leave=ready.leave, b_columns=ready.b_columns, c_columns=ready.c_columns,
+        w_gate=ready.w_gate, w_in=ready.w_in,
+    )
     held = call(
-        back(bit, urgent, others),
-        dict(group, received=received, **results, **slope, entering=first.entering,
-             leaving=first.leaving, entry=ready.entry, expander=ready.expander, enter=ready.enter,
-             leave=ready.leave, b=ready.b, c=ready.c, w_gate=ready.w_gate, w_in=ready.w_in),
-        dict(named(urgent), gate_rows=rest_rows,
-             pre_rows=rest_rows, bc=near((2 * states, tokens), F32)),
-        flops=4 * len(urgent) * piece * channels * depth, scratch=(graded, graded),
+        back(bit, urgent),
+        dict(shared, **group, received=received, entering=first.entering, leaving=first.leaving,
+             entry=ready.entry, expander=ready.expander),
+        dict(named(urgent), bc=near((2 * states, tokens), F32), state_in=entered, grad_in=entered),
+        flops=2 * tokens * channels * depth, scratch=(graded, graded),
     )
 
     def added(dtype, one, two, **options):
@@ -590,12 +605,12 @@
 
     far_sum = added(BF16, held.part2, swap(held.part3, TP, 1))
     distant = swap(far_sum, TP, 2)
+    shared.update(
+        bc=held.bc, state_in=ordered(held.state_in, far_sum), grad_in=held.grad_in
+    )
     held.update(call(
-        rest(others),
-        dict(gate_rows=ordered(held.gate_rows, far_sum), pre_rows=held.pre_rows, bc=held.bc,
-             w_gate=ready.w_gate, w_in=ready.w_in),
-        named(others),
-        flops=4 * len(others) * piece * channels * depth,
+        rest(others), shared, named(others),
+        flops=2 * tokens * channels * depth, scratch=(graded, graded),
     ))
     own = added(F32, held.part0, distant, flops=tokens * channels * depth)
     result = call(

time: 32.6 us -> 31.7 us (0.972)
  starting transfers between devices: 12.2 us -> 11.5 us
    ppermute x12 -> x13, starting transfers between devices: 12.2 us -> 11.5 us  [swap(): return lax.ppermute(value, axis, [(at, at ^ bit) for at in range(size)])]
    ppermute x12 -> x13, waiting for transfers between devices: 11.7 us -> 11.5 us  [swap(): return lax.ppermute(value, axis, [(at, at ^ bit) for at in range(size)])]
    pallas_call x13 -> x12, Pallas kernels: 7.75 us -> 7.73 us  [staged_call(): pl.pallas_call(kernel, name=body.__name__, out_shape=[jax.ShapeDtypeStruc...]
  transfers between devices with their start and end apart: 12 -> 13, of which waited for: 8 -> 9; matrix products, arithmetic and copies ran while one was open for 0% -> 0% of each run, Pallas kernels for 16% -> 17%
where the time goes in v4:
time: 31.7 us; the launch traced here: 31.5 us
  starting transfers between devices  11.5 us (36%)
  waiting for transfers between devices  11.5 us (36%)
  Pallas kernels  7.73 us (24%)
  between operations  0.75 us (2%)
    ppermute x13, starting transfers between devices, swap(): return lax.ppermute(value, axis, [(at, at ^ bit) for at in range(size)])  11.5 us
    ppermute x13, waiting for transfers between devices, swap(): return lax.ppermute(value, axis, [(at, at ^ bit) for at in range(size)])  11.5 us
    pallas_call x12, Pallas kernels, staged_call(): pl.pallas_call(kernel, name=body.__name__, out_shape=[jax.ShapeDtypeStruc...  7.73 us
  transfers between devices with their start and end apart: 13, of which 9 were waited for; matrix products, arithmetic and copies ran while one was open for 0% of the time, Pallas kernels for 17%

profile of v4, /device:TPU:0, one launch (start us, length us, event | category | flops | bytes accessed | tf_op | source)
XLA Modules:
  0.0 31.5 jit_solution(7737587985062368944)
XLA Ops:
  0.6 3.0 %collective-permute-start = (bf16[32,1600]{1,0:T(8,128)(2,1)}, bf16[32,1600]{1,0:T(8,128)(2,1)S(1)}, u32[]{:S(2)}, u32[]{:S(2)}) collective-permute-start(bf16[32,1600]{1,0:T(8,128)(2,1)} %refs_7_.1), channel_id=1, source_target_pairs={{0,2},{1,3},{2,0},{3,1},{4,6},{5,7},{6,4},{7,5},{8,10},{9,11},{10,... | collective-permute-start | bytes 307208 | tf_op jit(solution)/shard_map/ppermute | solution.py:494
  3.7 2.3 %prepare.1 = (f32[128,400]{1,0:T(8,128)S(1)}, f32[128,400]{1,0:T(8,128)S(1)}, f32[128,400]{1,0:T(8,128)S(1)}, f32[128,400]{1,0:T(8,128)S(1)}, f32[16,512]{1,0:T(...) custom-call(bf16[25,128]{1,0:T(8,128)(2,1)} %refs_0_.1, ...), custom_call_target="tpu_custom_call" | custom-call | flops 52428800 | bytes 1048576 | tf_op jit(solution)/shard_map/prepare/pallas_call | solution.py:187
  6.1 1.5 %collective-permute-done.refs_1_ = bf16[32,1600]{1,0:T(8,128)(2,1)S(1)} collective-permute-done((bf16[32,1600]{1,0:T(8,128)(2,1)}, bf16[32,1600]{1,0:T(8,128)(2,1)S(1)}, u32[]{:S(2)}, u32[]{:S(2)}) %collective-permute-start) | collective-permute-done | bytes 102432 | tf_op jit(solution)/shard_map/ppermute | solution.py:494
  7.6 0.5 %collective-permute-start.4 = (bf16[32,1600]{1,0:T(8,128)(2,1)S(1)}, bf16[32,1600]{1,0:T(8,128)(2,1)S(1)}, u32[]{:S(2)}, u32[]{:S(2)}) collective-permute-start(bf16[32,1600]{1,0:T(8,128)(2,1)S(1)} %copy-done.1), channel_id=1, source_target_pairs={{0,1},{1,0},{2,3},{3,2},{4,5},{5,4},{6,7},{7,6},{8,9},{9,8},{10,11... | collective-permute-start | bytes 307208 | tf_op jit(solution)/shard_map/ppermute | solution.py:494
  8.1 1.0 %collective-permute-done.3.refs_1_ = bf16[32,1600]{1,0:T(8,128)(2,1)S(1)} collective-permute-done((bf16[32,1600]{1,0:T(8,128)(2,1)}, bf16[32,1600]{1,0:T(8,128)(2,1)S(1)}, u32[]{:S(2)}, u32[]{:S(2)}) %collective-permute-start.3) | collective-permute-done | bytes 102432 | tf_op jit(solution)/shard_map/ppermute | solution.py:494
  9.1 1.1 %project.1 = (f32[128,400]{1,0:T(8,128)S(1)}, f32[128,400]{1,0:T(8,128)S(1)}, f32[128,400]{1,0:T(8,128)S(1)}, bf16[128,400]{1,0:T(8,128)(2,1)S(1)}, bf16[128,400]{1,0:T(8,128)(2,1)S(1)}, /*index=5*/f32[16,512]{1,0:T(8,128)S(1)}) custom-call(bf16[32,1600]{1,0:T(8,128)(2,1)S(1)} %get-tuple-element.63.refs_0_, ...), custom_call_target="tpu_custom_call" | custom-call | flops 327680000 | bytes 1048576 | tf_op jit(solution)/shard_map/project/pallas_call | solution.py:187
  10.4 0.7 %front.1 = (f32[128,400]{1,0:T(8,128)S(1)}, bf16[128,400]{1,0:T(8,128)(2,1)S(1)}, bf16[128,400]{1,0:T(8,128)(2,1)S(1)}, f32[16,512]{1,0:T(8,128)S(1)}, bf16[32,512]{1,0:T(8,128)(2,1)S(1)}) custom-call(bf16[32,1600]{1,0:T(8,128)(2,1)S(1)} %get-tuple-element.71.refs_0_, bf16[32,1600]{1,0:T(8,128)(2,1)S(1)} %collective-permute-done.3.refs_1_, ...), custom_call_target="tpu_custom_call" | custom-call | flops 163840000 | bytes 1048576 | tf_op jit(solution)/shard_map/front/pallas_call | solution.py:187
  11.1 2.8 %collective-permute-start.8 = (bf16[32,512]{1,0:T(8,128)(2,1)S(1)}, bf16[32,512]{1,0:T(8,128)(2,1)S(1)}, u32[]{:S(2)}, u32[]{:S(2)}) collective-permute-start(bf16[32,512]{1,0:T(8,128)(2,1)S(1)} %get-tuple-element.89), channel_id=1, source_target_pairs={{0,12},{4,8},{8,4},{12,0},{16,28},{20,24},{24,20},{28,16},{1,13},{... | collective-permute-start | bytes 98312 | tf_op jit(solution)/shard_map/ppermute | solution.py:494
  13.9 0.4 %collective-permute-start.7 = (bf16[32,512]{1,0:T(8,128)(2,1)S(1)}, bf16[32,512]{1,0:T(8,128)(2,1)S(1)}, u32[]{:S(2)}, u32[]{:S(2)}) collective-permute-start(bf16[32,512]{1,0:T(8,128)(2,1)S(1)} %get-tuple-element.89), channel_id=1, source_target_pairs={{0,8},{4,12},{8,0},{12,4},{16,24},{20,28},{24,16},{28,20},{1,9},{5... | collective-permute-start | bytes 98312 | tf_op jit(solution)/shard_map/ppermute | solution.py:494
  14.4 0.3 collective-permute-start.6
  14.8 0.5 %local_vectors.1.refs_0_ = f32[32,128]{1,0:T(8,128)S(1)} custom-call(f32[128,400]{1,0:T(8,128)S(1)} %get-tuple-element.58.refs_0_, f32[128,400]{1,0:T(8,128)S(1)} %get-tuple-element.59.refs_1_, f32[128,128]{1,0:T(8,128)S(1)} %get-tuple-element.60.refs_2_, bf16[16,128]{1,0:T(8,128)(2,1)S(1)} %get-tuple-element.61.refs_6_.refs_3_, ...), custom_call_target="tpu_custom_call" | custom-call | flops 52428800 | bytes 1048576 | tf_op jit(solution)/shard_map/local_vectors/pallas_call | solution.py:187
  15.3 0.7 %collective-permute-done.8.refs_6_ = bf16[32,512]{1,0:T(8,128)(2,1)S(1)} collective-permute-done((bf16[32,512]{1,0:T(8,128)(2,1)S(1)}, bf16[32,512]{1,0:T(8,128)(2,1)S(1)}, u32[]{:S(2)}, u32[]{:S(2)}) %collective-permute-start.8) | collective-permute-done | bytes 32800 | tf_op jit(solution)/shard_map/ppermute | solution.py:494
  15.9 1.9 %collective-permute-done.7.refs_5_ = bf16[32,512]{1,0:T(8,128)(2,1)S(1)} collective-permute-done((bf16[32,512]{1,0:T(8,128)(2,1)S(1)}, bf16[32,512]{1,0:T(8,128)(2,1)S(1)}, u32[]{:S(2)}, u32[]{:S(2)}) %collective-permute-start.7) | collective-permute-done | bytes 32800 | tf_op jit(solution)/shard_map/ppermute | solution.py:494
  17.8 0.4 %collective-permute-done.6.refs_4_ = bf16[32,512]{1,0:T(8,128)(2,1)S(1)} collective-permute-done((bf16[32,512]{1,0:T(8,128)(2,1)S(1)}, bf16[32,512]{1,0:T(8,128)(2,1)S(1)}, u32[]{:S(2)}, u32[]{:S(2)}) %collective-permute-start.6) | collective-permute-done | bytes 32800 | tf_op jit(solution)/shard_map/ppermute | solution.py:494
  18.3 0.2 join_body.1
  18.5 2.7 %collective-permute-start.9 = (bf16[16,512]{1,0:T(8,128)(2,1)S(1)}, bf16[16,512]{1,0:T(8,128)(2,1)S(1)}, u32[]{:S(2)}, u32[]{:S(2)}) collective-permute-start(bf16[16,512]{1,0:T(8,128)(2,1)S(1)} %get-tuple-element.101), channel_id=1, source_target_pairs={{0,16},{4,20},{8,24},{12,28},{16,0},{20,4},{24,8},{28,12},{1,17},{... | collective-permute-start | bytes 49160 | tf_op jit(solution)/shard_map/ppermute | solution.py:494
  21.1 0.4 %local_channels.1 = (f32[128,400]{1,0:T(8,128)S(1)}, f32[128,400]{1,0:T(8,128)S(1)}) custom-call(f32[128,400]{1,0:T(8,128)S(1)} %get-tuple-element.58.refs_0_, f32[128,400]{1,0:T(8,128)S(1)} %get-tuple-element.59.refs_1_, f32[128,128]{1,0:T(8,128)S(1)} %get-tuple-element.85.refs_2_, f32[128,128]{1,0:T(8,128)S(1)} %get-tuple-element.86.refs_3_, ...), custom_call_target="tpu_custom_call" | custom-call | flops 104857600 | bytes 1048576 | tf_op jit(solution)/shard_map/local_channels/pallas_call | solution.py:187
  21.5 1.7 %collective-permute-done.9.refs_15_ = bf16[16,512]{1,0:T(8,128)(2,1)S(1)} collective-permute-done((bf16[16,512]{1,0:T(8,128)(2,1)S(1)}, bf16[16,512]{1,0:T(8,128)(2,1)S(1)}, u32[]{:S(2)}, u32[]{:S(2)}) %collective-permute-start.9) | collective-permute-done | bytes 16416 | tf_op jit(solution)/shard_map/ppermute | solution.py:494
  23.2 0.9 %back_body.1 = (f32[32,1792]{1,0:T(8,128)S(1)}, bf16[32,1792]{1,0:T(8,128)(2,1)S(1)}, f32[32,128]{1,0:T(8,128)S(1)}, bf16[16,400]{1,0:T(8,128)(2,1)S(1)}, bf16[16,400]{1,0:T(8,128)(2,1)S(1)}) custom-call(f32[32,128]{1,0:T(8,128)S(1)} %local_vectors.1.refs_0_, f32[128,400]{1,0:T(8,128)S(1)} %get-tuple-element.93.refs_1_, ...), custom_call_target="tpu_custom_call" | custom-call | flops 163840000 | bytes 1048576 | tf_op jit(solution)/shard_map/back_body/pallas_call | solution.py:187
  24.2 1.3 %collective-permute-done.10.refs_1_ = bf16[32,1792]{1,0:T(8,128)(2,1)S(1)} collective-permute-done((bf16[32,1792]{1,0:T(8,128)(2,1)S(1)}, bf16[32,1792]{1,0:T(8,128)(2,1)S(1)}, u32[]{:S(2)}, u32[]{:S(2)}) %collective-permute-start.10) | collective-permute-done | bytes 114720 | tf_op jit(solution)/shard_map/ppermute | solution.py:494
  25.5 1.6 %collective-permute-start.11 = (bf16[32,1792]{1,0:T(8,128)(2,1)S(1)}, bf16[32,1792]{1,0:T(8,128)(2,1)S(1)}, u32[]{:S(2)}, u32[]{:S(2)}) collective-permute-start(bf16[32,1792]{1,0:T(8,128)(2,1)S(1)} %add.2), channel_id=1, source_target_pairs={{0,2},{1,3},{2,0},{3,1},{4,6},{5,7},{6,4},{7,5},{8,10},{9,11},{10,... | collective-permute-start | bytes 344072 | tf_op jit(solution)/shard_map/ppermute | solution.py:494
  27.1 0.8 %rest_body.1 = (f32[32,1792]{1,0:T(8,128)S(1)}, bf16[32,1792]{1,0:T(8,128)(2,1)S(1)}) custom-call(f32[32,128]{1,0:T(8,128)S(1)} %get-tuple-element.105.refs_0_, f32[128,400]{1,0:T(8,128)S(1)} %get-tuple-element.93.refs_1_, f32[128,400]{1,0:T(8,128)S(1)} %get-tuple-element.94.refs_2_, f32[128,400]{1,0:T(8,128)S(1)} %get-tuple-element.83.refs_3_, ...), custom_call_target="tpu_custom_call" | custom-call | flops 163840000 | bytes 1048576 | tf_op jit(solution)/shard_map/rest_body/pallas_call | solution.py:187
  27.9 2.9 %collective-permute-done.11.refs_1_ = bf16[32,1792]{1,0:T(8,128)(2,1)S(1)} collective-permute-done((bf16[32,1792]{1,0:T(8,128)(2,1)S(1)}, bf16[32,1792]{1,0:T(8,128)(2,1)S(1)}, u32[]{:S(2)}, u32[]{:S(2)}) %collective-permute-start.11) | collective-permute-done | bytes 114720 | tf_op jit(solution)/shard_map/ppermute | solution.py:494
  30.8 0.7 %total.1 = (bf16[32,1600]{1,0:T(8,128)(2,1)}, f32[16,128]{1,0:T(8,128)}, f32[16,128]{1,0:T(8,128)}) custom-call(f32[32,1792]{1,0:T(8,128)S(1)} %add.3.refs_0_, bf16[32,1792]{1,0:T(8,128)(2,1)S(1)} %collective-permute-done.12.refs_1_), custom_call_target="tpu_custom_call" | custom-call | bytes 1048576 | tf_op jit(solution)/shard_map/total/pallas_call | solution.py:187
  (18 shorter events, 0.7 us)
Async XLA Ops:
  0.6 7.0 %collective-permute-start = (bf16[32,1600]{1,0:T(8,128)(2,1)}, bf16[32,1600]{1,0:T(8,128)(2,1)S(1)}, u32[]{:S(2)}, u32[]{:S(2)}) collective-permute-start(bf16[32,1600]{1,0:T(8,128)(2,1)} %refs_7_.1), channel_id=1, source_target_pairs={{0,2},{1,3},{2,0},{3,1},{4,6},{5,7},{6,4},{7,5},{8,10},{9,11},{10,... | collective-permute-start | bytes 307208 | tf_op jit(solution)/shard_map/ppermute | solution.py:494
  3.6 5.5 %collective-permute-start.3 = (bf16[32,1600]{1,0:T(8,128)(2,1)}, bf16[32,1600]{1,0:T(8,128)(2,1)S(1)}, u32[]{:S(2)}, u32[]{:S(2)}) collective-permute-start(bf16[32,1600]{1,0:T(8,128)(2,1)} %refs_8_.1), channel_id=1, source_target_pairs={{0,2},{1,3},{2,0},{3,1},{4,6},{5,7},{6,4},{7,5},{8,10},{9,11},{10,... | collective-permute-start | bytes 307208 | tf_op jit(solution)/shard_map/ppermute | solution.py:494
  3.7 2.3 %copy-start = (bf16[32,1600]{1,0:T(8,128)(2,1)S(1)}, bf16[32,1600]{1,0:T(8,128)(2,1)}, u32[]{:S(2)}) copy-start(bf16[32,1600]{1,0:T(8,128)(2,1)} %refs_7_.1) | copy-start | bytes 307204
  3.7 3.9 %copy-start.1 = (bf16[32,1600]{1,0:T(8,128)(2,1)S(1)}, bf16[32,1600]{1,0:T(8,128)(2,1)}, u32[]{:S(2)}) copy-start(bf16[32,1600]{1,0:T(8,128)(2,1)} %refs_8_.1) | copy-start | bytes 307204
  6.1 3.0 %collective-permute-start.1 = (bf16[32,1600]{1,0:T(8,128)(2,1)S(1)}, bf16[32,1600]{1,0:T(8,128)(2,1)S(1)}, u32[]{:S(2)}, u32[]{:S(2)}) collective-permute-start(bf16[32,1600]{1,0:T(8,128)(2,1)S(1)} %copy-done), channel_id=1, source_target_pairs={{0,1},{1,0},{2,3},{3,2},{4,5},{5,4},{6,7},{7,6},{8,9},{9,8},{10,11... | collective-permute-start | bytes 307208 | tf_op jit(solution)/shard_map/ppermute | solution.py:494
  7.6 1.5 %collective-permute-start.2 = (bf16[32,1600]{1,0:T(8,128)(2,1)S(1)}, bf16[32,1600]{1,0:T(8,128)(2,1)S(1)}, u32[]{:S(2)}, u32[]{:S(2)}) collective-permute-start(bf16[32,1600]{1,0:T(8,128)(2,1)S(1)} %collective-permute-done.refs_1_), channel_id=1, source_target_pairs={{0,1},{1,0},{2,3},{3,2},{4,5},{5,4},{6,7},{7,6},{8,9},{9,8},{10,11... | collective-permute-start | bytes 307208 | tf_op jit(solution)/shard_map/ppermute | solution.py:494
  7.6 2.6 %collective-permute-start.4 = (bf16[32,1600]{1,0:T(8,128)(2,1)S(1)}, bf16[32,1600]{1,0:T(8,128)(2,1)S(1)}, u32[]{:S(2)}, u32[]{:S(2)}) collective-permute-start(bf16[32,1600]{1,0:T(8,128)(2,1)S(1)} %copy-done.1), channel_id=1, source_target_pairs={{0,1},{1,0},{2,3},{3,2},{4,5},{5,4},{6,7},{7,6},{8,9},{9,8},{10,11... | collective-permute-start | bytes 307208 | tf_op jit(solution)/shard_map/ppermute | solution.py:494
  9.1 1.3 %collective-permute-start.5 = (bf16[32,1600]{1,0:T(8,128)(2,1)S(1)}, bf16[32,1600]{1,0:T(8,128)(2,1)S(1)}, u32[]{:S(2)}, u32[]{:S(2)}) collective-permute-start(bf16[32,1600]{1,0:T(8,128)(2,1)S(1)} %collective-permute-done.3.refs_1_), channel_id=1, source_target_pairs={{0,1},{1,0},{2,3},{3,2},{4,5},{5,4},{6,7},{7,6},{8,9},{9,8},{10,11... | collective-permute-start | bytes 307208 | tf_op jit(solution)/shard_map/ppermute | solution.py:494
  11.1 4.8 %collective-permute-start.8 = (bf16[32,512]{1,0:T(8,128)(2,1)S(1)}, bf16[32,512]{1,0:T(8,128)(2,1)S(1)}, u32[]{:S(2)}, u32[]{:S(2)}) collective-permute-start(bf16[32,512]{1,0:T(8,128)(2,1)S(1)} %get-tuple-element.89), channel_id=1, source_target_pairs={{0,12},{4,8},{8,4},{12,0},{16,28},{20,24},{24,20},{28,16},{1,13},{... | collective-permute-start | bytes 98312 | tf_op jit(solution)/shard_map/ppermute | solution.py:494
  13.9 3.9 %collective-permute-start.7 = (bf16[32,512]{1,0:T(8,128)(2,1)S(1)}, bf16[32,512]{1,0:T(8,128)(2,1)S(1)}, u32[]{:S(2)}, u32[]{:S(2)}) collective-permute-start(bf16[32,512]{1,0:T(8,128)(2,1)S(1)} %get-tuple-element.89), channel_id=1, source_target_pairs={{0,8},{4,12},{8,0},{12,4},{16,24},{20,28},{24,16},{28,20},{1,9},{5... | collective-permute-start | bytes 98312 | tf_op jit(solution)/shard_map/ppermute | solution.py:494
  14.4 3.9 %collective-permute-start.6 = (bf16[32,512]{1,0:T(8,128)(2,1)S(1)}, bf16[32,512]{1,0:T(8,128)(2,1)S(1)}, u32[]{:S(2)}, u32[]{:S(2)}) collective-permute-start(bf16[32,512]{1,0:T(8,128)(2,1)S(1)} %get-tuple-element.89), channel_id=1, source_target_pairs={{0,4},{4,0},{8,12},{12,8},{16,20},{20,16},{24,28},{28,24},{1,5},{5... | collective-permute-start | bytes 98312 | tf_op jit(solution)/shard_map/ppermute | solution.py:494
  18.5 4.7 %collective-permute-start.9 = (bf16[16,512]{1,0:T(8,128)(2,1)S(1)}, bf16[16,512]{1,0:T(8,128)(2,1)S(1)}, u32[]{:S(2)}, u32[]{:S(2)}) collective-permute-start(bf16[16,512]{1,0:T(8,128)(2,1)S(1)} %get-tuple-element.101), channel_id=1, source_target_pairs={{0,16},{4,20},{8,24},{12,28},{16,0},{20,4},{24,8},{28,12},{1,17},{... | collective-permute-start | bytes 49160 | tf_op jit(solution)/shard_map/ppermute | solution.py:494
  24.1 1.4 %collective-permute-start.10 = (bf16[32,1792]{1,0:T(8,128)(2,1)S(1)}, bf16[32,1792]{1,0:T(8,128)(2,1)S(1)}, u32[]{:S(2)}, u32[]{:S(2)}) collective-permute-start(bf16[32,1792]{1,0:T(8,128)(2,1)S(1)} %get-tuple-element.108), channel_id=1, source_target_pairs={{0,1},{1,0},{2,3},{3,2},{4,5},{5,4},{6,7},{7,6},{8,9},{9,8},{10,11... | collective-permute-start | bytes 344072 | tf_op jit(solution)/shard_map/ppermute | solution.py:494
  25.5 5.3 %collective-permute-start.11 = (bf16[32,1792]{1,0:T(8,128)(2,1)S(1)}, bf16[32,1792]{1,0:T(8,128)(2,1)S(1)}, u32[]{:S(2)}, u32[]{:S(2)}) collective-permute-start(bf16[32,1792]{1,0:T(8,128)(2,1)S(1)} %add.2), channel_id=1, source_target_pairs={{0,2},{1,3},{2,0},{3,1},{4,6},{5,7},{6,4},{7,5},{8,10},{9,11},{10,... | collective-permute-start | bytes 344072 | tf_op jit(solution)/shard_map/ppermute | solution.py:494
  27.8 3.0 %collective-permute-start.12 = (bf16[32,1792]{1,0:T(8,128)(2,1)S(1)}, bf16[32,1792]{1,0:T(8,128)(2,1)S(1)}, u32[]{:S(2)}, u32[]{:S(2)}) collective-permute-start(bf16[32,1792]{1,0:T(8,128)(2,1)S(1)} %get-tuple-element.112), channel_id=1, source_target_pairs={{0,1},{1,0},{2,3},{3,2},{4,5},{5,4},{6,7},{7,6},{8,9},{9,8},{10,11... | collective-permute-start | bytes 344072 | tf_op jit(solution)/shard_map/ppermute | solution.py:494

commit v5 on v4

--- a/solution.py
+++ b/solution.py
@@ -498,12 +498,12 @@
         return staged_call(body, ins, outs, **options)
 
     far_ins = dict(
-        log=log_decay, doc=doc_start.reshape(1, tokens), b_in=b_proj, c_in=c_proj, w_gate=w_gate,
+        doc=doc_start.reshape(1, tokens), b_in=b_proj, c_in=c_proj, w_gate=w_gate,
         w_in=w_in, w_out=w_out, rows0=layer_input, grad0=out_grad, entry=entry_state,
         skip=d_skip.reshape(1, channels),
     )
     ready = call(
-        prepare, {name: far(value) for name, value in far_ins.items()},
+        prepare, dict(log=log_decay, **{name: far(value) for name, value in far_ins.items()}),
         dict(enter=wide, leave=wide, rise=wide, fall=wide, factor=summary,
              expander=near((width - channels // LANE * LANE, width), BF16), causal=square,
              crossed=square, crossed_back=square, b=row, c=row, b_columns=column, c_columns=column),

time: 31.7 us -> 31.7 us (level)
  waiting for transfers between devices: 11.5 us -> 10.8 us
  local copies, waits for them, and re-layouts: 0.01 us -> 0.7 us
    unnamed x4 -> x6, local copies, waits for them, and re-layouts: 0.01 us -> 0.7 us
    ppermute x13, waiting for transfers between devices: 11.5 us -> 10.8 us  [swap(): return lax.ppermute(value, axis, [(at, at ^ bit) for at in range(size)])]
where the time goes in v5:
time: 31.7 us; the launch traced here: 31.5 us
  starting transfers between devices  11.5 us (36%)
  waiting for transfers between devices  10.8 us (34%)
  Pallas kernels  7.71 us (24%)
  between operations  0.75 us (2%)
  local copies, waits for them, and re-layouts  0.7 us (2%)
    ppermute x13, starting transfers between devices, swap(): return lax.ppermute(value, axis, [(at, at ^ bit) for at in range(size)])  11.5 us
    ppermute x13, waiting for transfers between devices, swap(): return lax.ppermute(value, axis, [(at, at ^ bit) for at in range(size)])  10.8 us
    pallas_call x12, Pallas kernels, staged_call(): pl.pallas_call(kernel, name=body.__name__, out_shape=[jax.ShapeDtypeStruc...  7.71 us
    unnamed x6, local copies, waits for them, and re-layouts  0.7 us
  transfers between devices with their start and end apart: 13, of which 9 were waited for; matrix products, arithmetic and copies ran while one was open for 0% of the time, Pallas kernels for 17%

profile of v5, /device:TPU:0, one launch (start us, length us, event | category | flops | bytes accessed | tf_op | source)
XLA Modules:
  0.0 31.5 jit_solution(5210376692535315473)
XLA Ops:
  0.6 3.0 %collective-permute-start = (bf16[32,1600]{1,0:T(8,128)(2,1)}, bf16[32,1600]{1,0:T(8,128)(2,1)S(1)}, u32[]{:S(2)}, u32[]{:S(2)}) collective-permute-start(bf16[32,1600]{1,0:T(8,128)(2,1)} %refs_7_.1), channel_id=1, source_target_pairs={{0,2},{1,3},{2,0},{3,1},{4,6},{5,7},{6,4},{7,5},{8,10},{9,11},{10,... | collective-permute-start | bytes 307208 | tf_op jit(solution)/shard_map/ppermute | solution.py:494
  3.7 0.7 %copy-done = bf16[25,128]{1,0:T(8,128)(2,1)S(1)} copy-done((bf16[25,128]{1,0:T(8,128)(2,1)S(1)}, bf16[25,128]{1,0:T(8,128)(2,1)}, u32[]{:S(2)}) %copy-start) | copy-done | bytes 6424
  4.4 2.3 %prepare.1 = (f32[128,400]{1,0:T(8,128)S(1)}, f32[128,400]{1,0:T(8,128)S(1)}, f32[128,400]{1,0:T(8,128)S(1)}, f32[128,400]{1,0:T(8,128)S(1)}, f32[16,512]{1,0:T(...) custom-call(bf16[25,128]{1,0:T(8,128)(2,1)S(1)} %copy-done, ...), custom_call_target="tpu_custom_call" | custom-call | flops 52428800 | bytes 1048576 | tf_op jit(solution)/shard_map/prepare/pallas_call | solution.py:187
  6.8 0.8 %collective-permute-done.refs_1_ = bf16[32,1600]{1,0:T(8,128)(2,1)S(1)} collective-permute-done((bf16[32,1600]{1,0:T(8,128)(2,1)}, bf16[32,1600]{1,0:T(8,128)(2,1)S(1)}, u32[]{:S(2)}, u32[]{:S(2)}) %collective-permute-start) | collective-permute-done | bytes 102432 | tf_op jit(solution)/shard_map/ppermute | solution.py:494
  7.6 0.5 %collective-permute-start.4 = (bf16[32,1600]{1,0:T(8,128)(2,1)S(1)}, bf16[32,1600]{1,0:T(8,128)(2,1)S(1)}, u32[]{:S(2)}, u32[]{:S(2)}) collective-permute-start(bf16[32,1600]{1,0:T(8,128)(2,1)S(1)} %copy-done.2), channel_id=1, source_target_pairs={{0,1},{1,0},{2,3},{3,2},{4,5},{5,4},{6,7},{7,6},{8,9},{9,8},{10,11... | collective-permute-start | bytes 307208 | tf_op jit(solution)/shard_map/ppermute | solution.py:494
  8.1 1.0 %collective-permute-done.3.refs_1_ = bf16[32,1600]{1,0:T(8,128)(2,1)S(1)} collective-permute-done((bf16[32,1600]{1,0:T(8,128)(2,1)}, bf16[32,1600]{1,0:T(8,128)(2,1)S(1)}, u32[]{:S(2)}, u32[]{:S(2)}) %collective-permute-start.3) | collective-permute-done | bytes 102432 | tf_op jit(solution)/shard_map/ppermute | solution.py:494
  9.1 1.1 %project.1 = (f32[128,400]{1,0:T(8,128)S(1)}, f32[128,400]{1,0:T(8,128)S(1)}, f32[128,400]{1,0:T(8,128)S(1)}, bf16[128,400]{1,0:T(8,128)(2,1)S(1)}, bf16[128,400]{1,0:T(8,128)(2,1)S(1)}, /*index=5*/f32[16,512]{1,0:T(8,128)S(1)}) custom-call(bf16[32,1600]{1,0:T(8,128)(2,1)S(1)} %get-tuple-element.63.refs_0_, ...), custom_call_target="tpu_custom_call" | custom-call | flops 327680000 | bytes 1048576 | tf_op jit(solution)/shard_map/project/pallas_call | solution.py:187
  10.4 0.7 %front.1 = (f32[128,400]{1,0:T(8,128)S(1)}, bf16[128,400]{1,0:T(8,128)(2,1)S(1)}, bf16[128,400]{1,0:T(8,128)(2,1)S(1)}, f32[16,512]{1,0:T(8,128)S(1)}, bf16[32,512]{1,0:T(8,128)(2,1)S(1)}) custom-call(bf16[32,1600]{1,0:T(8,128)(2,1)S(1)} %get-tuple-element.71.refs_0_, bf16[32,1600]{1,0:T(8,128)(2,1)S(1)} %collective-permute-done.3.refs_1_, ...), custom_call_target="tpu_custom_call" | custom-call | flops 163840000 | bytes 1048576 | tf_op jit(solution)/shard_map/front/pallas_call | solution.py:187
  11.1 2.8 %collective-permute-start.8 = (bf16[32,512]{1,0:T(8,128)(2,1)S(1)}, bf16[32,512]{1,0:T(8,128)(2,1)S(1)}, u32[]{:S(2)}, u32[]{:S(2)}) collective-permute-start(bf16[32,512]{1,0:T(8,128)(2,1)S(1)} %get-tuple-element.89), channel_id=1, source_target_pairs={{0,12},{4,8},{8,4},{12,0},{16,28},{20,24},{24,20},{28,16},{1,13},{... | collective-permute-start | bytes 98312 | tf_op jit(solution)/shard_map/ppermute | solution.py:494
  13.9 0.5 %collective-permute-start.7 = (bf16[32,512]{1,0:T(8,128)(2,1)S(1)}, bf16[32,512]{1,0:T(8,128)(2,1)S(1)}, u32[]{:S(2)}, u32[]{:S(2)}) collective-permute-start(bf16[32,512]{1,0:T(8,128)(2,1)S(1)} %get-tuple-element.89), channel_id=1, source_target_pairs={{0,8},{4,12},{8,0},{12,4},{16,24},{20,28},{24,16},{28,20},{1,9},{5... | collective-permute-start | bytes 98312 | tf_op jit(solution)/shard_map/ppermute | solution.py:494
  14.4 0.3 collective-permute-start.6
  14.8 0.5 %local_vectors.1.refs_0_ = f32[32,128]{1,0:T(8,128)S(1)} custom-call(f32[128,400]{1,0:T(8,128)S(1)} %get-tuple-element.58.refs_0_, f32[128,400]{1,0:T(8,128)S(1)} %get-tuple-element.59.refs_1_, f32[128,128]{1,0:T(8,128)S(1)} %get-tuple-element.60.refs_2_, bf16[16,128]{1,0:T(8,128)(2,1)S(1)} %get-tuple-element.61.refs_6_.refs_3_, ...), custom_call_target="tpu_custom_call" | custom-call | flops 52428800 | bytes 1048576 | tf_op jit(solution)/shard_map/local_vectors/pallas_call | solution.py:187
  15.3 0.7 %collective-permute-done.8.refs_6_ = bf16[32,512]{1,0:T(8,128)(2,1)S(1)} collective-permute-done((bf16[32,512]{1,0:T(8,128)(2,1)S(1)}, bf16[32,512]{1,0:T(8,128)(2,1)S(1)}, u32[]{:S(2)}, u32[]{:S(2)}) %collective-permute-start.8) | collective-permute-done | bytes 32800 | tf_op jit(solution)/shard_map/ppermute | solution.py:494
  15.9 1.9 %collective-permute-done.7.refs_5_ = bf16[32,512]{1,0:T(8,128)(2,1)S(1)} collective-permute-done((bf16[32,512]{1,0:T(8,128)(2,1)S(1)}, bf16[32,512]{1,0:T(8,128)(2,1)S(1)}, u32[]{:S(2)}, u32[]{:S(2)}) %collective-permute-start.7) | collective-permute-done | bytes 32800 | tf_op jit(solution)/shard_map/ppermute | solution.py:494
  17.8 0.5 %collective-permute-done.6.refs_4_ = bf16[32,512]{1,0:T(8,128)(2,1)S(1)} collective-permute-done((bf16[32,512]{1,0:T(8,128)(2,1)S(1)}, bf16[32,512]{1,0:T(8,128)(2,1)S(1)}, u32[]{:S(2)}, u32[]{:S(2)}) %collective-permute-start.6) | collective-permute-done | bytes 32800 | tf_op jit(solution)/shard_map/ppermute | solution.py:494
  18.5 2.7 %collective-permute-start.9 = (bf16[16,512]{1,0:T(8,128)(2,1)S(1)}, bf16[16,512]{1,0:T(8,128)(2,1)S(1)}, u32[]{:S(2)}, u32[]{:S(2)}) collective-permute-start(bf16[16,512]{1,0:T(8,128)(2,1)S(1)} %get-tuple-element.101), channel_id=1, source_target_pairs={{0,16},{4,20},{8,24},{12,28},{16,0},{20,4},{24,8},{28,12},{1,17},{... | collective-permute-start | bytes 49160 | tf_op jit(solution)/shard_map/ppermute | solution.py:494
  21.1 0.4 %local_channels.1 = (f32[128,400]{1,0:T(8,128)S(1)}, f32[128,400]{1,0:T(8,128)S(1)}) custom-call(f32[128,400]{1,0:T(8,128)S(1)} %get-tuple-element.58.refs_0_, f32[128,400]{1,0:T(8,128)S(1)} %get-tuple-element.59.refs_1_, f32[128,128]{1,0:T(8,128)S(1)} %get-tuple-element.85.refs_2_, f32[128,128]{1,0:T(8,128)S(1)} %get-tuple-element.86.refs_3_, ...), custom_call_target="tpu_custom_call" | custom-call | flops 104857600 | bytes 1048576 | tf_op jit(solution)/shard_map/local_channels/pallas_call | solution.py:187
  21.5 1.7 %collective-permute-done.9.refs_15_ = bf16[16,512]{1,0:T(8,128)(2,1)S(1)} collective-permute-done((bf16[16,512]{1,0:T(8,128)(2,1)S(1)}, bf16[16,512]{1,0:T(8,128)(2,1)S(1)}, u32[]{:S(2)}, u32[]{:S(2)}) %collective-permute-start.9) | collective-permute-done | bytes 16416 | tf_op jit(solution)/shard_map/ppermute | solution.py:494
  23.2 0.9 %back_body.1 = (f32[32,1792]{1,0:T(8,128)S(1)}, bf16[32,1792]{1,0:T(8,128)(2,1)S(1)}, f32[32,128]{1,0:T(8,128)S(1)}, bf16[16,400]{1,0:T(8,128)(2,1)S(1)}, bf16[16,400]{1,0:T(8,128)(2,1)S(1)}) custom-call(f32[32,128]{1,0:T(8,128)S(1)} %local_vectors.1.refs_0_, f32[128,400]{1,0:T(8,128)S(1)} %get-tuple-element.93.refs_1_, ...), custom_call_target="tpu_custom_call" | custom-call | flops 163840000 | bytes 1048576 | tf_op jit(solution)/shard_map/back_body/pallas_call | solution.py:187
  24.2 1.3 %collective-permute-done.10.refs_1_ = bf16[32,1792]{1,0:T(8,128)(2,1)S(1)} collective-permute-done((bf16[32,1792]{1,0:T(8,128)(2,1)S(1)}, bf16[32,1792]{1,0:T(8,128)(2,1)S(1)}, u32[]{:S(2)}, u32[]{:S(2)}) %collective-permute-start.10) | collective-permute-done | bytes 114720 | tf_op jit(solution)/shard_map/ppermute | solution.py:494
  25.5 1.6 %collective-permute-start.11 = (bf16[32,1792]{1,0:T(8,128)(2,1)S(1)}, bf16[32,1792]{1,0:T(8,128)(2,1)S(1)}, u32[]{:S(2)}, u32[]{:S(2)}) collective-permute-start(bf16[32,1792]{1,0:T(8,128)(2,1)S(1)} %add.2), channel_id=1, source_target_pairs={{0,2},{1,3},{2,0},{3,1},{4,6},{5,7},{6,4},{7,5},{8,10},{9,11},{10,... | collective-permute-start | bytes 344072 | tf_op jit(solution)/shard_map/ppermute | solution.py:494
  27.1 0.8 %rest_body.1 = (f32[32,1792]{1,0:T(8,128)S(1)}, bf16[32,1792]{1,0:T(8,128)(2,1)S(1)}) custom-call(f32[32,128]{1,0:T(8,128)S(1)} %get-tuple-element.105.refs_0_, f32[128,400]{1,0:T(8,128)S(1)} %get-tuple-element.93.refs_1_, f32[128,400]{1,0:T(8,128)S(1)} %get-tuple-element.94.refs_2_, f32[128,400]{1,0:T(8,128)S(1)} %get-tuple-element.83.refs_3_, ...), custom_call_target="tpu_custom_call" | custom-call | flops 163840000 | bytes 1048576 | tf_op jit(solution)/shard_map/rest_body/pallas_call | solution.py:187
  27.9 2.9 %collective-permute-done.11.refs_1_ = bf16[32,1792]{1,0:T(8,128)(2,1)S(1)} collective-permute-done((bf16[32,1792]{1,0:T(8,128)(2,1)S(1)}, bf16[32,1792]{1,0:T(8,128)(2,1)S(1)}, u32[]{:S(2)}, u32[]{:S(2)}) %collective-permute-start.11) | collective-permute-done | bytes 114720 | tf_op jit(solution)/shard_map/ppermute | solution.py:494
  30.8 0.7 %total.1 = (bf16[32,1600]{1,0:T(8,128)(2,1)}, f32[16,128]{1,0:T(8,128)}, f32[16,128]{1,0:T(8,128)}) custom-call(f32[32,1792]{1,0:T(8,128)S(1)} %add.3.refs_0_, bf16[32,1792]{1,0:T(8,128)(2,1)S(1)} %collective-permute-done.12.refs_1_), custom_call_target="tpu_custom_call" | custom-call | bytes 1048576 | tf_op jit(solution)/shard_map/total/pallas_call | solution.py:187
  (20 shorter events, 0.9 us)
Async XLA Ops:
  0.6 7.0 %collective-permute-start = (bf16[32,1600]{1,0:T(8,128)(2,1)}, bf16[32,1600]{1,0:T(8,128)(2,1)S(1)}, u32[]{:S(2)}, u32[]{:S(2)}) collective-permute-start(bf16[32,1600]{1,0:T(8,128)(2,1)} %refs_7_.1), channel_id=1, source_target_pairs={{0,2},{1,3},{2,0},{3,1},{4,6},{5,7},{6,4},{7,5},{8,10},{9,11},{10,... | collective-permute-start | bytes 307208 | tf_op jit(solution)/shard_map/ppermute | solution.py:494
  3.6 5.5 %collective-permute-start.3 = (bf16[32,1600]{1,0:T(8,128)(2,1)}, bf16[32,1600]{1,0:T(8,128)(2,1)S(1)}, u32[]{:S(2)}, u32[]{:S(2)}) collective-permute-start(bf16[32,1600]{1,0:T(8,128)(2,1)} %refs_8_.1), channel_id=1, source_target_pairs={{0,2},{1,3},{2,0},{3,1},{4,6},{5,7},{6,4},{7,5},{8,10},{9,11},{10,... | collective-permute-start | bytes 307208 | tf_op jit(solution)/shard_map/ppermute | solution.py:494
  3.7 0.7 %copy-start = (bf16[25,128]{1,0:T(8,128)(2,1)S(1)}, bf16[25,128]{1,0:T(8,128)(2,1)}, u32[]{:S(2)}) copy-start(bf16[25,128]{1,0:T(8,128)(2,1)} %refs_0_.1) | copy-start | bytes 19204
  4.4 2.3 %copy-start.1 = (bf16[32,1600]{1,0:T(8,128)(2,1)S(1)}, bf16[32,1600]{1,0:T(8,128)(2,1)}, u32[]{:S(2)}) copy-start(bf16[32,1600]{1,0:T(8,128)(2,1)} %refs_7_.1) | copy-start | bytes 307204
  4.4 3.2 %copy-start.2 = (bf16[32,1600]{1,0:T(8,128)(2,1)S(1)}, bf16[32,1600]{1,0:T(8,128)(2,1)}, u32[]{:S(2)}) copy-start(bf16[32,1600]{1,0:T(8,128)(2,1)} %refs_8_.1) | copy-start | bytes 307204
  6.7 2.4 %collective-permute-start.1 = (bf16[32,1600]{1,0:T(8,128)(2,1)S(1)}, bf16[32,1600]{1,0:T(8,128)(2,1)S(1)}, u32[]{:S(2)}, u32[]{:S(2)}) collective-permute-start(bf16[32,1600]{1,0:T(8,128)(2,1)S(1)} %copy-done.1), channel_id=1, source_target_pairs={{0,1},{1,0},{2,3},{3,2},{4,5},{5,4},{6,7},{7,6},{8,9},{9,8},{10,11... | collective-permute-start | bytes 307208 | tf_op jit(solution)/shard_map/ppermute | solution.py:494
  7.6 1.5 %collective-permute-start.2 = (bf16[32,1600]{1,0:T(8,128)(2,1)S(1)}, bf16[32,1600]{1,0:T(8,128)(2,1)S(1)}, u32[]{:S(2)}, u32[]{:S(2)}) collective-permute-start(bf16[32,1600]{1,0:T(8,128)(2,1)S(1)} %collective-permute-done.refs_1_), channel_id=1, source_target_pairs={{0,1},{1,0},{2,3},{3,2},{4,5},{5,4},{6,7},{7,6},{8,9},{9,8},{10,11... | collective-permute-start | bytes 307208 | tf_op jit(solution)/shard_map/ppermute | solution.py:494
  7.6 2.6 %collective-permute-start.4 = (bf16[32,1600]{1,0:T(8,128)(2,1)S(1)}, bf16[32,1600]{1,0:T(8,128)(2,1)S(1)}, u32[]{:S(2)}, u32[]{:S(2)}) collective-permute-start(bf16[32,1600]{1,0:T(8,128)(2,1)S(1)} %copy-done.2), channel_id=1, source_target_pairs={{0,1},{1,0},{2,3},{3,2},{4,5},{5,4},{6,7},{7,6},{8,9},{9,8},{10,11... | collective-permute-start | bytes 307208 | tf_op jit(solution)/shard_map/ppermute | solution.py:494
  9.1 1.3 %collective-permute-start.5 = (bf16[32,1600]{1,0:T(8,128)(2,1)S(1)}, bf16[32,1600]{1,0:T(8,128)(2,1)S(1)}, u32[]{:S(2)}, u32[]{:S(2)}) collective-permute-start(bf16[32,1600]{1,0:T(8,128)(2,1)S(1)} %collective-permute-done.3.refs_1_), channel_id=1, source_target_pairs={{0,1},{1,0},{2,3},{3,2},{4,5},{5,4},{6,7},{7,6},{8,9},{9,8},{10,11... | collective-permute-start | bytes 307208 | tf_op jit(solution)/shard_map/ppermute | solution.py:494
  11.1 4.8 %collective-permute-start.8 = (bf16[32,512]{1,0:T(8,128)(2,1)S(1)}, bf16[32,512]{1,0:T(8,128)(2,1)S(1)}, u32[]{:S(2)}, u32[]{:S(2)}) collective-permute-start(bf16[32,512]{1,0:T(8,128)(2,1)S(1)} %get-tuple-element.89), channel_id=1, source_target_pairs={{0,12},{4,8},{8,4},{12,0},{16,28},{20,24},{24,20},{28,16},{1,13},{... | collective-permute-start | bytes 98312 | tf_op jit(solution)/shard_map/ppermute | solution.py:494
  13.9 3.9 %collective-permute-start.7 = (bf16[32,512]{1,0:T(8,128)(2,1)S(1)}, bf16[32,512]{1,0:T(8,128)(2,1)S(1)}, u32[]{:S(2)}, u32[]{:S(2)}) collective-permute-start(bf16[32,512]{1,0:T(8,128)(2,1)S(1)} %get-tuple-element.89), channel_id=1, source_target_pairs={{0,8},{4,12},{8,0},{12,4},{16,24},{20,28},{24,16},{28,20},{1,9},{5... | collective-permute-start | bytes 98312 | tf_op jit(solution)/shard_map/ppermute | solution.py:494
  14.4 3.9 %collective-permute-start.6 = (bf16[32,512]{1,0:T(8,128)(2,1)S(1)}, bf16[32,512]{1,0:T(8,128)(2,1)S(1)}, u32[]{:S(2)}, u32[]{:S(2)}) collective-permute-start(bf16[32,512]{1,0:T(8,128)(2,1)S(1)} %get-tuple-element.89), channel_id=1, source_target_pairs={{0,4},{4,0},{8,12},{12,8},{16,20},{20,16},{24,28},{28,24},{1,5},{5... | collective-permute-start | bytes 98312 | tf_op jit(solution)/shard_map/ppermute | solution.py:494
  18.5 4.7 %collective-permute-start.9 = (bf16[16,512]{1,0:T(8,128)(2,1)S(1)}, bf16[16,512]{1,0:T(8,128)(2,1)S(1)}, u32[]{:S(2)}, u32[]{:S(2)}) collective-permute-start(bf16[16,512]{1,0:T(8,128)(2,1)S(1)} %get-tuple-element.101), channel_id=1, source_target_pairs={{0,16},{4,20},{8,24},{12,28},{16,0},{20,4},{24,8},{28,12},{1,17},{... | collective-permute-start | bytes 49160 | tf_op jit(solution)/shard_map/ppermute | solution.py:494
  24.1 1.4 %collective-permute-start.10 = (bf16[32,1792]{1,0:T(8,128)(2,1)S(1)}, bf16[32,1792]{1,0:T(8,128)(2,1)S(1)}, u32[]{:S(2)}, u32[]{:S(2)}) collective-permute-start(bf16[32,1792]{1,0:T(8,128)(2,1)S(1)} %get-tuple-element.108), channel_id=1, source_target_pairs={{0,1},{1,0},{2,3},{3,2},{4,5},{5,4},{6,7},{7,6},{8,9},{9,8},{10,11... | collective-permute-start | bytes 344072 | tf_op jit(solution)/shard_map/ppermute | solution.py:494
  25.5 5.3 %collective-permute-start.11 = (bf16[32,1792]{1,0:T(8,128)(2,1)S(1)}, bf16[32,1792]{1,0:T(8,128)(2,1)S(1)}, u32[]{:S(2)}, u32[]{:S(2)}) collective-permute-start(bf16[32,1792]{1,0:T(8,128)(2,1)S(1)} %add.2), channel_id=1, source_target_pairs={{0,2},{1,3},{2,0},{3,1},{4,6},{5,7},{6,4},{7,5},{8,10},{9,11},{10,... | collective-permute-start | bytes 344072 | tf_op jit(solution)/shard_map/ppermute | solution.py:494
  27.8 3.0 %collective-permute-start.12 = (bf16[32,1792]{1,0:T(8,128)(2,1)S(1)}, bf16[32,1792]{1,0:T(8,128)(2,1)S(1)}, u32[]{:S(2)}, u32[]{:S(2)}) collective-permute-start(bf16[32,1792]{1,0:T(8,128)(2,1)S(1)} %get-tuple-element.112), channel_id=1, source_target_pairs={{0,1},{1,0},{2,3},{3,2},{4,5},{5,4},{6,7},{7,6},{8,9},{9,8},{10,11... | collective-permute-start | bytes 344072 | tf_op jit(solution)/shard_map/ppermute | solution.py:494

commit v6 on v5

--- a/solution.py
+++ b/solution.py
@@ -197,12 +197,16 @@
     return Values(zip(outs, results))
 
 
-def assemble(staged, name, whole):
-    for step in range(whole.shape[0] // staged.refs[name + "0"].shape[0]):
-        block = staged.take(name + "%d" % step)
-        piece = block.shape[0]
+def arrived_rows(staged, name, count):
+    return jnp.concatenate([staged.take(name + "%d" % step)[...] for step in range(count)], axis=0)
+
+
+def in_token_order(made, values, count):
+    piece = values.shape[0] // count
+    for step in range(count):
         start = pl.multiple_of((lax.axis_index(TP) ^ step) * piece, piece)
-        whole[pl.ds(start, piece), :] = block[...]
+        made[pl.ds(start, piece), :] = values[step * piece : (step + 1) * piece, :]
+    return made[...]
 
 
 def head_expander(channels, width):
@@ -279,26 +283,24 @@
     part[:, : values.shape[1]] = dot(staged.take(vectors)[...], values)
 
 
-def project(staged, rows_ref):
-    assemble(staged, "rows", rows_ref)
-    rows = rows_ref[...]
-    pre = dot(rows, staged.w_in[...], NT)
-    staged.put(pre=pre)
+def project(staged):
+    parts = lax.axis_size(TP)
+    rows = arrived_rows(staged, "rows", parts)
+    pre = in_token_order(staged.made.pre, dot(rows, staged.w_in[...], NT), parts)
     x_rows = (pre * jax.nn.sigmoid(pre)).astype(BF16)
     staged.put(x=x_rows)
     leaving = (x_rows.astype(F32) * staged.leave[...]).astype(BF16)
     staged.put(leaving=leaving)
     put_summary(staged, "state", "b", leaving)
-    gate = dot(rows, staged.w_gate[...], NT)
-    staged.put(gate=gate)
+    gate = in_token_order(staged.made.gate, dot(rows, staged.w_gate[...], NT), parts)
     staged.put(gated=gate * jax.nn.sigmoid(gate))
 
 
-def front(staged, grad_ref):
+def front(staged):
     channels = staged.made.mix.shape[1]
-    assemble(staged, "grad", grad_ref)
-    mix = dot(grad_ref[...], staged.w_out[...], NT)
-    staged.put(mix=mix)
+    parts = lax.axis_size(TP)
+    rows = arrived_rows(staged, "grad", parts)
+    mix = in_token_order(staged.made.mix, dot(rows, staged.w_out[...], NT), parts)
     y_grads = (mix * staged.gated[...]).astype(BF16)
     staged.put(y=y_grads)
     entering = (y_grads.astype(F32) * staged.enter[...]).astype(BF16)
@@ -522,21 +524,20 @@
     rows = {"rows%d" % step: block for step, block in row_blocks.items()}
     grads = {"grad%d" % step: block for step, block in grad_blocks.items()}
     rows["rows0"], grads["grad0"] = ready.rows0, ready.grad0
-    assembled = pltpu.VMEM((tokens, depth), BF16)
     both = near((2 * states, width), BF16)
     one = near((states, width), BF16)
     first = call(
         project,
         dict(rows, **dict(w_gate=ready.w_gate, w_in=ready.w_in, b=ready.b, leave=ready.leave)),
         dict(gate=wide, gated=wide, pre=wide, x=half, leaving=half, state=summary),
-        flops=4 * tokens * channels * depth, scratch=(assembled,),
+        flops=4 * tokens * channels * depth,
     )
     first.update(call(
         front,
         dict(grads, **dict(w_out=ready.w_out, c=ready.c, enter=ready.enter, factor=ready.factor),
              **dict(gated=first.gated, state=first.state)),
         dict(mix=wide, y=half, entering=half, grad=summary, message=both),
-        flops=2 * tokens * channels * depth, scratch=(assembled,),
+        flops=2 * tokens * channels * depth,
     ))
     group = dict(state=first.state, grad=first.grad, factor=ready.factor)
     message, x_rows, y_grads = first.message, first.x, first.y

time: 31.7 us -> 31.9 us (level)
  transfers between devices with their start and end apart: 13 -> 13, of which waited for: 9 -> 8; matrix products, arithmetic and copies ran while one was open for 0% -> 0% of each run, Pallas kernels for 17% -> 17%
where the time goes in v6:
time: 31.9 us; the launch traced here: 31.7 us
  starting transfers between devices  11.6 us (36%)
  waiting for transfers between devices  10.6 us (33%)
  Pallas kernels  8 us (25%)
  between operations  0.75 us (2%)
  local copies, waits for them, and re-layouts  0.7 us (2%)
    ppermute x13, starting transfers between devices, swap(): return lax.ppermute(value, axis, [(at, at ^ bit) for at in range(size)])  11.6 us
    ppermute x13, waiting for transfers between devices, swap(): return lax.ppermute(value, axis, [(at, at ^ bit) for at in range(size)])  10.6 us
    pallas_call x12, Pallas kernels, staged_call(): pl.pallas_call(kernel, name=body.__name__, out_shape=[jax.ShapeDtypeStruc...  8 us
    unnamed x6, local copies, waits for them, and re-layouts  0.7 us
  transfers between devices with their start and end apart: 13, of which 8 were waited for; matrix products, arithmetic and copies ran while one was open for 0% of the time, Pallas kernels for 17%

profile of v6, /device:TPU:0, one launch (start us, length us, event | category | flops | bytes accessed | tf_op | source)
XLA Modules:
  0.0 31.7 jit_solution(17186704038396002414)
XLA Ops:
  0.6 3.0 %collective-permute-start = (bf16[32,1600]{1,0:T(8,128)(2,1)}, bf16[32,1600]{1,0:T(8,128)(2,1)S(1)}, u32[]{:S(2)}, u32[]{:S(2)}) collective-permute-start(bf16[32,1600]{1,0:T(8,128)(2,1)} %refs_7_.1), channel_id=1, source_target_pairs={{0,2},{1,3},{2,0},{3,1},{4,6},{5,7},{6,4},{7,5},{8,10},{9,11},{10,... | collective-permute-start | bytes 307208 | tf_op jit(solution)/shard_map/ppermute | solution.py:496
  3.7 0.7 %copy-done = bf16[25,128]{1,0:T(8,128)(2,1)S(1)} copy-done((bf16[25,128]{1,0:T(8,128)(2,1)S(1)}, bf16[25,128]{1,0:T(8,128)(2,1)}, u32[]{:S(2)}) %copy-start) | copy-done | bytes 6424
  4.4 2.3 %prepare.1 = (f32[128,400]{1,0:T(8,128)S(1)}, f32[128,400]{1,0:T(8,128)S(1)}, f32[128,400]{1,0:T(8,128)S(1)}, f32[128,400]{1,0:T(8,128)S(1)}, f32[16,512]{1,0:T(...) custom-call(bf16[25,128]{1,0:T(8,128)(2,1)S(1)} %copy-done, ...), custom_call_target="tpu_custom_call" | custom-call | flops 52428800 | bytes 1048576 | tf_op jit(solution)/shard_map/prepare/pallas_call | solution.py:187
  6.8 0.8 %collective-permute-done.refs_1_ = bf16[32,1600]{1,0:T(8,128)(2,1)S(1)} collective-permute-done((bf16[32,1600]{1,0:T(8,128)(2,1)}, bf16[32,1600]{1,0:T(8,128)(2,1)S(1)}, u32[]{:S(2)}, u32[]{:S(2)}) %collective-permute-start) | collective-permute-done | bytes 102432 | tf_op jit(solution)/shard_map/ppermute | solution.py:496
  7.6 0.5 %collective-permute-start.4 = (bf16[32,1600]{1,0:T(8,128)(2,1)S(1)}, bf16[32,1600]{1,0:T(8,128)(2,1)S(1)}, u32[]{:S(2)}, u32[]{:S(2)}) collective-permute-start(bf16[32,1600]{1,0:T(8,128)(2,1)S(1)} %copy-done.2), channel_id=1, source_target_pairs={{0,1},{1,0},{2,3},{3,2},{4,5},{5,4},{6,7},{7,6},{8,9},{9,8},{10,11... | collective-permute-start | bytes 307208 | tf_op jit(solution)/shard_map/ppermute | solution.py:496
  8.1 1.0 %collective-permute-done.3.refs_1_ = bf16[32,1600]{1,0:T(8,128)(2,1)S(1)} collective-permute-done((bf16[32,1600]{1,0:T(8,128)(2,1)}, bf16[32,1600]{1,0:T(8,128)(2,1)S(1)}, u32[]{:S(2)}, u32[]{:S(2)}) %collective-permute-start.3) | collective-permute-done | bytes 102432 | tf_op jit(solution)/shard_map/ppermute | solution.py:496
  9.1 1.3 %project.1 = (f32[128,400]{1,0:T(8,128)S(1)}, f32[128,400]{1,0:T(8,128)S(1)}, f32[128,400]{1,0:T(8,128)S(1)}, bf16[128,400]{1,0:T(8,128)(2,1)S(1)}, bf16[128,400]{1,0:T(8,128)(2,1)S(1)}, /*index=5*/f32[16,512]{1,0:T(8,128)S(1)}) custom-call(bf16[32,1600]{1,0:T(8,128)(2,1)S(1)} %get-tuple-element.63.refs_0_, ...), custom_call_target="tpu_custom_call" | custom-call | flops 327680000 | bytes 1048576 | tf_op jit(solution)/shard_map/project/pallas_call | solution.py:187
  10.5 0.7 %front.1 = (f32[128,400]{1,0:T(8,128)S(1)}, bf16[128,400]{1,0:T(8,128)(2,1)S(1)}, bf16[128,400]{1,0:T(8,128)(2,1)S(1)}, f32[16,512]{1,0:T(8,128)S(1)}, bf16[32,512]{1,0:T(8,128)(2,1)S(1)}) custom-call(bf16[32,1600]{1,0:T(8,128)(2,1)S(1)} %get-tuple-element.71.refs_0_, bf16[32,1600]{1,0:T(8,128)(2,1)S(1)} %collective-permute-done.3.refs_1_, ...), custom_call_target="tpu_custom_call" | custom-call | flops 163840000 | bytes 1048576 | tf_op jit(solution)/shard_map/front/pallas_call | solution.py:187
  11.2 2.9 %collective-permute-start.8 = (bf16[32,512]{1,0:T(8,128)(2,1)S(1)}, bf16[32,512]{1,0:T(8,128)(2,1)S(1)}, u32[]{:S(2)}, u32[]{:S(2)}) collective-permute-start(bf16[32,512]{1,0:T(8,128)(2,1)S(1)} %get-tuple-element.89), channel_id=1, source_target_pairs={{0,12},{4,8},{8,4},{12,0},{16,28},{20,24},{24,20},{28,16},{1,13},{... | collective-permute-start | bytes 98312 | tf_op jit(solution)/shard_map/ppermute | solution.py:496
  14.1 0.4 %collective-permute-start.7 = (bf16[32,512]{1,0:T(8,128)(2,1)S(1)}, bf16[32,512]{1,0:T(8,128)(2,1)S(1)}, u32[]{:S(2)}, u32[]{:S(2)}) collective-permute-start(bf16[32,512]{1,0:T(8,128)(2,1)S(1)} %get-tuple-element.89), channel_id=1, source_target_pairs={{0,8},{4,12},{8,0},{12,4},{16,24},{20,28},{24,16},{28,20},{1,9},{5... | collective-permute-start | bytes 98312 | tf_op jit(solution)/shard_map/ppermute | solution.py:496
  14.9 0.5 %local_vectors.1.refs_0_ = f32[32,128]{1,0:T(8,128)S(1)} custom-call(f32[128,400]{1,0:T(8,128)S(1)} %get-tuple-element.58.refs_0_, f32[128,400]{1,0:T(8,128)S(1)} %get-tuple-element.59.refs_1_, f32[128,128]{1,0:T(8,128)S(1)} %get-tuple-element.60.refs_2_, bf16[16,128]{1,0:T(8,128)(2,1)S(1)} %get-tuple-element.61.refs_6_.refs_3_, ...), custom_call_target="tpu_custom_call" | custom-call | flops 52428800 | bytes 1048576 | tf_op jit(solution)/shard_map/local_vectors/pallas_call | solution.py:187
  15.4 0.7 %collective-permute-done.8.refs_6_ = bf16[32,512]{1,0:T(8,128)(2,1)S(1)} collective-permute-done((bf16[32,512]{1,0:T(8,128)(2,1)S(1)}, bf16[32,512]{1,0:T(8,128)(2,1)S(1)}, u32[]{:S(2)}, u32[]{:S(2)}) %collective-permute-start.8) | collective-permute-done | bytes 32800 | tf_op jit(solution)/shard_map/ppermute | solution.py:496
  16.1 1.9 %collective-permute-done.7.refs_5_ = bf16[32,512]{1,0:T(8,128)(2,1)S(1)} collective-permute-done((bf16[32,512]{1,0:T(8,128)(2,1)S(1)}, bf16[32,512]{1,0:T(8,128)(2,1)S(1)}, u32[]{:S(2)}, u32[]{:S(2)}) %collective-permute-start.7) | collective-permute-done | bytes 32800 | tf_op jit(solution)/shard_map/ppermute | solution.py:496
  18.0 0.4 %collective-permute-done.6.refs_4_ = bf16[32,512]{1,0:T(8,128)(2,1)S(1)} collective-permute-done((bf16[32,512]{1,0:T(8,128)(2,1)S(1)}, bf16[32,512]{1,0:T(8,128)(2,1)S(1)}, u32[]{:S(2)}, u32[]{:S(2)}) %collective-permute-start.6) | collective-permute-done | bytes 32800 | tf_op jit(solution)/shard_map/ppermute | solution.py:496
  18.5 0.2 join_body.1
  18.7 2.7 %collective-permute-start.9 = (bf16[16,512]{1,0:T(8,128)(2,1)S(1)}, bf16[16,512]{1,0:T(8,128)(2,1)S(1)}, u32[]{:S(2)}, u32[]{:S(2)}) collective-permute-start(bf16[16,512]{1,0:T(8,128)(2,1)S(1)} %get-tuple-element.101), channel_id=1, source_target_pairs={{0,16},{4,20},{8,24},{12,28},{16,0},{20,4},{24,8},{28,12},{1,17},{... | collective-permute-start | bytes 49160 | tf_op jit(solution)/shard_map/ppermute | solution.py:496
  21.3 0.4 %local_channels.1 = (f32[128,400]{1,0:T(8,128)S(1)}, f32[128,400]{1,0:T(8,128)S(1)}) custom-call(f32[128,400]{1,0:T(8,128)S(1)} %get-tuple-element.58.refs_0_, f32[128,400]{1,0:T(8,128)S(1)} %get-tuple-element.59.refs_1_, f32[128,128]{1,0:T(8,128)S(1)} %get-tuple-element.85.refs_2_, f32[128,128]{1,0:T(8,128)S(1)} %get-tuple-element.86.refs_3_, ...), custom_call_target="tpu_custom_call" | custom-call | flops 104857600 | bytes 1048576 | tf_op jit(solution)/shard_map/local_channels/pallas_call | solution.py:187
  21.7 1.7 %collective-permute-done.9.refs_15_ = bf16[16,512]{1,0:T(8,128)(2,1)S(1)} collective-permute-done((bf16[16,512]{1,0:T(8,128)(2,1)S(1)}, bf16[16,512]{1,0:T(8,128)(2,1)S(1)}, u32[]{:S(2)}, u32[]{:S(2)}) %collective-permute-start.9) | collective-permute-done | bytes 16416 | tf_op jit(solution)/shard_map/ppermute | solution.py:496
  23.4 0.9 %back_body.1 = (f32[32,1792]{1,0:T(8,128)S(1)}, bf16[32,1792]{1,0:T(8,128)(2,1)S(1)}, f32[32,128]{1,0:T(8,128)S(1)}, bf16[16,400]{1,0:T(8,128)(2,1)S(1)}, bf16[16,400]{1,0:T(8,128)(2,1)S(1)}) custom-call(f32[32,128]{1,0:T(8,128)S(1)} %local_vectors.1.refs_0_, f32[128,400]{1,0:T(8,128)S(1)} %get-tuple-element.93.refs_1_, ...), custom_call_target="tpu_custom_call" | custom-call | flops 163840000 | bytes 1048576 | tf_op jit(solution)/shard_map/back_body/pallas_call | solution.py:187
  24.4 1.3 %collective-permute-done.10.refs_1_ = bf16[32,1792]{1,0:T(8,128)(2,1)S(1)} collective-permute-done((bf16[32,1792]{1,0:T(8,128)(2,1)S(1)}, bf16[32,1792]{1,0:T(8,128)(2,1)S(1)}, u32[]{:S(2)}, u32[]{:S(2)}) %collective-permute-start.10) | collective-permute-done | bytes 114720 | tf_op jit(solution)/shard_map/ppermute | solution.py:496
  25.7 1.6 %collective-permute-start.11 = (bf16[32,1792]{1,0:T(8,128)(2,1)S(1)}, bf16[32,1792]{1,0:T(8,128)(2,1)S(1)}, u32[]{:S(2)}, u32[]{:S(2)}) collective-permute-start(bf16[32,1792]{1,0:T(8,128)(2,1)S(1)} %add.2), channel_id=1, source_target_pairs={{0,2},{1,3},{2,0},{3,1},{4,6},{5,7},{6,4},{7,5},{8,10},{9,11},{10,... | collective-permute-start | bytes 344072 | tf_op jit(solution)/shard_map/ppermute | solution.py:496
  27.3 0.8 %rest_body.1 = (f32[32,1792]{1,0:T(8,128)S(1)}, bf16[32,1792]{1,0:T(8,128)(2,1)S(1)}) custom-call(f32[32,128]{1,0:T(8,128)S(1)} %get-tuple-element.105.refs_0_, f32[128,400]{1,0:T(8,128)S(1)} %get-tuple-element.93.refs_1_, f32[128,400]{1,0:T(8,128)S(1)} %get-tuple-element.94.refs_2_, f32[128,400]{1,0:T(8,128)S(1)} %get-tuple-element.83.refs_3_, ...), custom_call_target="tpu_custom_call" | custom-call | flops 163840000 | bytes 1048576 | tf_op jit(solution)/shard_map/rest_body/pallas_call | solution.py:187
  28.2 2.8 %collective-permute-done.11.refs_1_ = bf16[32,1792]{1,0:T(8,128)(2,1)S(1)} collective-permute-done((bf16[32,1792]{1,0:T(8,128)(2,1)S(1)}, bf16[32,1792]{1,0:T(8,128)(2,1)S(1)}, u32[]{:S(2)}, u32[]{:S(2)}) %collective-permute-start.11) | collective-permute-done | bytes 114720 | tf_op jit(solution)/shard_map/ppermute | solution.py:496
  31.0 0.7 %total.1 = (bf16[32,1600]{1,0:T(8,128)(2,1)}, f32[16,128]{1,0:T(8,128)}, f32[16,128]{1,0:T(8,128)}) custom-call(f32[32,1792]{1,0:T(8,128)S(1)} %add.3.refs_0_, bf16[32,1792]{1,0:T(8,128)(2,1)S(1)} %collective-permute-done.12.refs_1_), custom_call_target="tpu_custom_call" | custom-call | bytes 1048576 | tf_op jit(solution)/shard_map/total/pallas_call | solution.py:187
  (20 shorter events, 0.7 us)
Async XLA Ops:
  0.6 7.0 %collective-permute-start = (bf16[32,1600]{1,0:T(8,128)(2,1)}, bf16[32,1600]{1,0:T(8,128)(2,1)S(1)}, u32[]{:S(2)}, u32[]{:S(2)}) collective-permute-start(bf16[32,1600]{1,0:T(8,128)(2,1)} %refs_7_.1), channel_id=1, source_target_pairs={{0,2},{1,3},{2,0},{3,1},{4,6},{5,7},{6,4},{7,5},{8,10},{9,11},{10,... | collective-permute-start | bytes 307208 | tf_op jit(solution)/shard_map/ppermute | solution.py:496
  3.6 5.5 %collective-permute-start.3 = (bf16[32,1600]{1,0:T(8,128)(2,1)}, bf16[32,1600]{1,0:T(8,128)(2,1)S(1)}, u32[]{:S(2)}, u32[]{:S(2)}) collective-permute-start(bf16[32,1600]{1,0:T(8,128)(2,1)} %refs_8_.1), channel_id=1, source_target_pairs={{0,2},{1,3},{2,0},{3,1},{4,6},{5,7},{6,4},{7,5},{8,10},{9,11},{10,... | collective-permute-start | bytes 307208 | tf_op jit(solution)/shard_map/ppermute | solution.py:496
  3.7 0.7 %copy-start = (bf16[25,128]{1,0:T(8,128)(2,1)S(1)}, bf16[25,128]{1,0:T(8,128)(2,1)}, u32[]{:S(2)}) copy-start(bf16[25,128]{1,0:T(8,128)(2,1)} %refs_0_.1) | copy-start | bytes 19204
  4.4 2.3 %copy-start.1 = (bf16[32,1600]{1,0:T(8,128)(2,1)S(1)}, bf16[32,1600]{1,0:T(8,128)(2,1)}, u32[]{:S(2)}) copy-start(bf16[32,1600]{1,0:T(8,128)(2,1)} %refs_7_.1) | copy-start | bytes 307204
  4.4 3.2 %copy-start.2 = (bf16[32,1600]{1,0:T(8,128)(2,1)S(1)}, bf16[32,1600]{1,0:T(8,128)(2,1)}, u32[]{:S(2)}) copy-start(bf16[32,1600]{1,0:T(8,128)(2,1)} %refs_8_.1) | copy-start | bytes 307204
  6.7 2.4 %collective-permute-start.1 = (bf16[32,1600]{1,0:T(8,128)(2,1)S(1)}, bf16[32,1600]{1,0:T(8,128)(2,1)S(1)}, u32[]{:S(2)}, u32[]{:S(2)}) collective-permute-start(bf16[32,1600]{1,0:T(8,128)(2,1)S(1)} %copy-done.1), channel_id=1, source_target_pairs={{0,1},{1,0},{2,3},{3,2},{4,5},{5,4},{6,7},{7,6},{8,9},{9,8},{10,11... | collective-permute-start | bytes 307208 | tf_op jit(solution)/shard_map/ppermute | solution.py:496
  7.6 1.5 %collective-permute-start.2 = (bf16[32,1600]{1,0:T(8,128)(2,1)S(1)}, bf16[32,1600]{1,0:T(8,128)(2,1)S(1)}, u32[]{:S(2)}, u32[]{:S(2)}) collective-permute-start(bf16[32,1600]{1,0:T(8,128)(2,1)S(1)} %collective-permute-done.refs_1_), channel_id=1, source_target_pairs={{0,1},{1,0},{2,3},{3,2},{4,5},{5,4},{6,7},{7,6},{8,9},{9,8},{10,11... | collective-permute-start | bytes 307208 | tf_op jit(solution)/shard_map/ppermute | solution.py:496
  7.6 2.8 %collective-permute-start.4 = (bf16[32,1600]{1,0:T(8,128)(2,1)S(1)}, bf16[32,1600]{1,0:T(8,128)(2,1)S(1)}, u32[]{:S(2)}, u32[]{:S(2)}) collective-permute-start(bf16[32,1600]{1,0:T(8,128)(2,1)S(1)} %copy-done.2), channel_id=1, source_target_pairs={{0,1},{1,0},{2,3},{3,2},{4,5},{5,4},{6,7},{7,6},{8,9},{9,8},{10,11... | collective-permute-start | bytes 307208 | tf_op jit(solution)/shard_map/ppermute | solution.py:496
  9.1 1.4 %collective-permute-start.5 = (bf16[32,1600]{1,0:T(8,128)(2,1)S(1)}, bf16[32,1600]{1,0:T(8,128)(2,1)S(1)}, u32[]{:S(2)}, u32[]{:S(2)}) collective-permute-start(bf16[32,1600]{1,0:T(8,128)(2,1)S(1)} %collective-permute-done.3.refs_1_), channel_id=1, source_target_pairs={{0,1},{1,0},{2,3},{3,2},{4,5},{5,4},{6,7},{7,6},{8,9},{9,8},{10,11... | collective-permute-start | bytes 307208 | tf_op jit(solution)/shard_map/ppermute | solution.py:496
  11.2 4.9 %collective-permute-start.8 = (bf16[32,512]{1,0:T(8,128)(2,1)S(1)}, bf16[32,512]{1,0:T(8,128)(2,1)S(1)}, u32[]{:S(2)}, u32[]{:S(2)}) collective-permute-start(bf16[32,512]{1,0:T(8,128)(2,1)S(1)} %get-tuple-element.89), channel_id=1, source_target_pairs={{0,12},{4,8},{8,4},{12,0},{16,28},{20,24},{24,20},{28,16},{1,13},{... | collective-permute-start | bytes 98312 | tf_op jit(solution)/shard_map/ppermute | solution.py:496
  14.1 3.9 %collective-permute-start.7 = (bf16[32,512]{1,0:T(8,128)(2,1)S(1)}, bf16[32,512]{1,0:T(8,128)(2,1)S(1)}, u32[]{:S(2)}, u32[]{:S(2)}) collective-permute-start(bf16[32,512]{1,0:T(8,128)(2,1)S(1)} %get-tuple-element.89), channel_id=1, source_target_pairs={{0,8},{4,12},{8,0},{12,4},{16,24},{20,28},{24,16},{28,20},{1,9},{5... | collective-permute-start | bytes 98312 | tf_op jit(solution)/shard_map/ppermute | solution.py:496
  14.5 3.9 %collective-permute-start.6 = (bf16[32,512]{1,0:T(8,128)(2,1)S(1)}, bf16[32,512]{1,0:T(8,128)(2,1)S(1)}, u32[]{:S(2)}, u32[]{:S(2)}) collective-permute-start(bf16[32,512]{1,0:T(8,128)(2,1)S(1)} %get-tuple-element.89), channel_id=1, source_target_pairs={{0,4},{4,0},{8,12},{12,8},{16,20},{20,16},{24,28},{28,24},{1,5},{5... | collective-permute-start | bytes 98312 | tf_op jit(solution)/shard_map/ppermute | solution.py:496
  18.7 4.7 %collective-permute-start.9 = (bf16[16,512]{1,0:T(8,128)(2,1)S(1)}, bf16[16,512]{1,0:T(8,128)(2,1)S(1)}, u32[]{:S(2)}, u32[]{:S(2)}) collective-permute-start(bf16[16,512]{1,0:T(8,128)(2,1)S(1)} %get-tuple-element.101), channel_id=1, source_target_pairs={{0,16},{4,20},{8,24},{12,28},{16,0},{20,4},{24,8},{28,12},{1,17},{... | collective-permute-start | bytes 49160 | tf_op jit(solution)/shard_map/ppermute | solution.py:496
  24.3 1.4 %collective-permute-start.10 = (bf16[32,1792]{1,0:T(8,128)(2,1)S(1)}, bf16[32,1792]{1,0:T(8,128)(2,1)S(1)}, u32[]{:S(2)}, u32[]{:S(2)}) collective-permute-start(bf16[32,1792]{1,0:T(8,128)(2,1)S(1)} %get-tuple-element.108), channel_id=1, source_target_pairs={{0,1},{1,0},{2,3},{3,2},{4,5},{5,4},{6,7},{7,6},{8,9},{9,8},{10,11... | collective-permute-start | bytes 344072 | tf_op jit(solution)/shard_map/ppermute | solution.py:496
  25.7 5.3 %collective-permute-start.11 = (bf16[32,1792]{1,0:T(8,128)(2,1)S(1)}, bf16[32,1792]{1,0:T(8,128)(2,1)S(1)}, u32[]{:S(2)}, u32[]{:S(2)}) collective-permute-start(bf16[32,1792]{1,0:T(8,128)(2,1)S(1)} %add.2), channel_id=1, source_target_pairs={{0,2},{1,3},{2,0},{3,1},{4,6},{5,7},{6,4},{7,5},{8,10},{9,11},{10,... | collective-permute-start | bytes 344072 | tf_op jit(solution)/shard_map/ppermute | solution.py:496
  28.1 2.9 %collective-permute-start.12 = (bf16[32,1792]{1,0:T(8,128)(2,1)S(1)}, bf16[32,1792]{1,0:T(8,128)(2,1)S(1)}, u32[]{:S(2)}, u32[]{:S(2)}) collective-permute-start(bf16[32,1792]{1,0:T(8,128)(2,1)S(1)} %get-tuple-element.112), channel_id=1, source_target_pairs={{0,1},{1,0},{2,3},{3,2},{4,5},{5,4},{6,7},{7,6},{8,9},{9,8},{10,11... | collective-permute-start | bytes 344072 | tf_op jit(solution)/shard_map/ppermute | solution.py:496
